TPU v7x, 256 devices: a whole 4x4x8 slice. The times are simulated.
256 devices in a mesh: cache: 64 (over y, z, core), tensor: 4 (over x).
Axes of the slice: x: 4, y: 4, z: 8, core: 2. Of those that a mesh axis runs over, the one named last changes fastest.
Arguments:
- hidden: bfloat16 [512, 4, 7168], P('cache', None, 'tensor'), may hold values from -6 to 6
- w_dkv: bfloat16 [7168, 576], P('tensor'), may hold values from -0.0625 to 0.0625
- kv_gain: float32 [512], replicated, may hold values from 0.5 to 1.5
- q_latent: bfloat16 [512, 4, 32768], P('cache', None, 'tensor'), may hold values from -6 to 6
- q_rope: bfloat16 [512, 4, 4096], P('cache', None, 'tensor'), may hold values from -6 to 6
- w_uv: bfloat16 [64, 512, 128], P('tensor'), may hold values from -0.25 to 0.25
- latent_cache: bfloat16 [4096, 64, 576], P('cache'), may hold values from -6 to 6
- block_slots: int32 [512, 64], P('cache'), may hold values from 0 to 63
- seg_owner: int32 [512, 8], P('cache'), may hold values from 0 to 63, all different within a row; in each aligned block of 8 rows (0 to 7, 8 to 15, ...) at most 2 rows name the same one
- lengths: int32 [512], P('cache'), may hold values from 1 to 4096
Outputs:
- attn_out: bfloat16 [512, 4, 8192], P('cache', None, 'tensor')
- new_latent: bfloat16 [512, 4, 576], P('cache')
Inputs may be any that keep to these rules, and one draw needn't show every extreme that they name: `seg_owner`: in each row the 8 owners are distinct. Among the rows of one device no owner is named more than 2 times, a bound that some block reaches.
All inputs are finite; a program needn't handle non-finite values.
Results may differ from a plain program's by a relative error of at most 0.0053.
Values may be sent and summed in bfloat16 or wider, within the bound.
No kernel may reach another device: no remote copies, remote signals or barrier semaphores. Data moves between devices by JAX's collectives and lax.ppermute only.
A program may use at most 128 MiB of HBM per device.

v0:
```python
import jax
import jax.numpy as jnp
from jax import lax
from jax.sharding import PartitionSpec as P

LAT = 512
SEGS = 8


softmax_scale = 192.0 ** (-0.5)
masked_score = -1e30
rope_base = 10000.0
group_slots = 8


def rotate(values, places):
    half_width = values.shape[-1] // 2
    frequency = rope_base ** (-(jnp.arange(half_width, dtype=jnp.float32) * 2.0 / values.shape[-1]))
    angles = places.astype(jnp.float32)[..., None] * frequency
    cosine = jnp.cos(angles)
    sine_part = jnp.sin(angles)
    front_half = values[..., :half_width]
    back_half = values[..., half_width:]
    return jnp.concatenate(
        [front_half * cosine - back_half * sine_part, front_half * sine_part + back_half * cosine],
        -1,
    )


def finish_latent(summed, places, kv_gain):
    latent = summed[..., :LAT]
    normed = latent * lax.rsqrt(jnp.mean(latent * latent, -1, keepdims=True) + 1e-06) * kv_gain
    return jnp.concatenate([normed, rotate(summed[..., LAT:], places)], -1).astype(jnp.bfloat16)


def attend_slots(latent_cache, queries, details):
    slot_count = queries.shape[0]
    step_count = queries.shape[1]
    channels = latent_cache.shape[-1]
    seg_blocks = details.shape[1] - 2
    groups = slot_count // group_slots
    grouped_query = queries.reshape(groups, group_slots, -1, channels)
    grouped_info = details.reshape(groups, group_slots, -1)

    def one_group(operands):
        query_rows, slot_info = operands
        tokens_kv = latent_cache[slot_info[:, :seg_blocks]].reshape(group_slots, -1, channels)
        token_span = tokens_kv.shape[1]
        scores = (
            jnp.einsum("gqc,gkc->gqk", query_rows, tokens_kv, preferred_element_type=jnp.float32)
            * softmax_scale
        )
        places = (
            slot_info[:, seg_blocks + 1 : seg_blocks + 2] * token_span
            + jnp.arange(token_span, dtype=jnp.int32)[None, :]
        )
        living = (places < slot_info[:, seg_blocks : seg_blocks + 1])[:, None, :]
        masked = jnp.where(living, scores, masked_score)
        highest = jnp.max(masked, -1)
        weights = jnp.where(living, jnp.exp(masked - highest[..., None]), 0.0)
        totals = jnp.sum(weights, -1)
        summed = jnp.einsum(
            "gqk,gkl->gql",
            weights.astype(jnp.bfloat16),
            tokens_kv[..., :LAT],
            preferred_element_type=jnp.float32,
        )
        return (summed.astype(jnp.bfloat16), highest, totals)

    summed, highest, totals = lax.map(one_group, (grouped_query, grouped_info))
    return (
        summed.reshape(slot_count, step_count, -1),
        highest.reshape(slot_count, step_count, -1),
        totals.reshape(slot_count, step_count, -1),
    )


def outgoing(summed_here, owners_count, item_count, step_count):
    sent = summed_here.astype(jnp.float32)
    return sent.reshape(owners_count, item_count, step_count, -1)


def body(
    hidden, w_dkv, kv_gain, q_latent, q_rope, w_uv, latent_cache, block_slots, seg_owner, lengths
):
    row_count = hidden.shape[0]
    step_count = hidden.shape[1]
    channels = latent_cache.shape[-1]
    heads_dev = q_latent.shape[2] // LAT
    owners_count = lax.axis_size("cache")
    capacity = max(2, row_count * SEGS // owners_count)
    positions = lengths[:, None] + jnp.arange(step_count, dtype=jnp.int32)[None, :]
    partial_sum = jnp.einsum("rsd,dc->rsc", hidden, w_dkv, preferred_element_type=jnp.float32)
    summed = lax.psum(partial_sum, "tensor")
    new_latent = finish_latent(summed, positions, kv_gain)
    rope_width = channels - LAT
    roped = rotate(
        q_rope.reshape(row_count, step_count, heads_dev, rope_width).astype(jnp.float32),
        positions[..., None],
    )
    queries = jnp.concatenate(
        [q_latent.reshape(row_count, step_count, heads_dev, LAT), roped.astype(jnp.bfloat16)], -1
    )
    own_scores = (
        jnp.einsum("rshc,rtc->rsht", queries, new_latent, preferred_element_type=jnp.float32)
        * softmax_scale
    )
    causal = (jnp.arange(step_count)[None, :] <= jnp.arange(step_count)[:, None])[None, :, None, :]
    own_masked = jnp.where(causal, own_scores, masked_score)
    own_top = jnp.max(own_masked, -1)
    own_weights = jnp.where(causal, jnp.exp(own_masked - own_top[..., None]), 0.0)
    own_total = jnp.sum(own_weights, -1)
    own_sum = jnp.einsum("rsht,rtl->rshl", own_weights, new_latent[..., :LAT].astype(jnp.float32))
    own_proj = jnp.einsum(
        "rshl,hlv->rshv", own_sum.astype(jnp.bfloat16), w_uv, preferred_element_type=jnp.float32
    )
    pair_count = row_count * SEGS
    seg_blocks = block_slots.shape[1] // SEGS
    owner_flat = seg_owner.reshape(pair_count)
    onehot = (owner_flat[:, None] == jnp.arange(owners_count, dtype=jnp.int32)[None, :]).astype(
        jnp.int32
    )
    earlier = jnp.cumsum(onehot, 0) - onehot
    rank_in_owner = jnp.sum(earlier * onehot, 1)
    slot_of_pair = owner_flat * capacity + rank_in_owner
    slot_total = owners_count * capacity
    matches = (slot_of_pair[:, None] == jnp.arange(slot_total, dtype=jnp.int32)[None, :]).astype(
        jnp.int32
    )
    pair_of_slot = jnp.sum(matches * jnp.arange(pair_count, dtype=jnp.int32)[:, None], 0)
    filled = jnp.sum(matches, 0) > 0
    row_of_slot = pair_of_slot // SEGS
    segment_of_slot = pair_of_slot % SEGS
    flat_query = queries.reshape(row_count, step_count, heads_dev * channels)
    send_query = jnp.take(flat_query, row_of_slot, axis=0).reshape(
        owners_count, capacity, step_count, heads_dev * channels
    )
    slot_blocks = jnp.take(block_slots.reshape(pair_count, seg_blocks), pair_of_slot, axis=0)
    slot_length = jnp.where(filled, jnp.take(lengths, row_of_slot), 0)
    send_info = jnp.concatenate([slot_blocks, slot_length[:, None], segment_of_slot[:, None]], 1)
    send_info = send_info.reshape(owners_count, capacity, seg_blocks + 2)
    got_query, got_info = (
        lax.all_to_all(send_query, "cache", split_axis=0, concat_axis=0, tiled=True),
        lax.all_to_all(send_info, "cache", split_axis=0, concat_axis=0, tiled=True),
    )
    summed_here, highest_here, totals_here = attend_slots(
        latent_cache,
        got_query.reshape(slot_total, step_count, -1),
        got_info.reshape(slot_total, -1),
    )
    back_sum, back_top, back_total = (
        lax.all_to_all(
            outgoing(summed_here, owners_count, capacity, step_count),
            "cache",
            split_axis=0,
            concat_axis=0,
            tiled=True,
        ),
        lax.all_to_all(
            highest_here.reshape(owners_count, capacity, step_count, heads_dev),
            "cache",
            split_axis=0,
            concat_axis=0,
            tiled=True,
        ),
        lax.all_to_all(
            totals_here.reshape(owners_count, capacity, step_count, heads_dev),
            "cache",
            split_axis=0,
            concat_axis=0,
            tiled=True,
        ),
    )
    seg_back = jnp.take(
        back_sum.reshape(slot_total, step_count, heads_dev, -1), slot_of_pair, axis=0
    )
    seg_back = seg_back.reshape(row_count, SEGS, step_count, heads_dev, -1)
    projected = jnp.einsum(
        "rkshl,hlv->rkshv", seg_back.astype(jnp.bfloat16), w_uv, preferred_element_type=jnp.float32
    )
    seg_top = jnp.take(back_top.reshape(slot_total, step_count, heads_dev), slot_of_pair, axis=0)
    seg_top = seg_top.reshape(row_count, SEGS, step_count, heads_dev)
    seg_total = jnp.take(
        back_total.reshape(slot_total, step_count, heads_dev), slot_of_pair, axis=0
    )
    seg_total = seg_total.reshape(row_count, SEGS, step_count, heads_dev)
    largest = jnp.maximum(own_top, jnp.max(seg_top, 1))
    factor = jnp.exp(seg_top - largest[:, None])
    own_factor = jnp.exp(own_top - largest)
    numerator = jnp.sum(factor[..., None] * projected, 1) + own_factor[..., None] * own_proj
    denominator = jnp.sum(factor * seg_total, 1) + own_factor * own_total
    attn_out = (numerator / denominator[..., None]).astype(jnp.bfloat16)
    return (attn_out.reshape(row_count, step_count, -1), new_latent)


def solution(mesh):
    in_specs = (
        P("cache", None, "tensor"),
        P("tensor", None),
        P(),
        P("cache", None, "tensor"),
        P("cache", None, "tensor"),
        P("tensor", None, None),
        P("cache", None, None),
        P("cache", None),
        P("cache", None),
        P("cache"),
    )
    out_specs = (P("cache", None, "tensor"), P("cache", None, None))
    return jax.shard_map(body, mesh=mesh, in_specs=in_specs, out_specs=out_specs, check_vma=False)
```

profile of v0, /device:TPU:1, one launch (start us, length us, event | category | flops | bytes accessed | tf_op | source)
XLA Modules:
  0.0 812.5 jit_solution(888102916594385417)
XLA Ops:
  22.3 35.7 %all-reduce.2.cloned.1.call-done = f32[8,4,576]{2,0,1:T(8,128)} async-done(((f32[8,4,576]{2,0,1:T(8,128)}), f32[8,4,576]{2,0,1:T(8,128)}) %all-reduce.2.cloned.1.call-update) | async-done | bytes 73744 | tf_op jit(solution)/shard_map/psum | solution.py:94
  61.0 11.3 %gather_fusion.2 = bf16[128,4,9216]{2,1,0:T(4,128)(2,1)} fusion(bf16[8,4,9216]{2,1,0:T(4,128)(2,1)S(1)} %reshape.491, s32[1024]{0:T(1024)S(1)} %pad_clamp_fusion.3), kind=kCustom, calls=%fused_computation.4 | custom fusion | bytes 18874880 | tf_op jit(solution)/shard_map/jit(_take)/gather | solution.py:135
  72.3 9.2 %broadcast_select_fusion = bf16[64,2,4,9216]{3,2,1,0:T(4,128)(2,1)} fusion(bf16[64,2,4,9216]{3,2,1,0:T(4,128)(2,1)} %bitcast.128, pred[64,2]{1,0:T(8,128)(4,1)S(1)} %get-tuple-element.97), kind=kLoop, calls=%fused_computation.31 | loop fusion | flops 4718592 | bytes 18874496 | tf_op jit(solution)/shard_map/jit(_take)/select_n | solution.py:135
  81.5 13.1 %all-to-all-start.1 = ((bf16[64,2,4,9216]{3,2,1,0:T(4,128)(2,1)}), bf16[64,2,4,9216]{3,2,1,0:T(4,128)(2,1)}, u32[]{:S(2)}, u32[]{:S(2)}) async-start(bf16[64,2,4,9216]{3,2,1,0:T(4,128)(2,1)} %broadcast_select_fusion), calls=%async_computation.1 | async-start | bytes 18874368 | tf_op jit(solution)/shard_map/all_to_all | solution.py:143
  97.8 205.0 %all-to-all-done.1 = bf16[64,2,4,9216]{3,2,1,0:T(4,128)(2,1)} async-done(((bf16[64,2,4,9216]{3,2,1,0:T(4,128)(2,1)}), bf16[64,2,4,9216]{3,2,1,0:T(4,128)(2,1)}, u32[]{:S(2)}, u32[]{:S(2)}) %all-to-all-start.1) | async-done | bytes 9437216 | tf_op jit(solution)/shard_map/all_to_all | solution.py:143
  302.9 6.0 all-to-all-start
  308.9 18.2 %reshape_reshape.13 = bf16[16,8,64,576]{3,2,1,0:T(8,128)(2,1)} reshape(bf16[64,2,4,9216]{3,2,1,0:T(4,128)(2,1)} %all-to-all-done.1) | data formatting | bytes 18874368 | tf_op jit(solution)/shard_map/reshape;reshape | solution.py:42
  327.1 211.0 %while.14 = (s32[]{:T(128)}, bf16[16,8,64,512]{3,2,1,0:T(8,128)(2,1)}, f32[16,8,64]{2,1,0:T(8,128)S(1)}, f32[16,8,64]{2,1,0:T(8,128)S(1)}, s32[16,8,10]{2,1,0:T(...) while((s32[]{:T(128)}, bf16[16,8,64,512]{3,2,1,0:T(8,128)(2,1)}, ...), condition=%wide.region_7.8_spmd, body=%wide.region_4.7_spmd.sunk | while | flops 573055168 | bytes 42123720 | solution.py:70
  327.5 6.0 gather_fusion
  340.7 6.0 gather_fusion
  353.9 6.0 gather_fusion
  367.1 6.0 gather_fusion
  380.3 6.0 gather_fusion
  393.5 6.0 gather_fusion
  406.6 6.0 gather_fusion
  419.8 6.0 gather_fusion
  433.0 6.0 gather_fusion
  446.2 6.0 gather_fusion
  459.4 6.0 gather_fusion
  472.6 6.0 gather_fusion
  485.9 6.0 gather_fusion
  499.0 6.0 gather_fusion
  512.2 6.0 gather_fusion
  525.4 6.0 gather_fusion
  539.2 10.3 %all-to-all-start.4 = ((f32[64,1,128]{2,1,0:T(1,128)}), f32[64,1,128]{2,1,0:T(1,128)S(1)}, u32[]{:S(2)}, u32[]{:S(2)}) async-start(f32[64,1,128]{2,1,0:T(1,128)} %reshape.582), calls=%async_computation.4 | async-start | bytes 65536 | tf_op jit(solution)/shard_map/all_to_all | solution.py:166
  550.5 8.2 %all-to-all-done.4 = f32[64,1,128]{2,1,0:T(1,128)S(1)} async-done(((f32[64,1,128]{2,1,0:T(1,128)}), f32[64,1,128]{2,1,0:T(1,128)S(1)}, u32[]{:S(2)}, u32[]{:S(2)}) %all-to-all-start.4) | async-done | bytes 32800 | tf_op jit(solution)/shard_map/all_to_all | solution.py:166
  563.4 14.6 %reshape.499 = bf16[64,2,4,8192]{3,2,1,0:T(4,128)(2,1)} reshape(bf16[16,8,64,512]{3,2,1,0:T(8,128)(2,1)} %get-tuple-element.43) | data formatting | bytes 16777216 | tf_op jit(solution)/shard_map/convert_element_type | solution.py:79
  578.0 10.8 %all-to-all-start.3 = ((bf16[64,2,4,8192]{3,2,1,0:T(4,128)(2,1)}), bf16[64,2,4,8192]{3,2,1,0:T(4,128)(2,1)}, u32[]{:S(2)}, u32[]{:S(2)}) async-start(bf16[64,2,4,8192]{3,2,1,0:T(4,128)(2,1)} %reshape.499), calls=%async_computation.3 | async-start | bytes 16777216 | tf_op jit(solution)/shard_map/all_to_all | solution.py:152
  596.2 178.4 %all-to-all-done.3 = bf16[64,2,4,8192]{3,2,1,0:T(4,128)(2,1)} async-done(((bf16[64,2,4,8192]{3,2,1,0:T(4,128)(2,1)}), bf16[64,2,4,8192]{3,2,1,0:T(4,128)(2,1)}, u32[]{:S(2)}, u32[]{:S(2)}) %all-to-all-start.3) | async-done | bytes 8388640 | tf_op jit(solution)/shard_map/all_to_all | solution.py:152
  774.6 14.4 %reshape.494 = bf16[128,4,16,512]{3,2,1,0:T(8,128)(2,1)} reshape(bf16[64,2,4,8192]{3,2,1,0:T(4,128)(2,1)} %all-to-all-done.3) | data formatting | bytes 16777216 | tf_op jit(solution)/shard_map/reshape | solution.py:175
  789.0 6.1 gather_fusion.3
  798.9 5.4 fusion.27
  (287 shorter events, 153.9 us)
Async XLA Ops:
  7.2 791.7 %copy-start = (bf16[16,512,128]{2,1,0:T(8,128)(2,1)S(1)}, bf16[16,512,128]{2,1,0:T(8,128)(2,1)}, u32[]{:S(2)}) copy-start(bf16[16,512,128]{2,1,0:T(8,128)(2,1)} %param.19) | copy-start | bytes 6291460
  7.2 50.9 %all-reduce.2.cloned.1.call-start = ((), (), s32[]{:S(2)}) async-start(), calls=%async_computation.5 | async-start | bytes 163840 | tf_op jit(solution)/shard_map/psum | solution.py:94
  81.5 14.1 %copy-start.5 = (s32[8,64]{1,0:T(8,128)S(1)}, s32[8,64]{1,0:T(8,128)}, u32[]{:S(2)}) copy-start(s32[8,64]{1,0:T(8,128)} %param.21) | copy-start | bytes 6148
  81.5 221.4 %all-to-all-start.1 = ((bf16[64,2,4,9216]{3,2,1,0:T(4,128)(2,1)}), bf16[64,2,4,9216]{3,2,1,0:T(4,128)(2,1)}, u32[]{:S(2)}, u32[]{:S(2)}) async-start(bf16[64,2,4,9216]{3,2,1,0:T(4,128)(2,1)} %broadcast_select_fusion), calls=%async_computation.1 | async-start | bytes 18874368 | tf_op jit(solution)/shard_map/all_to_all | solution.py:143
  302.9 24.3 %all-to-all-start = ((s32[64,2,10]{2,1,0:T(2,128)}), s32[64,2,10]{2,1,0:T(2,128)S(1)}, u32[]{:S(2)}, u32[]{:S(2)}) async-start(s32[64,2,10]{2,1,0:T(2,128)} %pad_add_fusion), calls=%async_computation | async-start | bytes 131072 | tf_op jit(solution)/shard_map/all_to_all | solution.py:144
  333.6 5.0 copy-start.1
  346.7 5.0 copy-start.1
  359.9 5.0 copy-start.1
  373.1 5.0 copy-start.1
  386.3 5.0 copy-start.1
  399.5 5.0 copy-start.1
  412.7 5.0 copy-start.1
  425.9 5.0 copy-start.1
  439.1 5.0 copy-start.1
  452.2 5.0 copy-start.1
  465.4 5.0 copy-start.1
  478.6 5.0 copy-start.1
  491.9 5.0 copy-start.1
  505.1 5.0 copy-start.1
  518.2 5.0 copy-start.1
  531.4 5.0 copy-start.1
  539.2 19.5 %all-to-all-start.4 = ((f32[64,1,128]{2,1,0:T(1,128)}), f32[64,1,128]{2,1,0:T(1,128)S(1)}, u32[]{:S(2)}, u32[]{:S(2)}) async-start(f32[64,1,128]{2,1,0:T(1,128)} %reshape.582), calls=%async_computation.4 | async-start | bytes 65536 | tf_op jit(solution)/shard_map/all_to_all | solution.py:166
  558.7 19.3 %all-to-all-start.2 = ((f32[64,1,128]{2,1,0:T(1,128)}), f32[64,1,128]{2,1,0:T(1,128)S(1)}, u32[]{:S(2)}, u32[]{:S(2)}) async-start(f32[64,1,128]{2,1,0:T(1,128)} %reshape.580), calls=%async_computation.2 | async-start | bytes 65536 | tf_op jit(solution)/shard_map/all_to_all | solution.py:159
  578.0 10.9 %copy-start.3 = (s32[8,8]{1,0:T(8,128)S(1)}, s32[8,8]{1,0:T(8,128)}, u32[]{:S(2)}) copy-start(s32[8,8]{1,0:T(8,128)} %param.22) | copy-start | bytes 772
  578.0 11.0 %copy-start.2 = (f32[8,4,576]{2,0,1:T(8,128)S(1)}, f32[8,4,576]{2,0,1:T(8,128)}, u32[]{:S(2)}) copy-start(f32[8,4,576]{2,0,1:T(8,128)} %all-reduce.2.cloned.1.call-done) | copy-start | bytes 221188
  578.0 11.2 %copy-start.4 = (f32[512]{0:T(512)S(1)}, f32[512]{0:T(512)}, u32[]{:S(2)}) copy-start(f32[512]{0:T(512)} %param.16) | copy-start | bytes 6148
  578.0 196.5 %all-to-all-start.3 = ((bf16[64,2,4,8192]{3,2,1,0:T(4,128)(2,1)}), bf16[64,2,4,8192]{3,2,1,0:T(4,128)(2,1)}, u32[]{:S(2)}, u32[]{:S(2)}) async-start(bf16[64,2,4,8192]{3,2,1,0:T(4,128)(2,1)} %reshape.499), calls=%async_computation.3 | async-start | bytes 16777216 | tf_op jit(solution)/shard_map/all_to_all | solution.py:152
Sparse Core Ops, SparseCore 0:
  10.9 47.0 all-reduce.1
where the time goes:
time: 815 us; the launch traced here: 813 us
  waiting for transfers between devices  427 us (52%)
  local copies, waits for them, and re-layouts  177 us (22%)
  matrix products  112 us (14%)
  starting transfers between devices  45 us (6%)
  other arithmetic  35.3 us (4%)
  between operations  14.5 us (2%)
    all_to_all x1, waiting for transfers between devices, body(): lax.all_to_all(send_query, 'cache', split_axis=0, concat_axis=0, tiled=True)  205 us
    all_to_all x1, waiting for transfers between devices, body(): lax.all_to_all(outgoing(summed_here, owners_count, capacity, step_count),...  178 us
    gather x16, local copies, waits for them, and re-layouts, one_group(): latent_cache[slot_info[:, :seg_blocks]].reshape(group_slots, -1, channels)  96.6 us
    dot_general x16, matrix products, one_group(): jnp.einsum('gqc,gkc->gqk', query_rows, tokens_kv, preferred_element_type=...  74.1 us
    psum x1, waiting for transfers between devices, body(): summed = lax.psum(partial_sum, 'tensor')  35.7 us
    dot_general x16, matrix products, one_group(): jnp.einsum('gqk,gkl->gql', weights.astype(jnp.bfloat16), tokens_kv[..., :...  27.6 us
    another operation x1, local copies, waits for them, and re-layouts, attend_slots(): grouped_query = queries.reshape(groups, group_slots, -1, channels)  18.2 us
  transfers between devices with their start and end apart: 6, of which 4 were waited for; matrix products, arithmetic and copies ran while one was open for 7% of the time, Pallas kernels for 0%

commit v1 on v0

v1 whole, which is shorter than its diff:
```python
import functools

import jax
import jax.numpy as jnp
from jax import lax
from jax.experimental import pallas as pl
from jax.experimental.pallas import tpu as pltpu
from jax.sharding import PartitionSpec as P

LAT = 512
SEGS = 8
NY, NZ, NC, NX = 4, 8, 2, 4
GROUP = NZ * NC
WIDE = 640
QUARTER = 16

softmax_scale = 192.0 ** (-0.5)
masked_score = -1e30
rope_base = 10000.0


def place(y, z, c):
    return (y % NY * NZ + z % NZ) * NC + c


def spots():
    return [(y, z, c) for y in range(NY) for z in range(NZ) for c in range(NC)]


def along_y(array, by):
    return lax.ppermute(
        array, "cache", [(place(y, z, c), place(y + by, z, c)) for y, z, c in spots()]
    )


def along_x(array, by):
    return lax.ppermute(array, "tensor", [(i, (i + by) % NX) for i in range(NX)])


def other_core(array):
    return lax.ppermute(
        array, "cache", [(place(y, z, c), place(y, z, 1 - c)) for y, z, c in spots()]
    )


def rotate(values, places):
    half_width = values.shape[-1] // 2
    frequency = rope_base ** (-(jnp.arange(half_width, dtype=jnp.float32) * 2.0 / values.shape[-1]))
    angles = places.astype(jnp.float32)[..., None] * frequency
    cosine = jnp.cos(angles)
    sine_part = jnp.sin(angles)
    front_half = values[..., :half_width]
    back_half = values[..., half_width:]
    return jnp.concatenate(
        [front_half * cosine - back_half * sine_part, front_half * sine_part + back_half * cosine],
        -1,
    )


def finish_latent(summed, places, kv_gain):
    latent = summed[..., :LAT]
    normed = latent * lax.rsqrt(jnp.mean(latent * latent, -1, keepdims=True) + 1e-06) * kv_gain
    return jnp.concatenate([normed, rotate(summed[..., LAT:], places)], -1).astype(jnp.bfloat16)


def attend_kernel(owners, pieces, prior, *refs):
    blk_ref, live_ref, par_ref = refs[:3]
    refs = refs[3:]
    q_ref, w_ref = refs[:2]
    refs = refs[2:]
    count = len(pieces)
    kv_in = refs[:count]
    refs = refs[count:]
    if prior:
        p_ref, plse_ref = refs[:2]
        refs = refs[2:]
    out_ref, lse_ref, kv, acc, top, total, items, sems = refs
    rows = q_ref.shape[0]
    g = pl.program_id(0)

    @pl.when(g == 0)
    def _():
        parity = par_ref[0]
        copies = []
        for n, (owner, kind, blocks) in enumerate(pieces):
            if kind == "all":
                first = owner * 64
            else:
                side = parity if kind in "AB" else 1 - parity
                first = owner * 64 + side * 32 + (QUARTER if kind in "BR" else 0)
            copies.append(pltpu.make_async_copy(kv_in[n], kv.at[pl.ds(first, blocks)], sems.at[n]))
        for copy in copies:
            copy.start()
        for copy in copies:
            copy.wait()

    acc[...] = jnp.zeros_like(acc)
    top[...] = jnp.full_like(top, masked_score)
    total[...] = jnp.zeros_like(total)
    first = g * (owners * rows)

    def scan(i, n):
        items[n] = first + i
        return n + (live_ref[first + i] > 0).astype(jnp.int32)

    found = lax.fori_loop(0, owners * rows, scan, jnp.int32(0))

    def one(item, live):
        row = item & (rows - 1)
        owner = item // rows - g * owners
        q = q_ref[row]
        blocks = [owner * 64 + blk_ref[item * 8 + t] for t in range(8)]
        scores = []
        for h in range(2):
            keys = jnp.concatenate([kv[b] for b in blocks[4 * h : 4 * h + 4]], 0)
            scores.append(
                lax.dot_general(
                    q, keys, (((1,), (1,)), ((), ())), preferred_element_type=jnp.float32
                )
            )
        score = jnp.concatenate(scores, 1) * softmax_scale
        alive = lax.broadcasted_iota(jnp.int32, score.shape, 1) < live
        masked = jnp.where(alive, score, masked_score)
        highest = jnp.max(masked, 1, keepdims=True)
        weights = jnp.where(alive, jnp.exp(masked - highest), 0.0)
        summed = jnp.sum(weights, 1, keepdims=True)
        weights_b = weights.astype(jnp.bfloat16)
        result = None
        for h in range(2):
            vals = jnp.concatenate([kv[b, :, :LAT] for b in blocks[4 * h : 4 * h + 4]], 0)
            part = jnp.dot(
                weights_b[:, 256 * h : 256 * h + 256], vals, preferred_element_type=jnp.float32
            )
            result = part if result is None else result + part
        return row, highest, summed, result

    def merge(row, highest, summed, result):
        before = top[row]
        now = jnp.maximum(before, highest)
        keep = jnp.exp(before - now)
        add = jnp.exp(highest - now)
        top[row] = now
        total[row] = total[row] * keep + summed * add
        acc[row] = acc[row] * keep[:, :1] + result * add[:, :1]

    def pair(j, carry):
        first_item = items[2 * j]
        second_item = items[jnp.minimum(2 * j + 1, found - 1)]
        second_live = jnp.where(2 * j + 1 < found, live_ref[second_item], 0)
        one_result = one(first_item, live_ref[first_item])
        two_result = one(second_item, second_live)
        merge(*one_result)
        merge(*two_result)
        return carry

    lax.fori_loop(0, (found + 1) // 2, pair, 0)

    sums = total[...]
    has = sums > 0.0
    inverse = jnp.where(has, 1.0 / jnp.where(has, sums, 1.0), 0.0)
    lse = jnp.where(has, top[...] + jnp.log(jnp.where(has, sums, 1.0)), masked_score)
    total[...] = inverse
    if prior:
        earlier = plse_ref[...]
        most = jnp.maximum(lse, earlier)
        w_new = jnp.exp(lse - most)
        w_old = jnp.exp(earlier - most)
        both = w_new + w_old
        top[...] = w_new / both
        lse = most + jnp.log(both)
        diagonal = lax.broadcasted_iota(jnp.int32, lse.shape, 1) == lax.broadcasted_iota(
            jnp.int32, lse.shape, 2
        )
        lse_ref[...] = jnp.sum(jnp.where(diagonal, lse, 0.0), 1)
    else:
        lse_ref[...] = lse
    for j in range(8):
        span = slice(8 * j, 8 * j + 8)
        x = acc[:, span, :] * total[:, span, :1]
        x = x.reshape(rows * 8, LAT).astype(jnp.bfloat16)
        y = jnp.dot(x, w_ref[j], preferred_element_type=jnp.float32)
        upper = (lax.broadcasted_iota(jnp.int32, (rows * 8, 128), 0) & 7) < 4
        y = jnp.where(upper, y[:, :128], y[:, 128:]).reshape(rows, 8, 128)
        if prior:
            w_new = top[:, span, :]
            y = y * w_new + p_ref[:, span, :] * (1.0 - w_new)
        out_ref[:, span, :] = y.astype(out_ref.dtype)


def attend(queries, w_pairs, blocks, live, parity, arrays, pieces, owners, earlier=None):
    total_rows = queries.shape[0]
    half = total_rows // 2
    prior = earlier is not None
    row_block = lambda *tail: pl.BlockSpec(
        (half,) + tail, lambda g, *_: (g,) + (0,) * len(tail)
    )
    in_specs = [
        row_block(64, WIDE),
        pl.BlockSpec(w_pairs.shape, lambda g, *_: (0, 0, 0)),
    ] + [pl.BlockSpec(memory_space=pl.ANY)] * len(arrays)
    operands = [queries, w_pairs, *arrays]
    if prior:
        in_specs += [row_block(64, 128), row_block(64, 128)]
        operands += list(earlier)
        out_shape = [
            jax.ShapeDtypeStruct((total_rows, 64, 128), jnp.bfloat16),
            jax.ShapeDtypeStruct((total_rows, 128), jnp.float32),
        ]
        out_specs = [row_block(64, 128), row_block(128)]
    else:
        out_shape = [
            jax.ShapeDtypeStruct((total_rows, 64, 128), jnp.float32),
            jax.ShapeDtypeStruct((total_rows, 64, 128), jnp.float32),
        ]
        out_specs = [row_block(64, 128), row_block(64, 128)]
    return pl.pallas_call(
        functools.partial(attend_kernel, owners, pieces, prior),
        out_shape=out_shape,
        grid_spec=pltpu.PrefetchScalarGridSpec(
            num_scalar_prefetch=3,
            grid=(2,),
            in_specs=in_specs,
            out_specs=out_specs,
            scratch_shapes=[
                pltpu.VMEM((owners * 64, 64, WIDE), jnp.bfloat16),
                pltpu.VMEM((half, 64, LAT), jnp.float32),
                pltpu.VMEM((half, 64, 128), jnp.float32),
                pltpu.VMEM((half, 64, 128), jnp.float32),
                pltpu.SMEM((owners * half,), jnp.int32),
                pltpu.SemaphoreType.DMA((len(arrays),)),
            ],
        ),
        compiler_params=pltpu.CompilerParams(vmem_limit_bytes=58 * 1024 * 1024),
        cost_estimate=pl.CostEstimate(
            flops=owners * 32 * 64 * 512 * 1088 * 2,
            bytes_accessed=owners * 5 * 2**20 + 2**24,
            transcendentals=owners * 32 * 64 * 512,
        ),
    )(blocks, live, parity, *operands)


def tables(info, targets, half):
    slots = info[:, 0, :]
    owners = info[:, 1, :SEGS]
    lengths = info[:, 1, SEGS] * 64 + info[:, 1, SEGS + 1]
    rows = info.shape[0]
    segment = jnp.arange(SEGS, dtype=jnp.int32)
    match = (owners[None] == targets[:, None, None]).astype(jnp.int32)
    tokens = jnp.clip(lengths[:, None] - segment[None, :] * 512, 0, 512)
    live = jnp.sum(match * tokens[None], -1)
    blocks = jnp.sum(match[..., None] * slots.reshape(rows, SEGS, SEGS)[None], 2)
    count = targets.shape[0]
    live = live.reshape(count, 2, half).swapaxes(0, 1).reshape(-1)
    blocks = blocks.reshape(count, 2, half, SEGS).swapaxes(0, 1).reshape(-1)
    return blocks, live


def body(
    hidden, w_dkv, kv_gain, q_latent, q_rope, w_uv, latent_cache, block_slots, seg_owner, lengths
):
    row_count, step_count = hidden.shape[:2]
    channels = latent_cache.shape[-1]
    heads_dev = q_latent.shape[2] // LAT
    rope_width = channels - LAT
    me = lax.axis_index("cache")
    core = me % NC
    y_here = me // GROUP
    parity = lax.axis_index("tensor") % 2
    positions = lengths[:, None] + jnp.arange(step_count, dtype=jnp.int32)[None, :]

    roped = rotate(
        q_rope.reshape(row_count, step_count, heads_dev, rope_width).astype(jnp.float32),
        positions[..., None],
    ).astype(jnp.bfloat16)
    queries = jnp.concatenate(
        [q_latent.reshape(row_count, step_count, heads_dev, LAT), roped], -1
    ).swapaxes(1, 2)
    queries = queries.reshape(row_count, heads_dev * step_count, channels)
    second = jnp.concatenate([seg_owner, lengths[:, None] // 64, lengths[:, None] % 64], 1)
    second = jnp.pad(second, ((0, 0), (0, 64 - second.shape[1])))
    info = jnp.stack([block_slots, second], 1).astype(jnp.bfloat16)
    info = jnp.pad(info, ((0, 0), (0, heads_dev * step_count - 2), (0, 0)))
    message = jnp.concatenate([queries, info], -1)
    all_queries = lax.all_gather(
        message,
        "cache",
        axis=0,
        tiled=True,
        axis_index_groups=[[y * GROUP + i for i in range(GROUP)] for y in range(NY)],
    )

    held = jnp.pad(latent_cache, ((0, 0), (0, 0), (0, WIDE - channels)))
    half_a = lax.dynamic_slice_in_dim(held, parity * 32, QUARTER, 0)
    half_b = lax.dynamic_slice_in_dim(held, parity * 32 + QUARTER, QUARTER, 0)
    m_a = along_y(half_a, 1)
    p_b = along_y(half_b, -1)
    m_b = along_y(half_b, 1)
    p_a = along_y(half_a, -1)
    m_l = along_x(m_a, 1)
    p_r = along_x(p_b, -1)
    t_a = along_y(m_a, 1)
    t_b = along_y(p_b, -1)
    m_r = along_x(m_b, -1)
    p_l = along_x(p_a, 1)
    t_l = along_x(t_a, 1)
    t_r = along_x(t_b, -1)

    partial_sum = jnp.einsum("rsd,dc->rsc", hidden, w_dkv, preferred_element_type=jnp.float32)
    summed = lax.psum(partial_sum, "tensor")
    new_latent = finish_latent(summed, positions, kv_gain)
    own_scores = (
        jnp.einsum("rqc,rtc->rqt", queries, new_latent, preferred_element_type=jnp.float32)
        * softmax_scale
    )
    steps_of = jnp.arange(heads_dev * step_count) % step_count
    causal = (jnp.arange(step_count)[None, :] <= steps_of[:, None])[None]
    own_masked = jnp.where(causal, own_scores, masked_score)
    own_top = jnp.max(own_masked, -1)
    own_weights = jnp.where(causal, jnp.exp(own_masked - own_top[..., None]), 0.0)
    own_total = jnp.sum(own_weights, -1)
    own_sum = jnp.einsum("rqt,rtl->rql", own_weights, new_latent[..., :LAT].astype(jnp.float32))
    own_b = own_sum.astype(jnp.bfloat16).reshape(row_count, heads_dev, step_count, LAT)
    own_proj = jnp.einsum("rhsl,hlv->rhsv", own_b, w_uv, preferred_element_type=jnp.float32)
    own_proj = own_proj.reshape(row_count, heads_dev * step_count, -1)
    own_part = own_proj / own_total[..., None]
    own_lse = own_top + jnp.log(own_total)

    w_pairs = w_uv.reshape(heads_dev // 2, 2, LAT, -1).swapaxes(1, 2)
    w_pairs = w_pairs.reshape(heads_dev // 2, LAT, -1)
    table = all_queries[:, :2, channels:].astype(jnp.float32).astype(jnp.int32)
    offsets = jnp.array([0, NY - 1, 1, 2], jnp.int32)
    targets = (y_here + offsets) % NY * GROUP + me % GROUP
    half = all_queries.shape[0] // 2
    parities = parity[None].astype(jnp.int32)
    near_pieces = [(0, "all", 64)]
    near_arrays = [held]
    for owner, arrays in ((1, (m_a, m_b, m_l, m_r)), (2, (p_a, p_b, p_l, p_r))):
        near_pieces += [(owner, kind, QUARTER) for kind in "ABLR"]
        near_arrays += arrays
    blocks, live = tables(table, targets[:3], half)
    near = attend(
        all_queries, w_pairs, blocks, live, parities, near_arrays, near_pieces, 3
    )
    blocks, live = tables(table, targets[3:], half)
    far_pieces = [(0, kind, QUARTER) for kind in "ABLR"]
    part, lse = attend(
        all_queries, w_pairs, blocks, live, parities, (t_a, t_b, t_l, t_r), far_pieces, 1, near
    )

    width = part.shape[1]
    part = part.reshape(NZ, NC, row_count, width, -1)
    lse = lse[:, :width].reshape(NZ, NC, row_count, width)
    pick = lambda array, which: lax.dynamic_index_in_dim(array, which, 1, keepdims=False)
    mine, theirs = pick(part, core), other_core(pick(part, 1 - core))
    lse_mine, lse_theirs = pick(lse, core), other_core(pick(lse, 1 - core))
    most = jnp.maximum(lse_mine, lse_theirs)
    w_mine, w_theirs = jnp.exp(lse_mine - most), jnp.exp(lse_theirs - most)
    both = w_mine + w_theirs
    chip_part = mine * (w_mine / both)[..., None] + theirs * (w_theirs / both)[..., None]
    chip_part = chip_part.astype(jnp.bfloat16)
    chip_lse = most + jnp.log(both)
    along_z = [[place(y, z, c) for z in range(NZ)] for y in range(NY) for c in range(NC)]
    exchange = lambda array: lax.all_to_all(
        array, "cache", split_axis=0, concat_axis=0, axis_index_groups=along_z, tiled=True
    )
    home_part = exchange(chip_part)
    home_lse = exchange(chip_lse)
    largest = jnp.maximum(own_lse, jnp.max(home_lse, 0))
    factor = jnp.exp(home_lse - largest[None])
    own_factor = jnp.exp(own_lse - largest)
    numerator = jnp.sum(factor[..., None] * home_part, 0) + own_factor[..., None] * own_part
    denominator = jnp.sum(factor, 0) + own_factor
    attn_out = (numerator / denominator[..., None]).astype(jnp.bfloat16)
    attn_out = attn_out.reshape(row_count, heads_dev, step_count, -1).swapaxes(1, 2)
    return (attn_out.reshape(row_count, step_count, -1), new_latent)


def solution(mesh):
    in_specs = (
        P("cache", None, "tensor"),
        P("tensor", None),
        P(),
        P("cache", None, "tensor"),
        P("cache", None, "tensor"),
        P("tensor", None, None),
        P("cache", None, None),
        P("cache", None),
        P("cache", None),
        P("cache"),
    )
    out_specs = (P("cache", None, "tensor"), P("cache", None, None))
    return jax.shard_map(body, mesh=mesh, in_specs=in_specs, out_specs=out_specs, check_vma=False)
```

time: 815 us -> 312 us (0.38)
  waiting for transfers between devices: 427 us -> 147 us
  local copies, waits for them, and re-layouts: 177 us -> 32.9 us
  matrix products: 112 us -> 5.23 us
  Pallas kernels: 0 us -> 66.6 us
  other arithmetic: 35.3 us -> 9.85 us
  starting transfers between devices: 45 us -> 30.8 us
    all_to_all x5 -> x2, waiting for transfers between devices: 392 us -> 26.5 us  [body(): lax.all_to_all(array, 'cache', split_axis=0, concat_axis=0, axis_index_gr...]
    gather x23 -> x0, local copies, waits for them, and re-layouts: 118 us -> none  [the longest x16 96.6 us: one_group(): latent_cache[slot_info[:, :seg_blocks]].reshape(group_slots, -1, channels)]
    dot_general x36 -> x3, matrix products: 109 us -> 3 us  [the longest x1 2.32 us: body(): jnp.einsum('rhsl,hlv->rhsv', own_b, w_uv, preferred_element_type=jnp.floa...]
    ppermute x0 -> x14, waiting for transfers between devices: none -> 70.1 us  [the longest x6 55.3 us: along_y(): lax.ppermute(array, 'cache', [(place(y, z, c), place(y + by, z, c)) for y...]
    pallas_call x0 -> x2, Pallas kernels: none -> 66.6 us  [attend(): pl.pallas_call(functools.partial(attend_kernel, owners, pieces, prior), o...]
    all_to_all x5 -> x2, starting transfers between devices: 44.9 us -> 11.9 us  [body(): lax.all_to_all(array, 'cache', split_axis=0, concat_axis=0, axis_index_gr...]
    ppermute x0 -> x14, starting transfers between devices: none -> 18.9 us  [the longest x6 9.36 us: along_x(): lax.ppermute(array, 'tensor', [(i, (i + by) % NX) for i in range(NX)])]
    another operation x3 -> x4, local copies, waits for them, and re-layouts: 18.6 us -> 0.69 us  [the longest x1 0.68 us: tables(): blocks = blocks.reshape(count, 2, half, SEGS).swapaxes(0, 1).reshape(-1)]
  transfers between devices with their start and end apart: 6 -> 18, of which waited for: 4 -> 9; matrix products, arithmetic and copies ran while one was open for 7% -> 12% of each run, Pallas kernels for 0% -> 13%
where the time goes in v1:
time: 312 us; the launch traced here: 307 us
  waiting for transfers between devices  147 us (47%)
  Pallas kernels  66.6 us (21%)
  local copies, waits for them, and re-layouts  32.9 us (11%)
  starting transfers between devices  30.8 us (10%)
  between operations  14.5 us (5%)
  other arithmetic  9.85 us (3%)
  matrix products  5.23 us (2%)
    pallas_call x2, Pallas kernels, attend(): pl.pallas_call(functools.partial(attend_kernel, owners, pieces, prior), o...  66.6 us
    ppermute x6, waiting for transfers between devices, along_y(): lax.ppermute(array, 'cache', [(place(y, z, c), place(y + by, z, c)) for y...  55.3 us
    psum x1, waiting for transfers between devices, body(): summed = lax.psum(partial_sum, 'tensor')  46.5 us
    all_to_all x2, waiting for transfers between devices, body(): lax.all_to_all(array, 'cache', split_axis=0, concat_axis=0, axis_index_gr...  26.5 us
    ppermute x6, waiting for transfers between devices, along_x(): lax.ppermute(array, 'tensor', [(i, (i + by) % NX) for i in range(NX)])  12.8 us
    all_to_all x2, starting transfers between devices, body(): lax.all_to_all(array, 'cache', split_axis=0, concat_axis=0, axis_index_gr...  11.9 us
    ppermute x6, starting transfers between devices, along_x(): lax.ppermute(array, 'tensor', [(i, (i + by) % NX) for i in range(NX)])  9.36 us
    ppermute x6, starting transfers between devices, along_y(): lax.ppermute(array, 'cache', [(place(y, z, c), place(y + by, z, c)) for y...  7.37 us
  transfers between devices with their start and end apart: 18, of which 9 were waited for; matrix products, arithmetic and copies ran while one was open for 12% of the time, Pallas kernels for 13%

profile of v1, /device:TPU:1, one launch (start us, length us, event | category | flops | bytes accessed | tf_op | source)
XLA Modules:
  0.0 306.6 jit_solution(18403408210090768268)
XLA Ops:
  7.3 1.5 copy-done
  8.8 2.2 fusion.4
  11.7 46.5 %all-reduce.5.cloned.1.call-done = f32[8,4,576]{2,0,1:T(8,128)} async-done(((f32[8,4,576]{2,0,1:T(8,128)}), f32[8,4,576]{2,0,1:T(8,128)}) %all-reduce.5.cloned.1.call-update) | async-done | bytes 73744 | tf_op jit(solution)/shard_map/psum | solution.py:309
  61.2 3.5 %constant_dynamic-slice_fusion = (bf16[16,64,640]{2,1,0:T(8,128)(2,1)}, bf16[16,64,640]{2,1,0:T(8,128)(2,1)}) fusion(s32[]{:T(128)S(6)} %select_n.86, bf16[64,64,576]{2,1,0:T(8,128)(2,1)} %param.17, s32[]{:T(128)S(6)} %select_n.85), kind=kLoop, calls=%fused_computation.81 | loop fusion | bytes 7340040 | tf_op jit(solution)/shard_map/dynamic_slice | solution.py:294
  64.7 2.5 collective-permute-start.9
  68.7 24.2 %collective-permute-done.9.refs_10_ = bf16[16,64,640]{2,1,0:T(8,128)(2,1)S(1)} collective-permute-done((bf16[16,64,640]{2,1,0:T(8,128)(2,1)}, bf16[16,64,640]{2,1,0:T(8,128)(2,1)S(1)}, u32[]{:S(2)}, u32[]{:S(2)}) %collective-permute-start.9) | collective-permute-done | bytes 1310752 | tf_op jit(solution)/shard_map/ppermute | solution.py:31
  92.9 1.3 collective-permute-start.10
  94.2 5.1 %copy.182 = bf16[8,2,512,128]{3,1,2,0:T(2,128)(2,1)} copy(bf16[8,2,512,128]{3,2,1,0:T(8,128)(2,1)} %bitcast.111) | data formatting | bytes 4194304 | tf_op jit(solution)/shard_map/reshape | solution.py:328
  99.3 4.4 %reshape.377.refs_4_ = bf16[8,512,256]{2,1,0:T(8,128)(2,1)} reshape(bf16[8,512,2,128]{3,2,1,0:T(2,128)(2,1)} %bitcast.108) | data formatting | bytes 4194304 | tf_op jit(solution)/shard_map/reshape | solution.py:329
  103.7 5.6 %pad.15.refs_5_ = bf16[64,64,640]{2,1,0:T(8,128)(2,1)} pad(bf16[64,64,576]{2,1,0:T(8,128)(2,1)} %param.17, bf16[]{:T(256)} %constant.129.clone.1), padding=0_0x0_0x0_64 | pad | bytes 9961474 | tf_op jit(solution)/shard_map/jit(_pad)/pad | solution.py:292
  109.9 11.0 %collective-permute-done.2.refs_11_ = bf16[16,64,640]{2,1,0:T(8,128)(2,1)S(1)} collective-permute-done((bf16[16,64,640]{2,1,0:T(8,128)(2,1)}, bf16[16,64,640]{2,1,0:T(8,128)(2,1)S(1)}, u32[]{:S(2)}, u32[]{:S(2)}) %collective-permute-start.2) | collective-permute-done | bytes 1310752 | tf_op jit(solution)/shard_map/ppermute | solution.py:31
  120.9 2.4 collective-permute-start.11
  123.3 3.4 %collective-permute-start.3 = (bf16[16,64,640]{2,1,0:T(8,128)(2,1)S(1)}, bf16[16,64,640]{2,1,0:T(8,128)(2,1)}, u32[]{:S(2)}, u32[]{:S(2)}) collective-permute-start(bf16[16,64,640]{2,1,0:T(8,128)(2,1)S(1)} %collective-permute-done.2.refs_11_), channel_id=1, source_target_pairs={{0,192},{4,196},{8,200},{12,204},{16,208},{20,212},{24,216},{28,22... | collective-permute-start | bytes 3932168 | tf_op jit(solution)/shard_map/ppermute | solution.py:31
  126.8 3.5 %all-gather.2.cloned.1.call-done.refs_3_ = bf16[128,64,640]{2,1,0:T(8,128)(2,1)} async-done(((bf16[8,64,640]{2,1,0:T(8,128)(2,1)}), bf16[128,64,640]{2,1,0:T(8,128)(2,1)}) %all-gather.2.cloned.1.call-update) | async-done | bytes 10485776 | tf_op jit(solution)/shard_map/all_gather | solution.py:284
  131.5 1.4 collective-permute-start.7
  133.0 1.5 collective-permute-start.8
  134.6 20.0 %collective-permute-done.1.refs_5_ = bf16[16,64,640]{2,1,0:T(8,128)(2,1)} collective-permute-done((bf16[16,64,640]{2,1,0:T(8,128)(2,1)}, bf16[16,64,640]{2,1,0:T(8,128)(2,1)}, u32[]{:S(2)}, u32[]{:S(2)}) %collective-permute-start.1) | collective-permute-done | bytes 1310752 | tf_op jit(solution)/shard_map/ppermute | solution.py:31
  154.6 2.7 collective-permute-start.5
  158.2 1.6 reshape.379.refs_0_
  162.1 1.2 select_reduce_fusion.refs_1_
  163.4 12.8 %collective-permute-done.8.refs_9_ = bf16[16,64,640]{2,1,0:T(8,128)(2,1)} collective-permute-done((bf16[16,64,640]{2,1,0:T(8,128)(2,1)}, bf16[16,64,640]{2,1,0:T(8,128)(2,1)}, u32[]{:S(2)}, u32[]{:S(2)}) %collective-permute-start.8) | collective-permute-done | bytes 1310752 | tf_op jit(solution)/shard_map/ppermute | solution.py:37
  176.1 41.1 %shard_map.122 = (f32[128,64,128]{2,1,0:T(8,128)}, f32[128,64,128]{2,1,0:T(8,128)}) custom-call(s32[3072]{0:T(1024)} %reshape.379.refs_0_, s32[384]{0:T(512)} %reshape.381.refs_1_, s32[1]{0:T(128)} %bitcast.11.refs_2_, bf16[128,64,640]{2,1,0:T(8,128)(2,1)} %all-gather.2.cloned.1.call-done.refs_3_, bf16[8,512,256]{2,1,0:T(8,128)(2,1)} %reshape.377.refs_4_, ...), custom_call_target="tpu_custom_call" | custom-call | flops 6845104128 | bytes 32505856 | tf_op jit(solution)/shard_map/pallas_call | solution.py:216
  218.3 25.5 %shard_map.123 = (bf16[128,64,128]{2,1,0:T(8,128)(2,1)}, f32[128,128]{1,0:T(8,128)}) custom-call(s32[1024]{0:T(1024)} %reshape_transpose_reshape.4.refs_0_, s32[128]{0:T(128)} %select_reduce_fusion.refs_1_, s32[1]{0:T(128)} %bitcast.11.refs_2_, bf16[128,64,640]{2,1,0:T(8,128)(2,1)} %all-gather.2.cloned.1.call-done.refs_3_, ...), custom_call_target="tpu_custom_call" | custom-call | flops 2281701376 | bytes 22020096 | tf_op jit(solution)/shard_map/pallas_call | solution.py:216
  243.9 1.3 dynamic-slice_bitcast_fusion
  245.2 2.1 collective-permute-start.13
  247.5 2.1 collective-permute-done.12
  250.3 8.3 %all-to-all-start = ((f32[8,1,512]{2,1,0:T(1,128)}), f32[8,1,512]{2,1,0:T(1,128)S(1)}, u32[]{:S(2)}, u32[]{:S(2)}) async-start(f32[8,1,512]{2,1,0:T(1,128)} %reshape.391), calls=%async_computation | async-start | bytes 32768 | tf_op jit(solution)/shard_map/all_to_all | solution.py:363
  258.6 3.1 %fusion.3 = bf16[8,8,64,128]{3,2,1,0:T(8,128)(2,1)} fusion(bf16[8,8,64,128]{3,2,1,0:T(8,128)(2,1)S(1)} %collective-permute-done.13, f32[8,8,64]{2,1,0:T(8,128)S(1)} %get-tuple-element.34, f32[8,8,64]{2,1,0:T(8,128)S(1)} %get-tuple-element.32, bf16[8,2,8,64,128]{4,3,2,1,0:T(8,128)(2,1)} %bitcast.110, s32[]{:T(128)S(6)} %select_n.88), kind=kLoop, calls=%fused_computation.4 | loop fusion | flops 3145728 | bytes 3178500 | tf_op jit(solution)/shard_map/convert_element_type | solution.py:360
  261.7 3.5 %all-to-all-done = f32[8,1,512]{2,1,0:T(1,128)S(1)} async-done(((f32[8,1,512]{2,1,0:T(1,128)}), f32[8,1,512]{2,1,0:T(1,128)S(1)}, u32[]{:S(2)}, u32[]{:S(2)}) %all-to-all-start) | async-done | bytes 16416 | tf_op jit(solution)/shard_map/all_to_all | solution.py:363
  265.2 3.6 %all-to-all-start.1 = ((bf16[8,8,64,128]{3,2,1,0:T(8,128)(2,1)}), bf16[8,8,64,128]{3,2,1,0:T(8,128)(2,1)S(1)}, u32[]{:S(2)}, u32[]{:S(2)}) async-start(bf16[8,8,64,128]{3,2,1,0:T(8,128)(2,1)} %fusion.3), calls=%async_computation.1 | async-start | bytes 2097152 | tf_op jit(solution)/shard_map/all_to_all | solution.py:363
  272.6 2.3 fusion.12
  274.9 23.0 %all-to-all-done.1 = bf16[8,8,64,128]{3,2,1,0:T(8,128)(2,1)S(1)} async-done(((bf16[8,8,64,128]{3,2,1,0:T(8,128)(2,1)}), bf16[8,8,64,128]{3,2,1,0:T(8,128)(2,1)S(1)}, u32[]{:S(2)}, u32[]{:S(2)}) %all-to-all-start.1) | async-done | bytes 1048608 | tf_op jit(solution)/shard_map/all_to_all | solution.py:363
  (120 shorter events, 17.8 us)
Async XLA Ops:
  7.2 1.6 copy-start
  7.2 3.9 %copy-start.13 = (s32[8]{0:T(128)S(1)}, s32[8]{0:T(128)}, u32[]{:S(2)}) copy-start(s32[8]{0:T(128)} %param.20) | copy-start | bytes 100
  7.2 3.9 %copy-start.8 = (bf16[8,4,1024]{2,1,0:T(4,128)(2,1)S(1)}, bf16[8,4,1024]{2,1,0:T(4,128)(2,1)}, u32[]{:S(2)}) copy-start(bf16[8,4,1024]{2,1,0:T(4,128)(2,1)} %param.15) | copy-start | bytes 196612
  7.2 4.4 %copy-start.10 = (s32[8,8]{1,0:T(8,128)S(1)}, s32[8,8]{1,0:T(8,128)}, u32[]{:S(2)}) copy-start(s32[8,8]{1,0:T(8,128)} %param.19) | copy-start | bytes 772
  7.2 4.4 %copy-start.11 = (s32[8,64]{1,0:T(8,128)S(1)}, s32[8,64]{1,0:T(8,128)}, u32[]{:S(2)}) copy-start(s32[8,64]{1,0:T(8,128)} %param.18) | copy-start | bytes 6148
  7.2 52.2 %copy-start.5 = (bf16[8,4,8192]{2,1,0:T(4,128)(2,1)S(1)}, bf16[8,4,8192]{2,1,0:T(4,128)(2,1)}, u32[]{:S(2)}) copy-start(bf16[8,4,8192]{2,1,0:T(4,128)(2,1)} %param.14) | copy-start | bytes 1572868
  7.2 51.0 %all-reduce.5.cloned.1.call-start = ((), (), s32[]{:S(2)}) async-start(), calls=%async_computation.3 | async-start | bytes 163840 | tf_op jit(solution)/shard_map/psum | solution.py:309
  11.0 119.3 %all-gather.2.cloned.1.call-start = ((), (), s32[]{:S(2)}) async-start(), calls=%async_computation.2 | async-start | bytes 11141120 | tf_op jit(solution)/shard_map/all_gather | solution.py:284
  64.7 28.1 %collective-permute-start.9 = (bf16[16,64,640]{2,1,0:T(8,128)(2,1)}, bf16[16,64,640]{2,1,0:T(8,128)(2,1)S(1)}, u32[]{:S(2)}, u32[]{:S(2)}) collective-permute-start(bf16[16,64,640]{2,1,0:T(8,128)(2,1)} %get-tuple-element.27), channel_id=1, source_target_pairs={{0,192},{4,196},{8,200},{12,204},{16,208},{20,212},{24,216},{28,22... | collective-permute-start | bytes 3932168 | tf_op jit(solution)/shard_map/ppermute | solution.py:31
  67.2 53.8 %collective-permute-start.2 = (bf16[16,64,640]{2,1,0:T(8,128)(2,1)}, bf16[16,64,640]{2,1,0:T(8,128)(2,1)S(1)}, u32[]{:S(2)}, u32[]{:S(2)}) collective-permute-start(bf16[16,64,640]{2,1,0:T(8,128)(2,1)} %get-tuple-element.26), channel_id=1, source_target_pairs={{0,192},{4,196},{8,200},{12,204},{16,208},{20,212},{24,216},{28,22... | collective-permute-start | bytes 3932168 | tf_op jit(solution)/shard_map/ppermute | solution.py:31
  67.7 59.0 %collective-permute-start = (bf16[16,64,640]{2,1,0:T(8,128)(2,1)}, bf16[16,64,640]{2,1,0:T(8,128)(2,1)}, u32[]{:S(2)}, u32[]{:S(2)}) collective-permute-start(bf16[16,64,640]{2,1,0:T(8,128)(2,1)} %get-tuple-element.27), channel_id=1, source_target_pairs={{0,64},{4,68},{8,72},{12,76},{16,80},{20,84},{24,88},{28,92},{32,9... | collective-permute-start | bytes 3932168 | tf_op jit(solution)/shard_map/ppermute | solution.py:31
  68.6 62.9 %collective-permute-start.6 = (bf16[16,64,640]{2,1,0:T(8,128)(2,1)}, bf16[16,64,640]{2,1,0:T(8,128)(2,1)}, u32[]{:S(2)}, u32[]{:S(2)}) collective-permute-start(bf16[16,64,640]{2,1,0:T(8,128)(2,1)} %get-tuple-element.26), channel_id=1, source_target_pairs={{0,64},{4,68},{8,72},{12,76},{16,80},{20,84},{24,88},{28,92},{32,9... | collective-permute-start | bytes 3932168 | tf_op jit(solution)/shard_map/ppermute | solution.py:31
  92.9 6.4 %copy-start.2 = (bf16[16,64,640]{2,1,0:T(8,128)(2,1)}, bf16[16,64,640]{2,1,0:T(8,128)(2,1)S(1)}, u32[]{:S(2)}) copy-start(bf16[16,64,640]{2,1,0:T(8,128)(2,1)S(1)} %collective-permute-done.9.refs_10_) | copy-start | bytes 3932164
  92.9 40.1 %collective-permute-start.10 = (bf16[16,64,640]{2,1,0:T(8,128)(2,1)S(1)}, bf16[16,64,640]{2,1,0:T(8,128)(2,1)}, u32[]{:S(2)}, u32[]{:S(2)}) collective-permute-start(bf16[16,64,640]{2,1,0:T(8,128)(2,1)S(1)} %collective-permute-done.9.refs_10_), channel_id=1, source_target_pairs={{0,1},{1,2},{2,3},{3,0},{4,5},{5,6},{6,7},{7,4},{8,9},{9,10},{10,1... | collective-permute-start | bytes 3932168 | tf_op jit(solution)/shard_map/ppermute | solution.py:37
  103.7 5.6 %copy-start.14 = (s32[4]{0:T(128)S(1)}, s32[4]{0:T(128)}, u32[]{:S(2)}) copy-start(s32[4]{0:T(128)} %constant.147.clone) | copy-start | bytes 52
  120.9 55.2 %copy-start.3 = (bf16[16,64,640]{2,1,0:T(8,128)(2,1)}, bf16[16,64,640]{2,1,0:T(8,128)(2,1)S(1)}, u32[]{:S(2)}) copy-start(bf16[16,64,640]{2,1,0:T(8,128)(2,1)S(1)} %collective-permute-done.2.refs_11_) | copy-start | bytes 3932164
  120.9 42.4 %collective-permute-start.11 = (bf16[16,64,640]{2,1,0:T(8,128)(2,1)S(1)}, bf16[16,64,640]{2,1,0:T(8,128)(2,1)}, u32[]{:S(2)}, u32[]{:S(2)}) collective-permute-start(bf16[16,64,640]{2,1,0:T(8,128)(2,1)S(1)} %collective-permute-done.2.refs_11_), channel_id=1, source_target_pairs={{0,3},{1,0},{2,1},{3,2},{4,7},{5,4},{6,5},{7,6},{8,11},{9,8},{10,9... | collective-permute-start | bytes 3932168 | tf_op jit(solution)/shard_map/ppermute | solution.py:37
  123.3 31.3 %collective-permute-start.3 = (bf16[16,64,640]{2,1,0:T(8,128)(2,1)S(1)}, bf16[16,64,640]{2,1,0:T(8,128)(2,1)}, u32[]{:S(2)}, u32[]{:S(2)}) collective-permute-start(bf16[16,64,640]{2,1,0:T(8,128)(2,1)S(1)} %collective-permute-done.2.refs_11_), channel_id=1, source_target_pairs={{0,192},{4,196},{8,200},{12,204},{16,208},{20,212},{24,216},{28,22... | collective-permute-start | bytes 3932168 | tf_op jit(solution)/shard_map/ppermute | solution.py:31
  126.8 27.9 %collective-permute-start.1 = (bf16[16,64,640]{2,1,0:T(8,128)(2,1)}, bf16[16,64,640]{2,1,0:T(8,128)(2,1)}, u32[]{:S(2)}, u32[]{:S(2)}) collective-permute-start(bf16[16,64,640]{2,1,0:T(8,128)(2,1)} %collective-permute-done.refs_6_), channel_id=1, source_target_pairs={{0,64},{4,68},{8,72},{12,76},{16,80},{20,84},{24,88},{28,92},{32,9... | collective-permute-start | bytes 3932168 | tf_op jit(solution)/shard_map/ppermute | solution.py:31
  131.5 31.9 %collective-permute-start.7 = (bf16[16,64,640]{2,1,0:T(8,128)(2,1)}, bf16[16,64,640]{2,1,0:T(8,128)(2,1)}, u32[]{:S(2)}, u32[]{:S(2)}) collective-permute-start(bf16[16,64,640]{2,1,0:T(8,128)(2,1)} %collective-permute-done.refs_6_), channel_id=1, source_target_pairs={{0,1},{1,2},{2,3},{3,0},{4,5},{5,6},{6,7},{7,4},{8,9},{9,10},{10,1... | collective-permute-start | bytes 3932168 | tf_op jit(solution)/shard_map/ppermute | solution.py:37
  133.0 43.2 %collective-permute-start.8 = (bf16[16,64,640]{2,1,0:T(8,128)(2,1)}, bf16[16,64,640]{2,1,0:T(8,128)(2,1)}, u32[]{:S(2)}, u32[]{:S(2)}) collective-permute-start(bf16[16,64,640]{2,1,0:T(8,128)(2,1)} %collective-permute-done.6.refs_7_), channel_id=1, source_target_pairs={{0,3},{1,0},{2,1},{3,2},{4,7},{5,4},{6,5},{7,6},{8,11},{9,8},{10,9... | collective-permute-start | bytes 3932168 | tf_op jit(solution)/shard_map/ppermute | solution.py:37
  154.6 62.6 %collective-permute-start.4 = (bf16[16,64,640]{2,1,0:T(8,128)(2,1)}, bf16[16,64,640]{2,1,0:T(8,128)(2,1)S(1)}, u32[]{:S(2)}, u32[]{:S(2)}) collective-permute-start(bf16[16,64,640]{2,1,0:T(8,128)(2,1)} %collective-permute-done.1.refs_5_), channel_id=1, source_target_pairs={{0,1},{1,2},{2,3},{3,0},{4,5},{5,6},{6,7},{7,4},{8,9},{9,10},{10,1... | collective-permute-start | bytes 3932168 | tf_op jit(solution)/shard_map/ppermute | solution.py:37
  154.6 62.6 %collective-permute-start.5 = (bf16[16,64,640]{2,1,0:T(8,128)(2,1)}, bf16[16,64,640]{2,1,0:T(8,128)(2,1)}, u32[]{:S(2)}, u32[]{:S(2)}) collective-permute-start(bf16[16,64,640]{2,1,0:T(8,128)(2,1)} %collective-permute-done.3.refs_6_), channel_id=1, source_target_pairs={{0,3},{1,0},{2,1},{3,2},{4,7},{5,4},{6,5},{7,6},{8,11},{9,8},{10,9... | collective-permute-start | bytes 3932168 | tf_op jit(solution)/shard_map/ppermute | solution.py:37
  243.8 3.4 %copy-start.6 = (f32[8,4,576]{2,0,1:T(8,128)S(1)}, f32[8,4,576]{2,0,1:T(8,128)}, u32[]{:S(2)}) copy-start(f32[8,4,576]{2,0,1:T(8,128)} %all-reduce.5.cloned.1.call-done) | copy-start | bytes 221188
  243.8 3.5 %copy-start.9 = (f32[128,128]{1,0:T(8,128)S(1)}, f32[128,128]{1,0:T(8,128)}, u32[]{:S(2)}) copy-start(f32[128,128]{1,0:T(8,128)} %get-tuple-element.8) | copy-start | bytes 196612
  245.2 13.4 %collective-permute-start.13 = (bf16[8,8,64,128]{3,2,1,0:T(8,128)(2,1)S(1)}, bf16[8,8,64,128]{3,2,1,0:T(8,128)(2,1)S(1)}, u32[]{:S(2)}, u32[]{:S(2)}) collective-permute-start(bf16[8,8,64,128]{3,2,1,0:T(8,128)(2,1)S(1)} %dynamic-slice_bitcast_fusion), channel_id=1, source_target_pairs={{0,4},{4,0},{8,12},{12,8},{16,20},{20,16},{24,28},{28,24},{32,36},... | collective-permute-start | bytes 3145736 | tf_op jit(solution)/shard_map/ppermute | solution.py:41
  247.4 2.2 collective-permute-start.12
  250.3 14.9 %all-to-all-start = ((f32[8,1,512]{2,1,0:T(1,128)}), f32[8,1,512]{2,1,0:T(1,128)S(1)}, u32[]{:S(2)}, u32[]{:S(2)}) async-start(f32[8,1,512]{2,1,0:T(1,128)} %reshape.391), calls=%async_computation | async-start | bytes 32768 | tf_op jit(solution)/shard_map/all_to_all | solution.py:363
  258.6 10.2 %copy-start.12 = (f32[512]{0:T(512)S(1)}, f32[512]{0:T(512)}, u32[]{:S(2)}) copy-start(f32[512]{0:T(512)} %param.13) | copy-start | bytes 6148
  265.2 32.7 %all-to-all-start.1 = ((bf16[8,8,64,128]{3,2,1,0:T(8,128)(2,1)}), bf16[8,8,64,128]{3,2,1,0:T(8,128)(2,1)S(1)}, u32[]{:S(2)}, u32[]{:S(2)}) async-start(bf16[8,8,64,128]{3,2,1,0:T(8,128)(2,1)} %fusion.3), calls=%async_computation.1 | async-start | bytes 2097152 | tf_op jit(solution)/shard_map/all_to_all | solution.py:363
  269.0 5.9 %copy-start.7 = (bf16[8,4,576]{2,1,0:T(4,128)(2,1)}, bf16[8,4,576]{2,1,0:T(4,128)(2,1)S(1)}, u32[]{:S(2)}) copy-start(bf16[8,4,576]{2,1,0:T(4,128)(2,1)S(1)} %copy.153) | copy-start | bytes 110596
  272.6 27.1 %copy-start.1 = (bf16[1792,576]{0,1:T(8,128)(2,1)S(1)}, bf16[1792,576]{0,1:T(8,128)(2,1)}, u32[]{:S(2)}) copy-start(bf16[1792,576]{0,1:T(8,128)(2,1)} %param.12) | copy-start | bytes 6193156
  (1 other events, 1.1 us)
Sparse Core Ops, SparseCore 0:
  11.1 47.0 all-reduce.4
  61.3 68.8 all-gather.1

commit v2 on v1

v2 whole, which is shorter than its diff:
```python
import functools

import jax
import jax.numpy as jnp
from jax import lax
from jax.experimental import pallas as pl
from jax.experimental.pallas import tpu as pltpu
from jax.sharding import PartitionSpec as P

LAT = 512
SEGS = 8
NY, NZ, NC, NX = 4, 8, 2, 4
GROUP = NZ * NC
WIDE = 640
AT_ONCE = 4
PAIRS = 8
VMEM_BYTES = 60 * 1024 * 1024

softmax_scale = 192.0 ** (-0.5)
masked_score = -1e30
rope_base = 10000.0


def place(y, z, c):
    return (y % NY * NZ + z % NZ) * NC + c


def spots():
    return [(y, z, c) for y in range(NY) for z in range(NZ) for c in range(NC)]


def along_y(array, by):
    return lax.ppermute(
        array, "cache", [(place(y, z, c), place(y + by, z, c)) for y, z, c in spots()]
    )


def along_x(array, by):
    return lax.ppermute(array, "tensor", [(i, (i + by) % NX) for i in range(NX)])


def other_core(array):
    return lax.ppermute(
        array, "cache", [(place(y, z, c), place(y, z, 1 - c)) for y, z, c in spots()]
    )


def angle_tables(places, width):
    half_width = width // 2
    frequency = rope_base ** (-(jnp.arange(half_width, dtype=jnp.float32) * 2.0 / width))
    angles = places.astype(jnp.float32)[..., None] * frequency
    return lax.optimization_barrier((jnp.cos(angles), jnp.sin(angles)))


def rotate(values, cosine, sine_part):
    half_width = values.shape[-1] // 2
    front_half = values[..., :half_width]
    back_half = values[..., half_width:]
    return jnp.concatenate(
        [front_half * cosine - back_half * sine_part, front_half * sine_part + back_half * cosine],
        -1,
    )


def finish_latent(summed, cosine, sine_part, kv_gain):
    latent = summed[..., :LAT]
    normed = latent * lax.rsqrt(jnp.mean(latent * latent, -1, keepdims=True) + 1e-06) * kv_gain
    roped = rotate(summed[..., LAT:], cosine, sine_part)
    return jnp.concatenate([normed, roped], -1).astype(jnp.bfloat16)


def gate(*arrays):
    anywhere = pl.BlockSpec(memory_space=pltpu.HBM)
    return pl.pallas_call(
        lambda *refs: None,
        out_shape=[jax.ShapeDtypeStruct(a.shape, a.dtype) for a in arrays],
        in_specs=[anywhere] * len(arrays),
        out_specs=[anywhere] * len(arrays),
        input_output_aliases={i: i for i in range(len(arrays))},
        compiler_params=pltpu.CompilerParams(vmem_limit_bytes=VMEM_BYTES),
    )(*arrays)


def pack_kernel(par_ref, len_in, cache, out_a, out_b, len_out, held, sem):
    copy = pltpu.make_async_copy(cache.at[pl.ds(par_ref[0] * 32, 32)], held, sem)
    copy.start()
    for row in range(len_in.shape[0]):
        len_out[row] = len_in[row]
    copy.wait()
    for quarter, out in enumerate((out_a, out_b)):

        def one(pair, carry):
            ropes = []
            for b in range(2):
                block = held[quarter * 2 * PAIRS + 2 * pair + b]
                out[pair, 64 * b : 64 * b + 64, :] = block[:, :LAT]
                rope = block[:, LAT:]
                rope = jnp.concatenate([rope[:32], rope[32:]], 1)
                ropes += [rope[:16], rope[16:]]
            out[pair, 128:, :] = jnp.concatenate(ropes, 1)
            return carry

        lax.fori_loop(0, PAIRS, one, 0)


def pack(latent_cache, parity, lengths):
    shape = jax.ShapeDtypeStruct((PAIRS, 144, LAT), latent_cache.dtype)
    return pl.pallas_call(
        pack_kernel,
        out_shape=[shape, shape, jax.ShapeDtypeStruct(lengths.shape, lengths.dtype)],
        grid_spec=pltpu.PrefetchScalarGridSpec(
            num_scalar_prefetch=2,
            grid=(),
            in_specs=[pl.BlockSpec(memory_space=pl.ANY)],
            out_specs=[pl.BlockSpec(memory_space=pltpu.VMEM)] * 2
            + [pl.BlockSpec(memory_space=pltpu.SMEM)],
            scratch_shapes=[
                pltpu.VMEM((32,) + latent_cache.shape[1:], latent_cache.dtype),
                pltpu.SemaphoreType.DMA,
            ],
        ),
        compiler_params=pltpu.CompilerParams(vmem_limit_bytes=VMEM_BYTES),
    )(parity, lengths, latent_cache)


def attend_kernel(owners, pieces, unused, stage, *refs):
    blk_ref, live_ref, par_ref, q_in, w_ref = refs[:5]
    refs = refs[5:]
    kv_in = refs[: len(pieces)]
    refs = refs[len(pieces) + unused :]
    if stage != "first":
        state_in, lse_in = refs[:2]
        refs = refs[2:]
    state, lse_ref, kv, queries, normal, slot_lse, projected, items, kv_sems, q_sems, row_sems = refs
    rows = lse_ref.shape[0]

    copies = [[] for _ in range(owners)]
    for n, (owner, side, offset) in enumerate(pieces):
        first = owner * 4 * PAIRS + offset
        if side == "mine":
            first = first + par_ref[0] * 2 * PAIRS
        elif side == "other":
            first = first + (1 - par_ref[0]) * 2 * PAIRS
        copies[owner].append(
            pltpu.make_async_copy(
                kv_in[n], kv.at[pl.ds(first, kv_in[n].shape[0])], kv_sems.at[n]
            )
        )
    for some in copies:
        for copy in some:
            copy.start()
    if stage == "middle":
        whole = pltpu.make_async_copy(state_in, state, row_sems.at[0])
        whole.start()

    def scan(i, n):
        items[n] = i
        return n + (live_ref[i] > 0).astype(jnp.int32)

    ends = [jnp.int32(0)]
    for o in range(owners):
        ends.append(lax.fori_loop(o * rows, (o + 1) * rows, scan, ends[-1], unroll=8))
    found = ends[-1]

    def row_of(slot):
        return items[slot] & (rows - 1)

    def fetch(slot):
        return pltpu.make_async_copy(q_in.at[row_of(slot)], queries.at[slot], q_sems.at[slot])

    def load_row(slot):
        return pltpu.make_async_copy(state.at[row_of(slot)], normal.at[slot, :, :128], row_sems.at[slot])

    def store_row(slot):
        return pltpu.make_async_copy(projected.at[slot], state.at[row_of(slot)], row_sems.at[slot])

    def each(action):
        def step(slot, carry):
            action(slot)
            return carry

        lax.fori_loop(0, found, step, 0)

    each(lambda slot: fetch(slot).start())
    if stage == "first":
        state[...] = jnp.zeros_like(state)
        lse_ref[...] = jnp.full_like(lse_ref, masked_score)
    else:
        lse_ref[...] = lse_in[...]

    low_lanes = lax.broadcasted_iota(jnp.int32, (16, 128), 1) < 64

    def blocks_of(slot):
        item = items[slot]
        return [(item // rows) * 64 + blk_ref[item * 8 + t] for t in range(8)]

    def latents(b):
        if stage == "first":
            return kv[b, :, :LAT]
        return kv[b // 2, pl.ds(pl.multiple_of((b & 1) * 64, 64), 64), :]

    def keys(b):
        if stage == "first":
            return kv[b]
        some = kv[b // 2, 128:, pl.ds(pl.multiple_of((b & 1) * 256, 256), 256)]
        nothing = jnp.zeros((16, 128), some.dtype)
        groups = [some[:, :128], some[:, 128:]]
        ropes = [jnp.where(low_lanes, g, nothing) for g in groups]
        ropes += [jnp.where(low_lanes, nothing, g) for g in groups]
        return jnp.concatenate([latents(b), jnp.concatenate(ropes, 0)], 1)

    def score_of(slot, blocks):
        q = queries[slot]
        channels = LAT + 64
        q = q[:, :channels]
        if stage != "first":
            q = jnp.concatenate([q, q[:, LAT:]], 1)
        scores = []
        for h in range(2):
            some = jnp.concatenate([keys(b) for b in blocks[4 * h : 4 * h + 4]], 0)
            scores.append(
                lax.dot_general(
                    q, some, (((1,), (1,)), ((), ())), preferred_element_type=jnp.float32
                )
            )
        return jnp.concatenate(scores, 1) * softmax_scale

    def soften(score, live):
        alive = lax.broadcasted_iota(jnp.int32, score.shape, 1) < live
        masked = jnp.where(alive, score, masked_score)
        highest = jnp.max(masked, 1, keepdims=True)
        weights = jnp.where(alive, jnp.exp(masked - highest), 0.0)
        summed = jnp.sum(weights, 1, keepdims=True)
        return weights.astype(jnp.bfloat16), 1.0 / summed, highest + jnp.log(summed)

    def value_of(weights_b, blocks):
        result = None
        for h in range(2):
            vals = jnp.concatenate([latents(b) for b in blocks[4 * h : 4 * h + 4]], 0)
            part = jnp.dot(
                weights_b[:, 256 * h : 256 * h + 256], vals, preferred_element_type=jnp.float32
            )
            result = part if result is None else result + part
        return result

    for o in range(owners):
        begin, end = ends[o], ends[o + 1]
        for copy in copies[o]:
            copy.wait()

        def several(j, carry):
            first = begin + AT_ONCE * j
            group = [jnp.minimum(first + i, end - 1) for i in range(AT_ONCE)]
            for i, slot in enumerate(group):

                @pl.when(first + i < end)
                def _():
                    fetch(slot).wait()

            blocks = [blocks_of(slot) for slot in group]
            scores = [score_of(slot, some) for slot, some in zip(group, blocks)]
            soft = [soften(score, live_ref[items[slot]]) for score, slot in zip(scores, group)]
            results = [value_of(one[0], some) for one, some in zip(soft, blocks)]
            for slot, one, result in zip(group, soft, results):
                normal[slot] = result * one[1]
                slot_lse[slot] = jnp.broadcast_to(one[2], slot_lse.shape[1:])
            return carry

        lax.fori_loop(0, (end - begin + AT_ONCE - 1) // AT_ONCE, several, 0)

    def project(group, carry):
        some = pl.ds(pl.multiple_of(group * 32, 32), 32)
        for j in range(8):
            span = slice(8 * j, 8 * j + 8)
            x = normal[some, span, :].reshape(32 * 8, LAT).astype(jnp.bfloat16)
            w = jnp.concatenate([w_ref[2 * j], w_ref[2 * j + 1]], 1)
            y = jnp.dot(x, w, preferred_element_type=jnp.float32)
            upper = (lax.broadcasted_iota(jnp.int32, (32 * 8, 128), 0) & 7) < 4
            projected[some, span, :] = jnp.where(upper, y[:, :128], y[:, 128:]).reshape(32, 8, 128)
        return carry

    lax.fori_loop(0, (found + 31) // 32, project, 0)
    if stage == "middle":
        whole.wait()
    if stage == "last":
        each(lambda slot: load_row(slot).start())
        each(lambda slot: load_row(slot).wait())

    diagonal = lax.broadcasted_iota(jnp.int32, (64, 128), 0) == lax.broadcasted_iota(
        jnp.int32, (64, 128), 1
    )
    for o in range(owners):
        begin, end = ends[o], ends[o + 1]

        def merge(j, carry):
            group = [jnp.minimum(begin + AT_ONCE * j + i, end - 1) for i in range(AT_ONCE)]
            where = [row_of(slot) for slot in group]
            values = []
            for slot, row in zip(group, where):
                across = jnp.broadcast_to(lse_ref[pl.ds(row, 1), :], (64, 128))
                before = jnp.sum(jnp.where(diagonal, across, 0.0), 1, keepdims=True)
                added = slot_lse[slot]
                most = jnp.maximum(before, added)
                keep = jnp.exp(before - most)
                add = jnp.exp(added - most)
                both = keep + add
                lse = most + jnp.log(both)
                lse_row = jnp.sum(jnp.where(diagonal, lse, 0.0), 0, keepdims=True)
                old = normal[slot, :, :128] if stage == "last" else state[row]
                values.append((lse_row, (old * keep + projected[slot] * add) / both))
            for slot, row, (lse_row, value) in zip(group, where, values):
                lse_ref[pl.ds(row, 1), :] = lse_row
                if stage == "last":
                    projected[slot] = value
                else:
                    state[row] = value
            return carry

        lax.fori_loop(0, (end - begin + AT_ONCE - 1) // AT_ONCE, merge, 0)
    if stage == "last":
        each(lambda slot: store_row(slot).start())
        each(lambda slot: store_row(slot).wait())


def attend(queries, w_uv, blocks, live, parity, arrays, pieces, owners, stage, after, earlier):
    rows = queries.shape[0]
    slots = owners * GROUP * 2
    all_blocks = (owners * 64,) if stage == "first" else (owners * 4 * PAIRS,)
    whole = pl.BlockSpec(memory_space=pltpu.VMEM)
    anywhere = pl.BlockSpec(memory_space=pltpu.HBM)
    in_specs = [anywhere, whole] + [anywhere] * len(arrays)
    in_specs += [anywhere] * len(after)
    operands = [queries, w_uv, *arrays, *after, *earlier]
    if earlier:
        in_specs += [anywhere, whole]
    return pl.pallas_call(
        functools.partial(attend_kernel, owners, pieces, len(after), stage),
        out_shape=[
            jax.ShapeDtypeStruct((rows, 64, 128), jnp.float32),
            jax.ShapeDtypeStruct((rows, 128), jnp.float32),
        ],
        grid_spec=pltpu.PrefetchScalarGridSpec(
            num_scalar_prefetch=3,
            grid=(),
            in_specs=in_specs,
            out_specs=[anywhere if stage == "last" else whole, whole],
            scratch_shapes=[
                pltpu.VMEM(all_blocks + arrays[0].shape[1:], jnp.bfloat16),
                pltpu.VMEM((slots, 64, WIDE), jnp.bfloat16),
                pltpu.VMEM((slots, 64, LAT), jnp.float32),
                pltpu.VMEM((slots, 64, 128), jnp.float32),
                pltpu.VMEM((slots, 64, 128), jnp.float32),
                pltpu.SMEM((owners * rows,), jnp.int32),
                pltpu.SemaphoreType.DMA((len(arrays),)),
                pltpu.SemaphoreType.DMA((slots,)),
                pltpu.SemaphoreType.DMA((slots,)),
            ],
        ),
        input_output_aliases={3 + len(operands) - 2: 0} if stage == "last" else {},
        compiler_params=pltpu.CompilerParams(vmem_limit_bytes=VMEM_BYTES),
        cost_estimate=pl.CostEstimate(
            flops=owners * 32 * 64 * 512 * 1088 * 2,
            bytes_accessed=owners * 5 * 2**20 + 2**24,
            transcendentals=owners * 32 * 64 * 512,
        ),
    )(blocks, live, parity, *operands)


def tables(info, targets):
    slots = info[:, 0, :]
    owners = info[:, 1, :SEGS]
    lengths = info[:, 1, SEGS] * 64 + info[:, 1, SEGS + 1]
    rows = info.shape[0]
    segment = jnp.arange(SEGS, dtype=jnp.int32)
    match = (owners[None] == targets[:, None, None]).astype(jnp.int32)
    tokens = jnp.clip(lengths[:, None] - segment[None, :] * 512, 0, 512)
    live = jnp.sum(match * tokens[None], -1)
    blocks = jnp.sum(match[..., None] * slots.reshape(rows, SEGS, SEGS)[None], 2)
    return blocks.reshape(-1), live.reshape(-1)


def body(
    hidden, w_dkv, kv_gain, q_latent, q_rope, w_uv, latent_cache, block_slots, seg_owner, lengths
):
    row_count, step_count = hidden.shape[:2]
    channels = latent_cache.shape[-1]
    heads_dev = q_latent.shape[2] // LAT
    rope_width = channels - LAT
    me = lax.axis_index("cache")
    core = me % NC
    y_here = me // GROUP
    parity = lax.axis_index("tensor") % 2
    parities = parity.astype(jnp.int32)[None]
    half_a, half_b, lengths = pack(latent_cache, parities, lengths)
    positions = lengths[:, None] + jnp.arange(step_count, dtype=jnp.int32)[None, :]

    cosine, sine_part = angle_tables(positions, rope_width)

    roped = rotate(
        q_rope.reshape(row_count, step_count, heads_dev, rope_width).astype(jnp.float32),
        cosine[:, :, None],
        sine_part[:, :, None],
    ).astype(jnp.bfloat16)
    queries = jnp.concatenate(
        [q_latent.reshape(row_count, step_count, heads_dev, LAT), roped], -1
    ).swapaxes(1, 2)
    queries = queries.reshape(row_count, heads_dev * step_count, channels)
    second = jnp.concatenate([seg_owner, lengths[:, None] // 64, lengths[:, None] % 64], 1)
    second = jnp.pad(second, ((0, 0), (0, 64 - second.shape[1])))
    info = jnp.stack([block_slots, second], 1).astype(jnp.bfloat16)
    info = jnp.pad(info, ((0, 0), (0, heads_dev * step_count - 2), (0, 0)))
    message = jnp.concatenate([queries, info], -1)
    all_queries = lax.all_gather(
        message,
        "cache",
        axis=0,
        tiled=True,
        axis_index_groups=[[y * GROUP + i for i in range(GROUP)] for y in range(NY)],
    )

    nothing = jnp.minimum(lengths[0], 0).astype(hidden.dtype)
    partial_sum = jnp.einsum("rsd,dc->rsc", hidden + nothing, w_dkv, preferred_element_type=jnp.float32)
    summed = lax.psum(partial_sum, "tensor")
    m_a = along_y(half_a, 1)
    p_b = along_y(half_b, -1)
    half_a, half_b, m_a, p_b = gate(half_a, half_b, m_a, p_b)
    m_b = along_y(half_b, 1)
    p_a = along_y(half_a, -1)
    m_l = along_x(m_a, 1)
    p_r = along_x(p_b, -1)
    m_b, p_a, m_l, p_r, m_a, p_b, summed = gate(m_b, p_a, m_l, p_r, m_a, p_b, summed)
    t_a = along_y(m_a, 1)
    t_b = along_y(p_b, -1)
    m_r = along_x(m_b, -1)
    p_l = along_x(p_a, 1)
    new_latent = finish_latent(summed, cosine, sine_part, kv_gain)
    own_scores = (
        jnp.einsum("rqc,rtc->rqt", queries, new_latent, preferred_element_type=jnp.float32)
        * softmax_scale
    )
    steps_of = jnp.arange(heads_dev * step_count) % step_count
    causal = (jnp.arange(step_count)[None, :] <= steps_of[:, None])[None]
    own_masked = jnp.where(causal, own_scores, masked_score)
    own_top = jnp.max(own_masked, -1)
    own_weights = jnp.where(causal, jnp.exp(own_masked - own_top[..., None]), 0.0)
    own_total = jnp.sum(own_weights, -1)
    own_sum = jnp.einsum("rqt,rtl->rql", own_weights, new_latent[..., :LAT].astype(jnp.float32))
    own_b = own_sum.astype(jnp.bfloat16).reshape(row_count, heads_dev, step_count, LAT)
    own_proj = jnp.einsum("rhsl,hlv->rhsv", own_b, w_uv, preferred_element_type=jnp.float32)
    own_proj = own_proj.reshape(row_count, heads_dev * step_count, -1)
    own_part = own_proj / own_total[..., None]
    own_lse = own_top + jnp.log(own_total)

    table = all_queries[:, :2, channels:].astype(jnp.float32).astype(jnp.int32)
    offsets = jnp.array([0, NY - 1, 1, 2], jnp.int32)
    targets = (y_here + offsets) % NY * GROUP + me % GROUP

    def stage_of(name, which, lists, after, earlier=()):
        blocks, live = tables(table, targets[which])
        pieces, arrays = [], []
        for owner, quarters in enumerate(lists):
            if quarters is None:
                pieces.append((owner, "all", 0))
                arrays.append(latent_cache)
            else:
                pieces += [(owner, "mine", 0), (owner, "mine", PAIRS)]
                pieces += [(owner, "other", 0), (owner, "other", PAIRS)]
                arrays += quarters
        return attend(
            all_queries, w_uv, blocks, live, parities, arrays, pieces, len(lists), name, after, earlier
        )

    state = stage_of("first", slice(0, 1), [None], (m_l, p_r))
    t_a, t_b, m_r, p_l, *state = gate(t_a, t_b, m_r, p_l, *state)
    t_l = along_x(t_a, 1)
    t_r = along_x(t_b, -1)
    state = stage_of(
        "middle",
        slice(1, 3),
        [(m_a, m_b, m_l, m_r), (p_a, p_b, p_l, p_r)],
        (t_a, t_b, own_lse),
        tuple(state),
    )
    part, lse = stage_of("last", slice(3, 4), [(t_a, t_b, t_l, t_r)], (), tuple(state))

    width = part.shape[1]
    part = part.reshape(NZ, NC, row_count, width, -1)
    lse = lse[:, :width].reshape(NZ, NC, row_count, width)
    pick = lambda array, which: lax.dynamic_index_in_dim(array, which, 1, keepdims=False)
    mine, theirs = pick(part, core), other_core(pick(part, 1 - core).astype(jnp.bfloat16))
    lse_mine, lse_theirs = pick(lse, core), other_core(pick(lse, 1 - core))
    most = jnp.maximum(lse_mine, lse_theirs)
    w_mine, w_theirs = jnp.exp(lse_mine - most), jnp.exp(lse_theirs - most)
    both = w_mine + w_theirs
    chip_part = mine * (w_mine / both)[..., None] + theirs * (w_theirs / both)[..., None]
    chip_lse = most + jnp.log(both)
    nearest = lambda array: lax.reduce_precision(array, 8, 7)
    high = nearest(chip_lse)
    middle = nearest(chip_lse - high)
    low = chip_lse - high - middle
    stats = jnp.concatenate(
        [jnp.concatenate([high, middle], 2), jnp.concatenate([low, jnp.zeros_like(low)], 2)], 1
    ).astype(jnp.bfloat16)
    chip_part = chip_part.astype(jnp.bfloat16).reshape(NZ, row_count * width, -1)
    along_z = [[place(y, z, c) for z in range(NZ)] for y in range(NY) for c in range(NC)]
    got = lax.all_to_all(
        jnp.concatenate([chip_part, stats], 1),
        "cache",
        split_axis=0,
        concat_axis=0,
        axis_index_groups=along_z,
        tiled=True,
    )
    home_part = got[:, : row_count * width].reshape(NZ, row_count, width, -1)
    stats = got[:, row_count * width :].astype(jnp.float32)
    home_lse = (
        stats[:, :row_count, :width] + stats[:, :row_count, width:]
    ) + stats[:, row_count:, :width]
    largest = jnp.maximum(own_lse, jnp.max(home_lse, 0))
    factor = jnp.exp(home_lse - largest[None])
    own_factor = jnp.exp(own_lse - largest)
    numerator = jnp.sum(factor[..., None] * home_part, 0) + own_factor[..., None] * own_part
    denominator = jnp.sum(factor, 0) + own_factor
    attn_out = (numerator / denominator[..., None]).astype(jnp.bfloat16)
    attn_out = attn_out.reshape(row_count, heads_dev, step_count, -1).swapaxes(1, 2)
    return (attn_out.reshape(row_count, step_count, -1), new_latent)


def solution(mesh):
    in_specs = (
        P("cache", None, "tensor"),
        P("tensor", None),
        P(),
        P("cache", None, "tensor"),
        P("cache", None, "tensor"),
        P("tensor", None, None),
        P("cache", None, None),
        P("cache", None),
        P("cache", None),
        P("cache"),
    )
    out_specs = (P("cache", None, "tensor"), P("cache", None, None))
    return jax.shard_map(body, mesh=mesh, in_specs=in_specs, out_specs=out_specs, check_vma=False)
```

time: 312 us -> 218 us (0.70); the launches traced: 307 us -> 217 us
  waiting for transfers between devices: 147 us -> 84.7 us
  local copies, waits for them, and re-layouts: 32.9 us -> 12.4 us
  Pallas kernels: 66.6 us -> 46.5 us
  starting transfers between devices: 30.8 us -> 36.4 us
  other arithmetic: 9.85 us -> 15 us
    psum x1, waiting for transfers between devices: 46.5 us -> 7.92 us  [body(): summed = lax.psum(partial_sum, 'tensor')]
    pallas_call x2 -> x7, Pallas kernels: 66.6 us -> 46.5 us  [the longest x3 41.4 us: attend(): pl.pallas_call(functools.partial(attend_kernel, owners, pieces, len(after...]
    ppermute x6, waiting for transfers between devices: 55.3 us -> 36.9 us  [along_y(): lax.ppermute(array, 'cache', [(place(y, z, c), place(y + by, z, c)) for y...]
    reshape x6 -> x3, local copies, waits for them, and re-layouts: 12 us -> 2.06 us  [tables(): return (blocks.reshape(-1), live.reshape(-1))]
    pad x1 -> x0, local copies, waits for them, and re-layouts: 5.56 us -> none  [body(): held = jnp.pad(latent_cache, ((0, 0), (0, 0), (0, WIDE - channels)))]
    ppermute x2, starting transfers between devices: 2.18 us -> 6.98 us  [other_core(): lax.ppermute(array, 'cache', [(place(y, z, c), place(y, z, 1 - c)) for y,...]
    ppermute x6, waiting for transfers between devices: 12.8 us -> 9.09 us  [along_x(): lax.ppermute(array, 'tensor', [(i, (i + by) % NX) for i in range(NX)])]
    all_gather x1, waiting for transfers between devices: 3.51 us -> 0.01 us  [body(): lax.all_gather(message, 'cache', axis=0, tiled=True, axis_index_groups=[[...]
  transfers between devices with their start and end apart: 18 -> 17, of which waited for: 9 -> 14; matrix products, arithmetic and copies ran while one was open for 12% -> 9% of each run, Pallas kernels for 13% -> 14%
where the time goes in v2:
time: 218 us; the launch traced here: 217 us
  waiting for transfers between devices  84.7 us (39%)
  Pallas kernels  46.5 us (21%)
  starting transfers between devices  36.4 us (17%)
  between operations  16.6 us (8%)
  other arithmetic  15 us (7%)
  local copies, waits for them, and re-layouts  12.4 us (6%)
  matrix products  5.24 us (2%)
    pallas_call x3, Pallas kernels, attend(): pl.pallas_call(functools.partial(attend_kernel, owners, pieces, len(after...  41.4 us
    ppermute x6, waiting for transfers between devices, along_y(): lax.ppermute(array, 'cache', [(place(y, z, c), place(y + by, z, c)) for y...  36.9 us
    all_to_all x1, waiting for transfers between devices, body(): lax.all_to_all(jnp.concatenate([chip_part, stats], 1), 'cache', split_axi...  28.3 us
    all_to_all x1, starting transfers between devices, body(): lax.all_to_all(jnp.concatenate([chip_part, stats], 1), 'cache', split_axi...  11.5 us
    ppermute x6, starting transfers between devices, along_y(): lax.ppermute(array, 'cache', [(place(y, z, c), place(y + by, z, c)) for y...  9.5 us
    ppermute x6, waiting for transfers between devices, along_x(): lax.ppermute(array, 'tensor', [(i, (i + by) % NX) for i in range(NX)])  9.09 us
    ppermute x6, starting transfers between devices, along_x(): lax.ppermute(array, 'tensor', [(i, (i + by) % NX) for i in range(NX)])  8.35 us
    psum x1, waiting for transfers between devices, body(): summed = lax.psum(partial_sum, 'tensor')  7.92 us
  transfers between devices with their start and end apart: 17, of which 14 were waited for; matrix products, arithmetic and copies ran while one was open for 9% of the time, Pallas kernels for 14%

profile of v2, /device:TPU:1, one launch (start us, length us, event | category | flops | bytes accessed | tf_op | source)
XLA Modules:
  0.0 216.8 jit_solution(3467694097755110971)
XLA Ops:
  8.1 5.1 %shard_map.122 = (bf16[8,144,512]{2,1,0:T(8,128)(2,1)}, bf16[8,144,512]{2,1,0:T(8,128)(2,1)}, s32[8]{0:T(128)}) custom-call(s32[1]{0:T(128)} %bitcast.1.par_ref.refs_2_, s32[8]{0:T(128)} %len_in.1, bf16[64,64,576]{2,1,0:T(8,128)(2,1)} %refs_5_.1), custom_call_target="tpu_custom_call" | custom-call | tf_op jit(solution)/shard_map/pallas_call | solution.py:108
  13.9 1.4 fusion.5
  16.2 1.5 maximum_bitcast_fusion
  19.4 2.2 %collective-permute-start = (bf16[8,144,512]{2,1,0:T(8,128)(2,1)}, bf16[8,144,512]{2,1,0:T(8,128)(2,1)S(1)}, u32[]{:S(2)}, u32[]{:S(2)}) collective-permute-start(bf16[8,144,512]{2,1,0:T(8,128)(2,1)} %get-tuple-element.33.refs_0_), channel_id=1, source_target_pairs={{0,64},{4,68},{8,72},{12,76},{16,80},{20,84},{24,88},{28,92},{32,9... | collective-permute-start | bytes 3538952 | tf_op jit(solution)/shard_map/ppermute | solution.py:33
  21.6 1.5 collective-permute-start.1
  23.2 23.9 %collective-permute-done.refs_2_ = bf16[8,144,512]{2,1,0:T(8,128)(2,1)S(1)} collective-permute-done((bf16[8,144,512]{2,1,0:T(8,128)(2,1)}, bf16[8,144,512]{2,1,0:T(8,128)(2,1)S(1)}, u32[]{:S(2)}, u32[]{:S(2)}) %collective-permute-start) | collective-permute-done | bytes 1179680 | tf_op jit(solution)/shard_map/ppermute | solution.py:33
  47.0 1.2 collective-permute-done.1.refs_3_
  48.2 1.6 collective-permute-start.2
  49.8 1.5 collective-permute-start.3
  51.3 2.5 %collective-permute-start.4 = (bf16[8,144,512]{2,1,0:T(8,128)(2,1)}, bf16[8,144,512]{2,1,0:T(8,128)(2,1)S(1)}, u32[]{:S(2)}, u32[]{:S(2)}) collective-permute-start(bf16[8,144,512]{2,1,0:T(8,128)(2,1)} %get-tuple-element.37.refs_4_), channel_id=1, source_target_pairs={{0,1},{1,2},{2,3},{3,0},{4,5},{5,6},{6,7},{7,4},{8,9},{9,10},{10,1... | collective-permute-start | bytes 3538952 | tf_op jit(solution)/shard_map/ppermute | solution.py:39
  53.8 1.3 collective-permute-start.5
  55.7 7.9 %all-reduce.5.cloned.1.call-done.refs_6_ = f32[8,4,576]{2,1,0:T(4,128)} async-done(((f32[8,4,576]{2,1,0:T(4,128)}), f32[8,4,576]{2,1,0:T(4,128)}) %all-reduce.5.cloned.1.call-update) | async-done | bytes 73744 | tf_op jit(solution)/shard_map/psum | solution.py:423
  63.7 11.2 %collective-permute-done.2.refs_0_ = bf16[8,144,512]{2,1,0:T(8,128)(2,1)} collective-permute-done((bf16[8,144,512]{2,1,0:T(8,128)(2,1)}, bf16[8,144,512]{2,1,0:T(8,128)(2,1)}, u32[]{:S(2)}, u32[]{:S(2)}) %collective-permute-start.2) | collective-permute-done | bytes 1179680 | tf_op jit(solution)/shard_map/ppermute | solution.py:33
  75.4 4.5 %collective-permute-done.4.refs_2_ = bf16[8,144,512]{2,1,0:T(8,128)(2,1)S(1)} collective-permute-done((bf16[8,144,512]{2,1,0:T(8,128)(2,1)}, bf16[8,144,512]{2,1,0:T(8,128)(2,1)S(1)}, u32[]{:S(2)}, u32[]{:S(2)}) %collective-permute-start.4) | collective-permute-done | bytes 1179680 | tf_op jit(solution)/shard_map/ppermute | solution.py:39
  81.0 2.7 %collective-permute-start.7 = (bf16[8,144,512]{2,1,0:T(8,128)(2,1)}, bf16[8,144,512]{2,1,0:T(8,128)(2,1)}, u32[]{:S(2)}, u32[]{:S(2)}) collective-permute-start(bf16[8,144,512]{2,1,0:T(8,128)(2,1)} %get-tuple-element.40.refs_10_), channel_id=1, source_target_pairs={{0,192},{4,196},{8,200},{12,204},{16,208},{20,212},{24,216},{28,22... | collective-permute-start | bytes 3538952 | tf_op jit(solution)/shard_map/ppermute | solution.py:33
  83.6 1.9 collective-permute-start.8
  88.4 1.4 fusion.65
  91.7 1.3 compare_convert_fusion.2
  93.7 1.9 select_reduce_fusion
  95.6 11.3 %shard_map.125 = (f32[128,64,128]{2,1,0:T(8,128)}, f32[128,128]{1,0:T(8,128)}) custom-call(s32[1024]{0:T(1024)} %reshape.434.refs_0_, s32[128]{0:T(128)} %get-tuple-element.66.refs_1_, s32[1]{0:T(128)} %bitcast.1.par_ref.refs_2_, bf16[128,64,640]{2,1,0:T(8,128)(2,1)} %all-gather.2.cloned.1.call-done.refs_3_, bf16[16,512,128]{2,1,0:T(8,128)(2,1)} %refs_4_.5, ...), custom_call_target="tpu_custom_call" | custom-call | flops 2281701376 | bytes 22020096 | tf_op jit(solution)/shard_map/pallas_call | solution.py:336
  108.0 3.0 %collective-permute-done.9.refs_3_ = bf16[8,144,512]{2,1,0:T(8,128)(2,1)} collective-permute-done((bf16[8,144,512]{2,1,0:T(8,128)(2,1)}, bf16[8,144,512]{2,1,0:T(8,128)(2,1)}, u32[]{:S(2)}, u32[]{:S(2)}) %collective-permute-start.9) | collective-permute-done | bytes 1179680 | tf_op jit(solution)/shard_map/ppermute | solution.py:39
  111.0 2.7 %collective-permute-start.11 = (bf16[8,144,512]{2,1,0:T(8,128)(2,1)}, bf16[8,144,512]{2,1,0:T(8,128)(2,1)}, u32[]{:S(2)}, u32[]{:S(2)}) collective-permute-start(bf16[8,144,512]{2,1,0:T(8,128)(2,1)} %get-tuple-element.48.refs_14_.refs_6_), channel_id=1, source_target_pairs={{0,3},{1,0},{2,1},{3,2},{4,7},{5,4},{6,5},{7,6},{8,11},{9,8},{10,9... | collective-permute-start | bytes 3538952 | tf_op jit(solution)/shard_map/ppermute | solution.py:39
  116.1 18.9 %shard_map.127 = (f32[128,64,128]{2,1,0:T(8,128)}, f32[128,128]{1,0:T(8,128)}) custom-call(s32[2048]{0:T(1024)} %reshape.435.refs_0_, s32[256]{0:T(256)} %bitcast.143, s32[1]{0:T(128)} %bitcast.1.par_ref.refs_2_, bf16[128,64,640]{2,1,0:T(8,128)(2,1)} %all-gather.2.cloned.1.call-done.refs_3_, bf16[16,512,128]{2,1,0:T(8,128)(2,1)} %refs_4_.5, ...), custom_call_target="tpu_custom_call" | custom-call | flops 4563402752 | bytes 27262976 | tf_op jit(solution)/shard_map/pallas_call | solution.py:336
  136.5 11.2 %shard_map.128 = (f32[128,64,128]{2,1,0:T(8,128)}, f32[128,128]{1,0:T(8,128)}) custom-call(s32[1024]{0:T(1024)} %reshape.433.refs_0_, s32[128]{0:T(128)} %get-tuple-element.67.refs_1_, s32[1]{0:T(128)} %bitcast.1.par_ref.refs_2_, bf16[128,64,640]{2,1,0:T(8,128)(2,1)} %all-gather.2.cloned.1.call-done.refs_3_, ...), custom_call_target="tpu_custom_call", output_to_operand_aliasing={{0}: (9, {})} | custom-call | flops 2281701376 | bytes 22020096 | tf_op jit(solution)/shard_map/pallas_call | solution.py:336
  147.8 2.8 %fusion.30 = bf16[8,8,64,128]{3,2,1,0:T(8,128)(2,1)} fusion(f32[8,2,8,64,128]{4,3,2,1,0:T(8,128)} %bitcast.128, s32[]{:T(128)S(6)} %select_n.84), kind=kLoop, calls=%fused_computation.22 | loop fusion | bytes 2097156 | tf_op jit(solution)/shard_map/convert_element_type | solution.py:490
  150.6 6.9 %collective-permute-start.13 = (bf16[8,8,64,128]{3,2,1,0:T(8,128)(2,1)}, bf16[8,8,64,128]{3,2,1,0:T(8,128)(2,1)S(1)}, u32[]{:S(2)}, u32[]{:S(2)}) collective-permute-start(bf16[8,8,64,128]{3,2,1,0:T(8,128)(2,1)} %fusion.30), channel_id=1, source_target_pairs={{0,4},{4,0},{8,12},{12,8},{16,20},{20,16},{24,28},{28,24},{32,36},... | collective-permute-start | bytes 3145736 | tf_op jit(solution)/shard_map/ppermute | solution.py:43
  157.6 2.1 collective-permute-done.12
  160.0 2.5 %fusion.4 = bf16[8,8,64,128]{3,2,1,0:T(8,128)(2,1)S(1)} fusion(bf16[8,8,64,128]{3,2,1,0:T(8,128)(2,1)S(1)} %collective-permute-done.13, f32[8,2,8,64,128]{4,3,2,1,0:T(8,128)} %bitcast.129, s32[]{:T(128)S(6)} %select_n.83, f32[8,8,64]{2,1,0:T(8,128)S(1)} %get-tuple-element.83, f32[8,8,64]{2,1,0:T(8,128)S(1)} %get-tuple-element.82), kind=kLoop, calls=%fused_computation.6 | loop fusion | flops 2621440 | bytes 4227076 | tf_op jit(solution)/shard_map/convert_element_type | solution.py:504
  163.6 11.5 %all-to-all-start = ((bf16[8,528,128]{2,1,0:T(8,128)(2,1)}), bf16[8,528,128]{2,1,0:T(8,128)(2,1)S(1)}, u32[]{:S(2)}, u32[]{:S(2)}) async-start(bf16[8,528,128]{2,1,0:T(8,128)(2,1)} %fusion.29), calls=%async_computation | async-start | bytes 2162688 | tf_op jit(solution)/shard_map/all_to_all | solution.py:506
  175.6 1.1 copy.135
  176.7 28.3 %all-to-all-done = bf16[8,528,128]{2,1,0:T(8,128)(2,1)S(1)} async-done(((bf16[8,528,128]{2,1,0:T(8,128)(2,1)}), bf16[8,528,128]{2,1,0:T(8,128)(2,1)S(1)}, u32[]{:S(2)}, u32[]{:S(2)}) %all-to-all-start) | async-done | bytes 1081376 | tf_op jit(solution)/shard_map/all_to_all | solution.py:506
  206.5 2.1 fusion.25
  (119 shorter events, 19.5 us)
Async XLA Ops:
  8.0 5.9 %copy-start = (bf16[1792,576]{0,1:T(8,128)(2,1)S(1)}, bf16[1792,576]{0,1:T(8,128)(2,1)}, u32[]{:S(2)}) copy-start(bf16[1792,576]{0,1:T(8,128)(2,1)} %param.12) | copy-start | bytes 6193156
  8.0 55.7 %all-reduce.5.cloned.1.call-start = ((), (), s32[]{:S(2)}) async-start(), calls=%async_computation.2 | async-start | bytes 163840 | tf_op jit(solution)/shard_map/psum | solution.py:423
  8.1 5.9 %copy-start.8 = (bf16[8,4,1792]{2,1,0:T(4,128)(2,1)S(1)}, bf16[8,4,1792]{2,1,0:T(4,128)(2,1)}, u32[]{:S(2)}) copy-start(bf16[8,4,1792]{2,1,0:T(4,128)(2,1)} %param.11) | copy-start | bytes 344068
  13.2 2.2 %copy-start.15 = (s32[8]{0:T(128)S(1)}, s32[8]{0:T(128)}, u32[]{:S(2)}) copy-start(s32[8]{0:T(128)} %get-tuple-element.30) | copy-start | bytes 100
  13.2 2.5 %copy-start.9 = (bf16[8,4,1024]{2,1,0:T(4,128)(2,1)S(1)}, bf16[8,4,1024]{2,1,0:T(4,128)(2,1)}, u32[]{:S(2)}) copy-start(bf16[8,4,1024]{2,1,0:T(4,128)(2,1)} %param.15) | copy-start | bytes 196612
  15.3 75.1 %all-gather.2.cloned.1.call-start = ((), (), s32[]{:S(2)}) async-start(), calls=%async_computation.1 | async-start | bytes 11141120 | tf_op jit(solution)/shard_map/all_gather | solution.py:413
  16.2 2.0 copy-start.12
  16.2 2.1 copy-start.13
  18.0 1.4 copy-start.4
  19.4 27.6 %collective-permute-start = (bf16[8,144,512]{2,1,0:T(8,128)(2,1)}, bf16[8,144,512]{2,1,0:T(8,128)(2,1)S(1)}, u32[]{:S(2)}, u32[]{:S(2)}) collective-permute-start(bf16[8,144,512]{2,1,0:T(8,128)(2,1)} %get-tuple-element.33.refs_0_), channel_id=1, source_target_pairs={{0,64},{4,68},{8,72},{12,76},{16,80},{20,84},{24,88},{28,92},{32,9... | collective-permute-start | bytes 3538952 | tf_op jit(solution)/shard_map/ppermute | solution.py:33
  21.6 33.4 %copy-start.16 = (s32[4]{0:T(128)S(1)}, s32[4]{0:T(128)}, u32[]{:S(2)}) copy-start(s32[4]{0:T(128)} %constant.147.clone) | copy-start | bytes 52
  21.6 26.6 %collective-permute-start.1 = (bf16[8,144,512]{2,1,0:T(8,128)(2,1)}, bf16[8,144,512]{2,1,0:T(8,128)(2,1)}, u32[]{:S(2)}, u32[]{:S(2)}) collective-permute-start(bf16[8,144,512]{2,1,0:T(8,128)(2,1)} %get-tuple-element.34.refs_1_), channel_id=1, source_target_pairs={{0,192},{4,196},{8,200},{12,204},{16,208},{20,212},{24,216},{28,22... | collective-permute-start | bytes 3538952 | tf_op jit(solution)/shard_map/ppermute | solution.py:33
  47.0 1.2 copy-start.3
  48.2 26.7 %collective-permute-start.2 = (bf16[8,144,512]{2,1,0:T(8,128)(2,1)}, bf16[8,144,512]{2,1,0:T(8,128)(2,1)}, u32[]{:S(2)}, u32[]{:S(2)}) collective-permute-start(bf16[8,144,512]{2,1,0:T(8,128)(2,1)} %get-tuple-element.35), channel_id=1, source_target_pairs={{0,64},{4,68},{8,72},{12,76},{16,80},{20,84},{24,88},{28,92},{32,9... | collective-permute-start | bytes 3538952 | tf_op jit(solution)/shard_map/ppermute | solution.py:33
  49.8 25.6 %collective-permute-start.3 = (bf16[8,144,512]{2,1,0:T(8,128)(2,1)}, bf16[8,144,512]{2,1,0:T(8,128)(2,1)}, u32[]{:S(2)}, u32[]{:S(2)}) collective-permute-start(bf16[8,144,512]{2,1,0:T(8,128)(2,1)} %get-tuple-element.36), channel_id=1, source_target_pairs={{0,192},{4,196},{8,200},{12,204},{16,208},{20,212},{24,216},{28,22... | collective-permute-start | bytes 3538952 | tf_op jit(solution)/shard_map/ppermute | solution.py:33
  51.3 28.7 %collective-permute-start.4 = (bf16[8,144,512]{2,1,0:T(8,128)(2,1)}, bf16[8,144,512]{2,1,0:T(8,128)(2,1)S(1)}, u32[]{:S(2)}, u32[]{:S(2)}) collective-permute-start(bf16[8,144,512]{2,1,0:T(8,128)(2,1)} %get-tuple-element.37.refs_4_), channel_id=1, source_target_pairs={{0,1},{1,2},{2,3},{3,0},{4,5},{5,6},{6,7},{7,4},{8,9},{9,10},{10,1... | collective-permute-start | bytes 3538952 | tf_op jit(solution)/shard_map/ppermute | solution.py:39
  53.8 26.3 %collective-permute-start.5 = (bf16[8,144,512]{2,1,0:T(8,128)(2,1)}, bf16[8,144,512]{2,1,0:T(8,128)(2,1)}, u32[]{:S(2)}, u32[]{:S(2)}) collective-permute-start(bf16[8,144,512]{2,1,0:T(8,128)(2,1)} %get-tuple-element.38.refs_5_), channel_id=1, source_target_pairs={{0,3},{1,0},{2,1},{3,2},{4,7},{5,4},{6,5},{7,6},{8,11},{9,8},{10,9... | collective-permute-start | bytes 3538952 | tf_op jit(solution)/shard_map/ppermute | solution.py:39
  55.7 31.6 %copy-start.14 = (f32[512]{0:T(512)S(1)}, f32[512]{0:T(512)}, u32[]{:S(2)}) copy-start(f32[512]{0:T(512)} %param.13) | copy-start | bytes 6148
  80.9 26.2 %collective-permute-start.6 = (bf16[8,144,512]{2,1,0:T(8,128)(2,1)}, bf16[8,144,512]{2,1,0:T(8,128)(2,1)S(1)}, u32[]{:S(2)}, u32[]{:S(2)}) collective-permute-start(bf16[8,144,512]{2,1,0:T(8,128)(2,1)} %get-tuple-element.39.refs_5_), channel_id=1, source_target_pairs={{0,64},{4,68},{8,72},{12,76},{16,80},{20,84},{24,88},{28,92},{32,9... | collective-permute-start | bytes 3538952 | tf_op jit(solution)/shard_map/ppermute | solution.py:33
  81.0 26.2 %collective-permute-start.7 = (bf16[8,144,512]{2,1,0:T(8,128)(2,1)}, bf16[8,144,512]{2,1,0:T(8,128)(2,1)}, u32[]{:S(2)}, u32[]{:S(2)}) collective-permute-start(bf16[8,144,512]{2,1,0:T(8,128)(2,1)} %get-tuple-element.40.refs_10_), channel_id=1, source_target_pairs={{0,192},{4,196},{8,200},{12,204},{16,208},{20,212},{24,216},{28,22... | collective-permute-start | bytes 3538952 | tf_op jit(solution)/shard_map/ppermute | solution.py:33
  83.6 24.4 %collective-permute-start.8 = (bf16[8,144,512]{2,1,0:T(8,128)(2,1)}, bf16[8,144,512]{2,1,0:T(8,128)(2,1)}, u32[]{:S(2)}, u32[]{:S(2)}) collective-permute-start(bf16[8,144,512]{2,1,0:T(8,128)(2,1)} %get-tuple-element.41.refs_6_), channel_id=1, source_target_pairs={{0,3},{1,0},{2,1},{3,2},{4,7},{5,4},{6,5},{7,6},{8,11},{9,8},{10,9... | collective-permute-start | bytes 3538952 | tf_op jit(solution)/shard_map/ppermute | solution.py:39
  85.5 25.5 %collective-permute-start.9 = (bf16[8,144,512]{2,1,0:T(8,128)(2,1)}, bf16[8,144,512]{2,1,0:T(8,128)(2,1)}, u32[]{:S(2)}, u32[]{:S(2)}) collective-permute-start(bf16[8,144,512]{2,1,0:T(8,128)(2,1)} %get-tuple-element.42.refs_9_), channel_id=1, source_target_pairs={{0,1},{1,2},{2,3},{3,0},{4,5},{5,6},{6,7},{7,4},{8,9},{9,10},{10,1... | collective-permute-start | bytes 3538952 | tf_op jit(solution)/shard_map/ppermute | solution.py:39
  88.4 18.5 %copy-start.7 = (bf16[8,4,576]{2,1,0:T(4,128)(2,1)}, bf16[8,4,576]{2,1,0:T(4,128)(2,1)S(1)}, u32[]{:S(2)}) copy-start(bf16[8,4,576]{2,1,0:T(4,128)(2,1)S(1)} %pad_maximum_fusion.1) | copy-start | bytes 110596
  107.1 3.9 %copy-start.1 = (bf16[8,144,512]{2,1,0:T(8,128)(2,1)}, bf16[8,144,512]{2,1,0:T(8,128)(2,1)S(1)}, u32[]{:S(2)}) copy-start(bf16[8,144,512]{2,1,0:T(8,128)(2,1)S(1)} %collective-permute-done.6.refs_0_) | copy-start | bytes 3538948
  111.0 24.5 %collective-permute-start.10 = (bf16[8,144,512]{2,1,0:T(8,128)(2,1)}, bf16[8,144,512]{2,1,0:T(8,128)(2,1)S(1)}, u32[]{:S(2)}, u32[]{:S(2)}) collective-permute-start(bf16[8,144,512]{2,1,0:T(8,128)(2,1)} %get-tuple-element.47.refs_13_.refs_5_), channel_id=1, source_target_pairs={{0,1},{1,2},{2,3},{3,0},{4,5},{5,6},{6,7},{7,4},{8,9},{9,10},{10,1... | collective-permute-start | bytes 3538952 | tf_op jit(solution)/shard_map/ppermute | solution.py:39
  111.0 24.5 %collective-permute-start.11 = (bf16[8,144,512]{2,1,0:T(8,128)(2,1)}, bf16[8,144,512]{2,1,0:T(8,128)(2,1)}, u32[]{:S(2)}, u32[]{:S(2)}) collective-permute-start(bf16[8,144,512]{2,1,0:T(8,128)(2,1)} %get-tuple-element.48.refs_14_.refs_6_), channel_id=1, source_target_pairs={{0,3},{1,0},{2,1},{3,2},{4,7},{5,4},{6,5},{7,6},{8,11},{9,8},{10,9... | collective-permute-start | bytes 3538952 | tf_op jit(solution)/shard_map/ppermute | solution.py:39
  135.5 1.0 copy-start.5
  147.8 9.7 %copy-start.10 = (f32[128,128]{1,0:T(8,128)S(1)}, f32[128,128]{1,0:T(8,128)}, u32[]{:S(2)}) copy-start(f32[128,128]{1,0:T(8,128)} %get-tuple-element.57) | copy-start | bytes 196612
  150.6 9.4 %collective-permute-start.13 = (bf16[8,8,64,128]{3,2,1,0:T(8,128)(2,1)}, bf16[8,8,64,128]{3,2,1,0:T(8,128)(2,1)S(1)}, u32[]{:S(2)}, u32[]{:S(2)}) collective-permute-start(bf16[8,8,64,128]{3,2,1,0:T(8,128)(2,1)} %fusion.30), channel_id=1, source_target_pairs={{0,4},{4,0},{8,12},{12,8},{16,20},{20,16},{24,28},{28,24},{32,36},... | collective-permute-start | bytes 3145736 | tf_op jit(solution)/shard_map/ppermute | solution.py:43
  157.5 2.2 %collective-permute-start.12 = (f32[8,8,64]{2,1,0:T(8,128)S(1)}, f32[8,8,64]{2,1,0:T(8,128)S(1)}, u32[]{:S(2)}, u32[]{:S(2)}) collective-permute-start(f32[8,8,64]{2,1,0:T(8,128)S(1)} %dynamic-slice_bitcast_fusion), channel_id=1, source_target_pairs={{0,4},{4,0},{8,12},{12,8},{16,20},{20,16},{24,28},{28,24},{32,36},... | collective-permute-start | bytes 49160 | tf_op jit(solution)/shard_map/ppermute | solution.py:43
  163.6 41.5 %all-to-all-start = ((bf16[8,528,128]{2,1,0:T(8,128)(2,1)}), bf16[8,528,128]{2,1,0:T(8,128)(2,1)S(1)}, u32[]{:S(2)}, u32[]{:S(2)}) async-start(bf16[8,528,128]{2,1,0:T(8,128)(2,1)} %fusion.29), calls=%async_computation | async-start | bytes 2162688 | tf_op jit(solution)/shard_map/all_to_all | solution.py:506
  175.1 30.0 %copy-start.11 = (f32[8,64]{1,0:T(8,128)S(1)}, f32[8,64]{1,0:T(8,128)}, u32[]{:S(2)}) copy-start(f32[8,64]{1,0:T(8,128)} %log_add_fusion.1.refs_15_) | copy-start | bytes 6148
  (2 other events, 2.1 us)
Sparse Core Ops, SparseCore 0:
  15.5 48.1 all-reduce.4
Sparse Core Ops, SparseCore 1:
  19.5 69.9 all-gather.1

commit v3 on v2

--- a/solution.py
+++ b/solution.py
@@ -81,26 +81,49 @@
     )(*arrays)
 
 
-def pack_kernel(par_ref, len_in, cache, out_a, out_b, len_out, held, sem):
-    copy = pltpu.make_async_copy(cache.at[pl.ds(par_ref[0] * 32, 32)], held, sem)
-    copy.start()
+def pack_kernel(par_ref, len_in, cache, out_a, out_b, len_out, held, packed, in_sems, out_sems):
+    count = 4
+    blocks, pairs = 32 // count, 2 * PAIRS // count
+    first = par_ref[0] * 32
+    copies = [
+        pltpu.make_async_copy(
+            cache.at[pl.ds(first + n * blocks, blocks)],
+            held.at[pl.ds(n * blocks, blocks)],
+            in_sems.at[n],
+        )
+        for n in range(count)
+    ]
+    for copy in copies:
+        copy.start()
     for row in range(len_in.shape[0]):
         len_out[row] = len_in[row]
-    copy.wait()
-    for quarter, out in enumerate((out_a, out_b)):
+    sends = []
+    for n in range(count):
+        copies[n].wait()
 
         def one(pair, carry):
             ropes = []
             for b in range(2):
-                block = held[quarter * 2 * PAIRS + 2 * pair + b]
-                out[pair, 64 * b : 64 * b + 64, :] = block[:, :LAT]
+                block = held[2 * pair + b]
+                packed[pair, 64 * b : 64 * b + 64, :] = block[:, :LAT]
                 rope = block[:, LAT:]
                 rope = jnp.concatenate([rope[:32], rope[32:]], 1)
                 ropes += [rope[:16], rope[16:]]
-            out[pair, 128:, :] = jnp.concatenate(ropes, 1)
+            packed[pair, 128:, :] = jnp.concatenate(ropes, 1)
             return carry
 
-        lax.fori_loop(0, PAIRS, one, 0)
+        lax.fori_loop(n * pairs, (n + 1) * pairs, one, 0)
+        out = out_a if n < count // 2 else out_b
+        sends.append(
+            pltpu.make_async_copy(
+                packed.at[pl.ds(n * pairs, pairs)],
+                out.at[pl.ds(n * pairs % PAIRS, pairs)],
+                out_sems.at[n],
+            )
+        )
+        sends[-1].start()
+    for send in sends:
+        send.wait()
 
 
 def pack(latent_cache, parity, lengths):
@@ -111,12 +134,14 @@
         grid_spec=pltpu.PrefetchScalarGridSpec(
             num_scalar_prefetch=2,
             grid=(),
-            in_specs=[pl.BlockSpec(memory_space=pl.ANY)],
-            out_specs=[pl.BlockSpec(memory_space=pltpu.VMEM)] * 2
+            in_specs=[pl.BlockSpec(memory_space=pltpu.HBM)],
+            out_specs=[pl.BlockSpec(memory_space=pltpu.HBM)] * 2
             + [pl.BlockSpec(memory_space=pltpu.SMEM)],
             scratch_shapes=[
                 pltpu.VMEM((32,) + latent_cache.shape[1:], latent_cache.dtype),
-                pltpu.SemaphoreType.DMA,
+                pltpu.VMEM((2 * PAIRS,) + shape.shape[1:], latent_cache.dtype),
+                pltpu.SemaphoreType.DMA((4,)),
+                pltpu.SemaphoreType.DMA((4,)),
             ],
         ),
         compiler_params=pltpu.CompilerParams(vmem_limit_bytes=VMEM_BYTES),
@@ -124,14 +149,14 @@
 
 
 def attend_kernel(owners, pieces, unused, stage, *refs):
-    blk_ref, live_ref, par_ref, q_in, w_ref = refs[:5]
+    blk_ref, live_ref, par_ref, q_in, w_in = refs[:5]
     refs = refs[5:]
     kv_in = refs[: len(pieces)]
     refs = refs[len(pieces) + unused :]
     if stage != "first":
         state_in, lse_in = refs[:2]
         refs = refs[2:]
-    state, lse_ref, kv, queries, normal, slot_lse, projected, items, kv_sems, q_sems, row_sems = refs
+    state, lse_ref, kv, queries, normal, slot_lse, projected, w_ref, items, kv_sems, q_sems, row_sems = refs
     rows = lse_ref.shape[0]
 
     copies = [[] for _ in range(owners)]
@@ -149,9 +174,11 @@
     for some in copies:
         for copy in some:
             copy.start()
+    extra = [pltpu.make_async_copy(w_in, w_ref, kv_sems.at[len(pieces)])]
+    if stage != "first":
+        extra.append(pltpu.make_async_copy(lse_in, lse_ref, kv_sems.at[len(pieces) + 1]))
     if stage == "middle":
-        whole = pltpu.make_async_copy(state_in, state, row_sems.at[0])
-        whole.start()
+        extra.append(pltpu.make_async_copy(state_in, state, kv_sems.at[len(pieces) + 2]))
 
     def scan(i, n):
         items[n] = i
@@ -185,8 +212,6 @@
     if stage == "first":
         state[...] = jnp.zeros_like(state)
         lse_ref[...] = jnp.full_like(lse_ref, masked_score)
-    else:
-        lse_ref[...] = lse_in[...]
 
     low_lanes = lax.broadcasted_iota(jnp.int32, (16, 128), 1) < 64
 
@@ -247,6 +272,9 @@
         begin, end = ends[o], ends[o + 1]
         for copy in copies[o]:
             copy.wait()
+        if o == 0:
+            for copy in extra:
+                copy.start()
 
         def several(j, carry):
             first = begin + AT_ONCE * j
@@ -267,6 +295,9 @@
             return carry
 
         lax.fori_loop(0, (end - begin + AT_ONCE - 1) // AT_ONCE, several, 0)
+
+    for copy in extra:
+        copy.wait()
 
     def project(group, carry):
         some = pl.ds(pl.multiple_of(group * 32, 32), 32)
@@ -280,8 +311,6 @@
         return carry
 
     lax.fori_loop(0, (found + 31) // 32, project, 0)
-    if stage == "middle":
-        whole.wait()
     if stage == "last":
         each(lambda slot: load_row(slot).start())
         each(lambda slot: load_row(slot).wait())
@@ -328,11 +357,11 @@
     all_blocks = (owners * 64,) if stage == "first" else (owners * 4 * PAIRS,)
     whole = pl.BlockSpec(memory_space=pltpu.VMEM)
     anywhere = pl.BlockSpec(memory_space=pltpu.HBM)
-    in_specs = [anywhere, whole] + [anywhere] * len(arrays)
+    in_specs = [anywhere, anywhere] + [anywhere] * len(arrays)
     in_specs += [anywhere] * len(after)
     operands = [queries, w_uv, *arrays, *after, *earlier]
     if earlier:
-        in_specs += [anywhere, whole]
+        in_specs += [anywhere, anywhere]
     return pl.pallas_call(
         functools.partial(attend_kernel, owners, pieces, len(after), stage),
         out_shape=[
@@ -350,8 +379,9 @@
                 pltpu.VMEM((slots, 64, LAT), jnp.float32),
                 pltpu.VMEM((slots, 64, 128), jnp.float32),
                 pltpu.VMEM((slots, 64, 128), jnp.float32),
+                pltpu.VMEM(w_uv.shape, w_uv.dtype),
                 pltpu.SMEM((owners * rows,), jnp.int32),
-                pltpu.SemaphoreType.DMA((len(arrays),)),
+                pltpu.SemaphoreType.DMA((len(arrays) + 3,)),
                 pltpu.SemaphoreType.DMA((slots,)),
                 pltpu.SemaphoreType.DMA((slots,)),
             ],

time: 218 us -> 215 us (0.986)
  Pallas kernels: 46.5 us -> 41.6 us
  waiting for transfers between devices: 84.7 us -> 89 us
  starting transfers between devices: 36.4 us -> 32.9 us
    pallas_call x3, Pallas kernels: 41.4 us -> 37.1 us  [attend(): pl.pallas_call(functools.partial(attend_kernel, owners, pieces, len(after...]
    ppermute x6, waiting for transfers between devices: 9.09 us -> 13.2 us  [along_x(): lax.ppermute(array, 'tensor', [(i, (i + by) % NX) for i in range(NX)])]
  transfers between devices with their start and end apart: 17 -> 17, of which waited for: 14 -> 14; matrix products, arithmetic and copies ran while one was open for 9% -> 9% of each run, Pallas kernels for 14% -> 12%
where the time goes in v3:
time: 215 us; the launch traced here: 213 us
  waiting for transfers between devices  89 us (41%)
  Pallas kernels  41.6 us (19%)
  starting transfers between devices  32.9 us (15%)
  between operations  16.6 us (8%)
  other arithmetic  15 us (7%)
  local copies, waits for them, and re-layouts  12.4 us (6%)
  matrix products  5.23 us (2%)
    pallas_call x3, Pallas kernels, attend(): pl.pallas_call(functools.partial(attend_kernel, owners, pieces, len(after...  37.1 us
    ppermute x6, waiting for transfers between devices, along_y(): lax.ppermute(array, 'cache', [(place(y, z, c), place(y + by, z, c)) for y...  37.1 us
    all_to_all x1, waiting for transfers between devices, body(): lax.all_to_all(jnp.concatenate([chip_part, stats], 1), 'cache', split_axi...  28.3 us
    ppermute x6, waiting for transfers between devices, along_x(): lax.ppermute(array, 'tensor', [(i, (i + by) % NX) for i in range(NX)])  13.2 us
    ppermute x6, starting transfers between devices, along_y(): lax.ppermute(array, 'cache', [(place(y, z, c), place(y + by, z, c)) for y...  9.49 us
    all_to_all x1, starting transfers between devices, body(): lax.all_to_all(jnp.concatenate([chip_part, stats], 1), 'cache', split_axi...  9.48 us
    ppermute x6, starting transfers between devices, along_x(): lax.ppermute(array, 'tensor', [(i, (i + by) % NX) for i in range(NX)])  8.35 us
    psum x1, waiting for transfers between devices, body(): summed = lax.psum(partial_sum, 'tensor')  7.92 us
  transfers between devices with their start and end apart: 17, of which 14 were waited for; matrix products, arithmetic and copies ran while one was open for 9% of the time, Pallas kernels for 12%

profile of v3, /device:TPU:1, one launch (start us, length us, event | category | flops | bytes accessed | tf_op | source)
XLA Modules:
  0.0 212.7 jit_solution(3126067034264778808)
XLA Ops:
  8.1 4.5 %shard_map.122 = (bf16[8,144,512]{2,1,0:T(8,128)(2,1)}, bf16[8,144,512]{2,1,0:T(8,128)(2,1)}, s32[8]{0:T(128)}) custom-call(s32[1]{0:T(128)} %bitcast.1.par_ref.refs_2_, s32[8]{0:T(128)} %len_in.1, bf16[64,64,576]{2,1,0:T(8,128)(2,1)} %refs_5_.1), custom_call_target="tpu_custom_call" | custom-call | tf_op jit(solution)/shard_map/pallas_call | solution.py:131
  13.3 1.4 fusion.5
  15.6 1.5 maximum_bitcast_fusion
  18.8 2.2 %collective-permute-start = (bf16[8,144,512]{2,1,0:T(8,128)(2,1)}, bf16[8,144,512]{2,1,0:T(8,128)(2,1)S(1)}, u32[]{:S(2)}, u32[]{:S(2)}) collective-permute-start(bf16[8,144,512]{2,1,0:T(8,128)(2,1)} %get-tuple-element.33.refs_0_), channel_id=1, source_target_pairs={{0,64},{4,68},{8,72},{12,76},{16,80},{20,84},{24,88},{28,92},{32,9... | collective-permute-start | bytes 3538952 | tf_op jit(solution)/shard_map/ppermute | solution.py:33
  21.0 1.5 collective-permute-start.1
  22.5 23.9 %collective-permute-done.refs_2_ = bf16[8,144,512]{2,1,0:T(8,128)(2,1)S(1)} collective-permute-done((bf16[8,144,512]{2,1,0:T(8,128)(2,1)}, bf16[8,144,512]{2,1,0:T(8,128)(2,1)S(1)}, u32[]{:S(2)}, u32[]{:S(2)}) %collective-permute-start) | collective-permute-done | bytes 1179680 | tf_op jit(solution)/shard_map/ppermute | solution.py:33
  46.4 1.2 collective-permute-done.1.refs_3_
  47.6 1.6 collective-permute-start.2
  49.1 1.5 collective-permute-start.3
  50.6 2.5 %collective-permute-start.4 = (bf16[8,144,512]{2,1,0:T(8,128)(2,1)}, bf16[8,144,512]{2,1,0:T(8,128)(2,1)S(1)}, u32[]{:S(2)}, u32[]{:S(2)}) collective-permute-start(bf16[8,144,512]{2,1,0:T(8,128)(2,1)} %get-tuple-element.37.refs_4_), channel_id=1, source_target_pairs={{0,1},{1,2},{2,3},{3,0},{4,5},{5,6},{6,7},{7,4},{8,9},{9,10},{10,1... | collective-permute-start | bytes 3538952 | tf_op jit(solution)/shard_map/ppermute | solution.py:39
  53.1 1.3 collective-permute-start.5
  55.1 7.9 %all-reduce.5.cloned.1.call-done.refs_6_ = f32[8,4,576]{2,1,0:T(4,128)} async-done(((f32[8,4,576]{2,1,0:T(4,128)}), f32[8,4,576]{2,1,0:T(4,128)}) %all-reduce.5.cloned.1.call-update) | async-done | bytes 73744 | tf_op jit(solution)/shard_map/psum | solution.py:453
  63.1 11.2 %collective-permute-done.2.refs_0_ = bf16[8,144,512]{2,1,0:T(8,128)(2,1)} collective-permute-done((bf16[8,144,512]{2,1,0:T(8,128)(2,1)}, bf16[8,144,512]{2,1,0:T(8,128)(2,1)}, u32[]{:S(2)}, u32[]{:S(2)}) %collective-permute-start.2) | collective-permute-done | bytes 1179680 | tf_op jit(solution)/shard_map/ppermute | solution.py:33
  74.8 4.5 %collective-permute-done.4.refs_2_ = bf16[8,144,512]{2,1,0:T(8,128)(2,1)S(1)} collective-permute-done((bf16[8,144,512]{2,1,0:T(8,128)(2,1)}, bf16[8,144,512]{2,1,0:T(8,128)(2,1)S(1)}, u32[]{:S(2)}, u32[]{:S(2)}) %collective-permute-start.4) | collective-permute-done | bytes 1179680 | tf_op jit(solution)/shard_map/ppermute | solution.py:39
  80.3 2.7 %collective-permute-start.7 = (bf16[8,144,512]{2,1,0:T(8,128)(2,1)}, bf16[8,144,512]{2,1,0:T(8,128)(2,1)}, u32[]{:S(2)}, u32[]{:S(2)}) collective-permute-start(bf16[8,144,512]{2,1,0:T(8,128)(2,1)} %get-tuple-element.40.refs_10_), channel_id=1, source_target_pairs={{0,192},{4,196},{8,200},{12,204},{16,208},{20,212},{24,216},{28,22... | collective-permute-start | bytes 3538952 | tf_op jit(solution)/shard_map/ppermute | solution.py:33
  83.0 1.9 collective-permute-start.8
  87.8 1.4 fusion.65
  91.0 1.3 compare_convert_fusion.2
  93.1 1.9 select_reduce_fusion
  95.0 11.1 %shard_map.125 = (f32[128,64,128]{2,1,0:T(8,128)}, f32[128,128]{1,0:T(8,128)}) custom-call(s32[1024]{0:T(1024)} %reshape.434.refs_0_, s32[128]{0:T(128)} %get-tuple-element.66.refs_1_, s32[1]{0:T(128)} %bitcast.1.par_ref.refs_2_, bf16[128,64,640]{2,1,0:T(8,128)(2,1)} %all-gather.2.cloned.1.call-done.refs_3_, bf16[16,512,128]{2,1,0:T(8,128)(2,1)} %refs_4_.5, ...), custom_call_target="tpu_custom_call" | custom-call | flops 2281701376 | bytes 22020096 | tf_op jit(solution)/shard_map/pallas_call | solution.py:365
  107.4 3.0 %collective-permute-done.9.refs_3_ = bf16[8,144,512]{2,1,0:T(8,128)(2,1)} collective-permute-done((bf16[8,144,512]{2,1,0:T(8,128)(2,1)}, bf16[8,144,512]{2,1,0:T(8,128)(2,1)}, u32[]{:S(2)}, u32[]{:S(2)}) %collective-permute-start.9) | collective-permute-done | bytes 1179680 | tf_op jit(solution)/shard_map/ppermute | solution.py:39
  110.4 2.7 %collective-permute-start.11 = (bf16[8,144,512]{2,1,0:T(8,128)(2,1)}, bf16[8,144,512]{2,1,0:T(8,128)(2,1)}, u32[]{:S(2)}, u32[]{:S(2)}) collective-permute-start(bf16[8,144,512]{2,1,0:T(8,128)(2,1)} %get-tuple-element.48.refs_14_.refs_6_), channel_id=1, source_target_pairs={{0,3},{1,0},{2,1},{3,2},{4,7},{5,4},{6,5},{7,6},{8,11},{9,8},{10,9... | collective-permute-start | bytes 3538952 | tf_op jit(solution)/shard_map/ppermute | solution.py:39
  115.5 14.7 %shard_map.127 = (f32[128,64,128]{2,1,0:T(8,128)}, f32[128,128]{1,0:T(8,128)}) custom-call(s32[2048]{0:T(1024)} %reshape.435.refs_0_, s32[256]{0:T(256)} %bitcast.143, s32[1]{0:T(128)} %bitcast.1.par_ref.refs_2_, bf16[128,64,640]{2,1,0:T(8,128)(2,1)} %all-gather.2.cloned.1.call-done.refs_3_, bf16[16,512,128]{2,1,0:T(8,128)(2,1)} %refs_4_.5, ...), custom_call_target="tpu_custom_call" | custom-call | flops 4563402752 | bytes 27262976 | tf_op jit(solution)/shard_map/pallas_call | solution.py:365
  130.2 4.6 %collective-permute-done.10.refs_7_ = bf16[8,144,512]{2,1,0:T(8,128)(2,1)S(1)} collective-permute-done((bf16[8,144,512]{2,1,0:T(8,128)(2,1)}, bf16[8,144,512]{2,1,0:T(8,128)(2,1)S(1)}, u32[]{:S(2)}, u32[]{:S(2)}) %collective-permute-start.10) | collective-permute-done | bytes 1179680 | tf_op jit(solution)/shard_map/ppermute | solution.py:39
  135.9 11.3 %shard_map.128 = (f32[128,64,128]{2,1,0:T(8,128)}, f32[128,128]{1,0:T(8,128)}) custom-call(s32[1024]{0:T(1024)} %reshape.433.refs_0_, s32[128]{0:T(128)} %get-tuple-element.67.refs_1_, s32[1]{0:T(128)} %bitcast.1.par_ref.refs_2_, bf16[128,64,640]{2,1,0:T(8,128)(2,1)} %all-gather.2.cloned.1.call-done.refs_3_, ...), custom_call_target="tpu_custom_call", output_to_operand_aliasing={{0}: (9, {})} | custom-call | flops 2281701376 | bytes 22020096 | tf_op jit(solution)/shard_map/pallas_call | solution.py:365
  147.2 2.8 %fusion.30 = bf16[8,8,64,128]{3,2,1,0:T(8,128)(2,1)} fusion(f32[8,2,8,64,128]{4,3,2,1,0:T(8,128)} %bitcast.128, s32[]{:T(128)S(6)} %select_n.84), kind=kLoop, calls=%fused_computation.22 | loop fusion | bytes 2097156 | tf_op jit(solution)/shard_map/convert_element_type | solution.py:520
  150.0 5.4 %collective-permute-start.13 = (bf16[8,8,64,128]{3,2,1,0:T(8,128)(2,1)}, bf16[8,8,64,128]{3,2,1,0:T(8,128)(2,1)S(1)}, u32[]{:S(2)}, u32[]{:S(2)}) collective-permute-start(bf16[8,8,64,128]{3,2,1,0:T(8,128)(2,1)} %fusion.30), channel_id=1, source_target_pairs={{0,4},{4,0},{8,12},{12,8},{16,20},{20,16},{24,28},{28,24},{32,36},... | collective-permute-start | bytes 3145736 | tf_op jit(solution)/shard_map/ppermute | solution.py:43
  155.5 2.1 collective-permute-done.12
  157.9 2.5 %fusion.4 = bf16[8,8,64,128]{3,2,1,0:T(8,128)(2,1)S(1)} fusion(bf16[8,8,64,128]{3,2,1,0:T(8,128)(2,1)S(1)} %collective-permute-done.13, f32[8,2,8,64,128]{4,3,2,1,0:T(8,128)} %bitcast.129, s32[]{:T(128)S(6)} %select_n.83, f32[8,8,64]{2,1,0:T(8,128)S(1)} %get-tuple-element.83, f32[8,8,64]{2,1,0:T(8,128)S(1)} %get-tuple-element.82), kind=kLoop, calls=%fused_computation.6 | loop fusion | flops 2621440 | bytes 4227076 | tf_op jit(solution)/shard_map/convert_element_type | solution.py:534
  161.5 9.5 %all-to-all-start = ((bf16[8,528,128]{2,1,0:T(8,128)(2,1)}), bf16[8,528,128]{2,1,0:T(8,128)(2,1)S(1)}, u32[]{:S(2)}, u32[]{:S(2)}) async-start(bf16[8,528,128]{2,1,0:T(8,128)(2,1)} %fusion.29), calls=%async_computation | async-start | bytes 2162688 | tf_op jit(solution)/shard_map/all_to_all | solution.py:536
  172.6 28.3 %all-to-all-done = bf16[8,528,128]{2,1,0:T(8,128)(2,1)S(1)} async-done(((bf16[8,528,128]{2,1,0:T(8,128)(2,1)}), bf16[8,528,128]{2,1,0:T(8,128)(2,1)S(1)}, u32[]{:S(2)}, u32[]{:S(2)}) %all-to-all-start) | async-done | bytes 1081376 | tf_op jit(solution)/shard_map/all_to_all | solution.py:536
  202.4 2.1 fusion.25
  (119 shorter events, 20.2 us)
Async XLA Ops:
  8.0 5.3 %copy-start = (bf16[1792,576]{0,1:T(8,128)(2,1)S(1)}, bf16[1792,576]{0,1:T(8,128)(2,1)}, u32[]{:S(2)}) copy-start(bf16[1792,576]{0,1:T(8,128)(2,1)} %param.12) | copy-start | bytes 6193156
  8.0 55.0 %all-reduce.5.cloned.1.call-start = ((), (), s32[]{:S(2)}) async-start(), calls=%async_computation.2 | async-start | bytes 163840 | tf_op jit(solution)/shard_map/psum | solution.py:453
  8.1 5.3 %copy-start.8 = (bf16[8,4,1792]{2,1,0:T(4,128)(2,1)S(1)}, bf16[8,4,1792]{2,1,0:T(4,128)(2,1)}, u32[]{:S(2)}) copy-start(bf16[8,4,1792]{2,1,0:T(4,128)(2,1)} %param.11) | copy-start | bytes 344068
  12.6 2.2 %copy-start.15 = (s32[8]{0:T(128)S(1)}, s32[8]{0:T(128)}, u32[]{:S(2)}) copy-start(s32[8]{0:T(128)} %get-tuple-element.30) | copy-start | bytes 100
  12.6 2.5 %copy-start.9 = (bf16[8,4,1024]{2,1,0:T(4,128)(2,1)S(1)}, bf16[8,4,1024]{2,1,0:T(4,128)(2,1)}, u32[]{:S(2)}) copy-start(bf16[8,4,1024]{2,1,0:T(4,128)(2,1)} %param.15) | copy-start | bytes 196612
  14.7 75.1 %all-gather.2.cloned.1.call-start = ((), (), s32[]{:S(2)}) async-start(), calls=%async_computation.1 | async-start | bytes 11141120 | tf_op jit(solution)/shard_map/all_gather | solution.py:443
  15.6 2.0 copy-start.12
  15.6 2.1 copy-start.13
  17.4 1.4 copy-start.4
  18.8 27.6 %collective-permute-start = (bf16[8,144,512]{2,1,0:T(8,128)(2,1)}, bf16[8,144,512]{2,1,0:T(8,128)(2,1)S(1)}, u32[]{:S(2)}, u32[]{:S(2)}) collective-permute-start(bf16[8,144,512]{2,1,0:T(8,128)(2,1)} %get-tuple-element.33.refs_0_), channel_id=1, source_target_pairs={{0,64},{4,68},{8,72},{12,76},{16,80},{20,84},{24,88},{28,92},{32,9... | collective-permute-start | bytes 3538952 | tf_op jit(solution)/shard_map/ppermute | solution.py:33
  21.0 33.4 %copy-start.16 = (s32[4]{0:T(128)S(1)}, s32[4]{0:T(128)}, u32[]{:S(2)}) copy-start(s32[4]{0:T(128)} %constant.147.clone) | copy-start | bytes 52
  21.0 26.6 %collective-permute-start.1 = (bf16[8,144,512]{2,1,0:T(8,128)(2,1)}, bf16[8,144,512]{2,1,0:T(8,128)(2,1)}, u32[]{:S(2)}, u32[]{:S(2)}) collective-permute-start(bf16[8,144,512]{2,1,0:T(8,128)(2,1)} %get-tuple-element.34.refs_1_), channel_id=1, source_target_pairs={{0,192},{4,196},{8,200},{12,204},{16,208},{20,212},{24,216},{28,22... | collective-permute-start | bytes 3538952 | tf_op jit(solution)/shard_map/ppermute | solution.py:33
  46.4 1.2 copy-start.3
  47.6 26.7 %collective-permute-start.2 = (bf16[8,144,512]{2,1,0:T(8,128)(2,1)}, bf16[8,144,512]{2,1,0:T(8,128)(2,1)}, u32[]{:S(2)}, u32[]{:S(2)}) collective-permute-start(bf16[8,144,512]{2,1,0:T(8,128)(2,1)} %get-tuple-element.35), channel_id=1, source_target_pairs={{0,64},{4,68},{8,72},{12,76},{16,80},{20,84},{24,88},{28,92},{32,9... | collective-permute-start | bytes 3538952 | tf_op jit(solution)/shard_map/ppermute | solution.py:33
  49.1 25.6 %collective-permute-start.3 = (bf16[8,144,512]{2,1,0:T(8,128)(2,1)}, bf16[8,144,512]{2,1,0:T(8,128)(2,1)}, u32[]{:S(2)}, u32[]{:S(2)}) collective-permute-start(bf16[8,144,512]{2,1,0:T(8,128)(2,1)} %get-tuple-element.36), channel_id=1, source_target_pairs={{0,192},{4,196},{8,200},{12,204},{16,208},{20,212},{24,216},{28,22... | collective-permute-start | bytes 3538952 | tf_op jit(solution)/shard_map/ppermute | solution.py:33
  50.6 28.7 %collective-permute-start.4 = (bf16[8,144,512]{2,1,0:T(8,128)(2,1)}, bf16[8,144,512]{2,1,0:T(8,128)(2,1)S(1)}, u32[]{:S(2)}, u32[]{:S(2)}) collective-permute-start(bf16[8,144,512]{2,1,0:T(8,128)(2,1)} %get-tuple-element.37.refs_4_), channel_id=1, source_target_pairs={{0,1},{1,2},{2,3},{3,0},{4,5},{5,6},{6,7},{7,4},{8,9},{9,10},{10,1... | collective-permute-start | bytes 3538952 | tf_op jit(solution)/shard_map/ppermute | solution.py:39
  53.1 26.3 %collective-permute-start.5 = (bf16[8,144,512]{2,1,0:T(8,128)(2,1)}, bf16[8,144,512]{2,1,0:T(8,128)(2,1)}, u32[]{:S(2)}, u32[]{:S(2)}) collective-permute-start(bf16[8,144,512]{2,1,0:T(8,128)(2,1)} %get-tuple-element.38.refs_5_), channel_id=1, source_target_pairs={{0,3},{1,0},{2,1},{3,2},{4,7},{5,4},{6,5},{7,6},{8,11},{9,8},{10,9... | collective-permute-start | bytes 3538952 | tf_op jit(solution)/shard_map/ppermute | solution.py:39
  55.1 31.6 %copy-start.14 = (f32[512]{0:T(512)S(1)}, f32[512]{0:T(512)}, u32[]{:S(2)}) copy-start(f32[512]{0:T(512)} %param.13) | copy-start | bytes 6148
  80.3 26.2 %collective-permute-start.6 = (bf16[8,144,512]{2,1,0:T(8,128)(2,1)}, bf16[8,144,512]{2,1,0:T(8,128)(2,1)S(1)}, u32[]{:S(2)}, u32[]{:S(2)}) collective-permute-start(bf16[8,144,512]{2,1,0:T(8,128)(2,1)} %get-tuple-element.39.refs_5_), channel_id=1, source_target_pairs={{0,64},{4,68},{8,72},{12,76},{16,80},{20,84},{24,88},{28,92},{32,9... | collective-permute-start | bytes 3538952 | tf_op jit(solution)/shard_map/ppermute | solution.py:33
  80.3 26.2 %collective-permute-start.7 = (bf16[8,144,512]{2,1,0:T(8,128)(2,1)}, bf16[8,144,512]{2,1,0:T(8,128)(2,1)}, u32[]{:S(2)}, u32[]{:S(2)}) collective-permute-start(bf16[8,144,512]{2,1,0:T(8,128)(2,1)} %get-tuple-element.40.refs_10_), channel_id=1, source_target_pairs={{0,192},{4,196},{8,200},{12,204},{16,208},{20,212},{24,216},{28,22... | collective-permute-start | bytes 3538952 | tf_op jit(solution)/shard_map/ppermute | solution.py:33
  83.0 24.4 %collective-permute-start.8 = (bf16[8,144,512]{2,1,0:T(8,128)(2,1)}, bf16[8,144,512]{2,1,0:T(8,128)(2,1)}, u32[]{:S(2)}, u32[]{:S(2)}) collective-permute-start(bf16[8,144,512]{2,1,0:T(8,128)(2,1)} %get-tuple-element.41.refs_6_), channel_id=1, source_target_pairs={{0,3},{1,0},{2,1},{3,2},{4,7},{5,4},{6,5},{7,6},{8,11},{9,8},{10,9... | collective-permute-start | bytes 3538952 | tf_op jit(solution)/shard_map/ppermute | solution.py:39
  84.9 25.5 %collective-permute-start.9 = (bf16[8,144,512]{2,1,0:T(8,128)(2,1)}, bf16[8,144,512]{2,1,0:T(8,128)(2,1)}, u32[]{:S(2)}, u32[]{:S(2)}) collective-permute-start(bf16[8,144,512]{2,1,0:T(8,128)(2,1)} %get-tuple-element.42.refs_9_), channel_id=1, source_target_pairs={{0,1},{1,2},{2,3},{3,0},{4,5},{5,6},{6,7},{7,4},{8,9},{9,10},{10,1... | collective-permute-start | bytes 3538952 | tf_op jit(solution)/shard_map/ppermute | solution.py:39
  87.8 18.3 %copy-start.7 = (bf16[8,4,576]{2,1,0:T(4,128)(2,1)}, bf16[8,4,576]{2,1,0:T(4,128)(2,1)S(1)}, u32[]{:S(2)}) copy-start(bf16[8,4,576]{2,1,0:T(4,128)(2,1)S(1)} %pad_maximum_fusion.1) | copy-start | bytes 110596
  106.5 3.9 %copy-start.1 = (bf16[8,144,512]{2,1,0:T(8,128)(2,1)}, bf16[8,144,512]{2,1,0:T(8,128)(2,1)S(1)}, u32[]{:S(2)}) copy-start(bf16[8,144,512]{2,1,0:T(8,128)(2,1)S(1)} %collective-permute-done.6.refs_0_) | copy-start | bytes 3538948
  110.4 24.5 %collective-permute-start.10 = (bf16[8,144,512]{2,1,0:T(8,128)(2,1)}, bf16[8,144,512]{2,1,0:T(8,128)(2,1)S(1)}, u32[]{:S(2)}, u32[]{:S(2)}) collective-permute-start(bf16[8,144,512]{2,1,0:T(8,128)(2,1)} %get-tuple-element.47.refs_13_.refs_5_), channel_id=1, source_target_pairs={{0,1},{1,2},{2,3},{3,0},{4,5},{5,6},{6,7},{7,4},{8,9},{9,10},{10,1... | collective-permute-start | bytes 3538952 | tf_op jit(solution)/shard_map/ppermute | solution.py:39
  110.4 24.5 %collective-permute-start.11 = (bf16[8,144,512]{2,1,0:T(8,128)(2,1)}, bf16[8,144,512]{2,1,0:T(8,128)(2,1)}, u32[]{:S(2)}, u32[]{:S(2)}) collective-permute-start(bf16[8,144,512]{2,1,0:T(8,128)(2,1)} %get-tuple-element.48.refs_14_.refs_6_), channel_id=1, source_target_pairs={{0,3},{1,0},{2,1},{3,2},{4,7},{5,4},{6,5},{7,6},{8,11},{9,8},{10,9... | collective-permute-start | bytes 3538952 | tf_op jit(solution)/shard_map/ppermute | solution.py:39
  134.9 1.0 copy-start.5
  147.2 8.2 %copy-start.10 = (f32[128,128]{1,0:T(8,128)S(1)}, f32[128,128]{1,0:T(8,128)}, u32[]{:S(2)}) copy-start(f32[128,128]{1,0:T(8,128)} %get-tuple-element.57) | copy-start | bytes 196612
  150.0 7.9 %collective-permute-start.13 = (bf16[8,8,64,128]{3,2,1,0:T(8,128)(2,1)}, bf16[8,8,64,128]{3,2,1,0:T(8,128)(2,1)S(1)}, u32[]{:S(2)}, u32[]{:S(2)}) collective-permute-start(bf16[8,8,64,128]{3,2,1,0:T(8,128)(2,1)} %fusion.30), channel_id=1, source_target_pairs={{0,4},{4,0},{8,12},{12,8},{16,20},{20,16},{24,28},{28,24},{32,36},... | collective-permute-start | bytes 3145736 | tf_op jit(solution)/shard_map/ppermute | solution.py:43
  155.4 2.2 %collective-permute-start.12 = (f32[8,8,64]{2,1,0:T(8,128)S(1)}, f32[8,8,64]{2,1,0:T(8,128)S(1)}, u32[]{:S(2)}, u32[]{:S(2)}) collective-permute-start(f32[8,8,64]{2,1,0:T(8,128)S(1)} %dynamic-slice_bitcast_fusion), channel_id=1, source_target_pairs={{0,4},{4,0},{8,12},{12,8},{16,20},{20,16},{24,28},{28,24},{32,36},... | collective-permute-start | bytes 49160 | tf_op jit(solution)/shard_map/ppermute | solution.py:43
  161.5 39.4 %all-to-all-start = ((bf16[8,528,128]{2,1,0:T(8,128)(2,1)}), bf16[8,528,128]{2,1,0:T(8,128)(2,1)S(1)}, u32[]{:S(2)}, u32[]{:S(2)}) async-start(bf16[8,528,128]{2,1,0:T(8,128)(2,1)} %fusion.29), calls=%async_computation | async-start | bytes 2162688 | tf_op jit(solution)/shard_map/all_to_all | solution.py:536
  171.0 30.0 %copy-start.11 = (f32[8,64]{1,0:T(8,128)S(1)}, f32[8,64]{1,0:T(8,128)}, u32[]{:S(2)}) copy-start(f32[8,64]{1,0:T(8,128)} %log_add_fusion.1.refs_15_) | copy-start | bytes 6148
  (2 other events, 2.1 us)
Sparse Core Ops, SparseCore 0:
  14.8 48.1 all-reduce.4
Sparse Core Ops, SparseCore 1:
  18.9 69.9 all-gather.1

commit v4 on v3

--- a/solution.py
+++ b/solution.py
@@ -148,7 +148,7 @@
     )(parity, lengths, latent_cache)
 
 
-def attend_kernel(owners, pieces, unused, stage, *refs):
+def attend_kernel(base, owners, pieces, unused, stage, *refs):
     blk_ref, live_ref, par_ref, q_in, w_in = refs[:5]
     refs = refs[5:]
     kv_in = refs[: len(pieces)]
@@ -171,9 +171,8 @@
                 kv_in[n], kv.at[pl.ds(first, kv_in[n].shape[0])], kv_sems.at[n]
             )
         )
-    for some in copies:
-        for copy in some:
-            copy.start()
+    for copy in copies[0]:
+        copy.start()
     extra = [pltpu.make_async_copy(w_in, w_ref, kv_sems.at[len(pieces)])]
     if stage != "first":
         extra.append(pltpu.make_async_copy(lse_in, lse_ref, kv_sems.at[len(pieces) + 1]))
@@ -186,7 +185,8 @@
 
     ends = [jnp.int32(0)]
     for o in range(owners):
-        ends.append(lax.fori_loop(o * rows, (o + 1) * rows, scan, ends[-1], unroll=8))
+        first = (base + o) * rows
+        ends.append(lax.fori_loop(first, first + rows, scan, ends[-1], unroll=8))
     found = ends[-1]
 
     def row_of(slot):
@@ -217,7 +217,7 @@
 
     def blocks_of(slot):
         item = items[slot]
-        return [(item // rows) * 64 + blk_ref[item * 8 + t] for t in range(8)]
+        return [(item // rows - base) * 64 + blk_ref[item * 8 + t] for t in range(8)]
 
     def latents(b):
         if stage == "first":
@@ -272,9 +272,8 @@
         begin, end = ends[o], ends[o + 1]
         for copy in copies[o]:
             copy.wait()
-        if o == 0:
-            for copy in extra:
-                copy.start()
+        for copy in (copies[o + 1] if o + 1 < owners else []) + (extra if o == 0 else []):
+            copy.start()
 
         def several(j, carry):
             first = begin + AT_ONCE * j
@@ -351,7 +350,7 @@
         each(lambda slot: store_row(slot).wait())
 
 
-def attend(queries, w_uv, blocks, live, parity, arrays, pieces, owners, stage, after, earlier):
+def attend(queries, w_uv, blocks, live, parity, arrays, pieces, base, owners, stage, after, earlier):
     rows = queries.shape[0]
     slots = owners * GROUP * 2
     all_blocks = (owners * 64,) if stage == "first" else (owners * 4 * PAIRS,)
@@ -363,7 +362,7 @@
     if earlier:
         in_specs += [anywhere, anywhere]
     return pl.pallas_call(
-        functools.partial(attend_kernel, owners, pieces, len(after), stage),
+        functools.partial(attend_kernel, base, owners, pieces, len(after), stage),
         out_shape=[
             jax.ShapeDtypeStruct((rows, 64, 128), jnp.float32),
             jax.ShapeDtypeStruct((rows, 128), jnp.float32),
@@ -485,8 +484,9 @@
     offsets = jnp.array([0, NY - 1, 1, 2], jnp.int32)
     targets = (y_here + offsets) % NY * GROUP + me % GROUP
 
-    def stage_of(name, which, lists, after, earlier=()):
-        blocks, live = tables(table, targets[which])
+    blocks, live = tables(table, targets)
+
+    def stage_of(name, base, lists, after, earlier=()):
         pieces, arrays = [], []
         for owner, quarters in enumerate(lists):
             if quarters is None:
@@ -497,27 +497,40 @@
                 pieces += [(owner, "other", 0), (owner, "other", PAIRS)]
                 arrays += quarters
         return attend(
-            all_queries, w_uv, blocks, live, parities, arrays, pieces, len(lists), name, after, earlier
+            all_queries,
+            w_uv,
+            blocks,
+            live,
+            parities,
+            arrays,
+            pieces,
+            base,
+            len(lists),
+            name,
+            after,
+            earlier,
         )
 
-    state = stage_of("first", slice(0, 1), [None], (m_l, p_r))
-    t_a, t_b, m_r, p_l, *state = gate(t_a, t_b, m_r, p_l, *state)
+    state = stage_of("first", 0, [None], (m_l, p_r))
+    t_a, t_b, m_r, p_l, own_lse, *state = gate(t_a, t_b, m_r, p_l, own_lse, *state)
     t_l = along_x(t_a, 1)
     t_r = along_x(t_b, -1)
     state = stage_of(
         "middle",
-        slice(1, 3),
+        1,
         [(m_a, m_b, m_l, m_r), (p_a, p_b, p_l, p_r)],
-        (t_a, t_b, own_lse),
+        (t_a, t_b),
         tuple(state),
     )
-    part, lse = stage_of("last", slice(3, 4), [(t_a, t_b, t_l, t_r)], (), tuple(state))
+    part, lse = stage_of("last", 3, [(t_a, t_b, t_l, t_r)], (), tuple(state))
 
     width = part.shape[1]
     part = part.reshape(NZ, NC, row_count, width, -1)
     lse = lse[:, :width].reshape(NZ, NC, row_count, width)
     pick = lambda array, which: lax.dynamic_index_in_dim(array, which, 1, keepdims=False)
-    mine, theirs = pick(part, core), other_core(pick(part, 1 - core).astype(jnp.bfloat16))
+    theirs = other_core(pick(part, 1 - core).astype(jnp.bfloat16))
+    part, theirs = gate(part, theirs)
+    mine = pick(part, core)
     lse_mine, lse_theirs = pick(lse, core), other_core(pick(lse, 1 - core))
     most = jnp.maximum(lse_mine, lse_theirs)
     w_mine, w_theirs = jnp.exp(lse_mine - most), jnp.exp(lse_theirs - most)

time: 215 us -> 216 us (level); the launches traced: 213 us -> 216 us
  Pallas kernels: 41.6 us -> 44.2 us
    ppermute x2, starting transfers between devices: 5.45 us -> 0.58 us  [other_core(): lax.ppermute(array, 'cache', [(place(y, z, c), place(y, z, 1 - c)) for y,...]
    all_to_all x1, starting transfers between devices: 9.48 us -> 13.2 us  [body(): lax.all_to_all(jnp.concatenate([chip_part, stats], 1), 'cache', split_axi...]
    pallas_call x3, Pallas kernels: 37.1 us -> 39.7 us  [attend(): pl.pallas_call(functools.partial(attend_kernel, base, owners, pieces, len...]
    unnamed x37 -> x57, local copies, waits for them, and re-layouts: 3.14 us -> 4.76 us
  transfers between devices with their start and end apart: 17 -> 17, of which waited for: 14 -> 12; matrix products, arithmetic and copies ran while one was open for 9% -> 8% of each run, Pallas kernels for 12% -> 11%
where the time goes in v4:
time: 216 us
  waiting for transfers between devices  90.8 us (42%)
  Pallas kernels  44.2 us (20%)
  starting transfers between devices  31.7 us (15%)
  between operations  16.7 us (8%)
  other arithmetic  15.2 us (7%)
  local copies, waits for them, and re-layouts  12.4 us (6%)
  matrix products  5.24 us (2%)
    pallas_call x3, Pallas kernels, attend(): pl.pallas_call(functools.partial(attend_kernel, base, owners, pieces, len...  39.7 us
    ppermute x6, waiting for transfers between devices, along_y(): lax.ppermute(array, 'cache', [(place(y, z, c), place(y + by, z, c)) for y...  36.7 us
    all_to_all x1, waiting for transfers between devices, body(): lax.all_to_all(jnp.concatenate([chip_part, stats], 1), 'cache', split_axi...  28.4 us
    ppermute x6, waiting for transfers between devices, along_x(): lax.ppermute(array, 'tensor', [(i, (i + by) % NX) for i in range(NX)])  15.2 us
    all_to_all x1, starting transfers between devices, body(): lax.all_to_all(jnp.concatenate([chip_part, stats], 1), 'cache', split_axi...  13.2 us
    ppermute x6, starting transfers between devices, along_y(): lax.ppermute(array, 'cache', [(place(y, z, c), place(y + by, z, c)) for y...  9.45 us
    ppermute x6, starting transfers between devices, along_x(): lax.ppermute(array, 'tensor', [(i, (i + by) % NX) for i in range(NX)])  8.35 us
    psum x1, waiting for transfers between devices, body(): summed = lax.psum(partial_sum, 'tensor')  8.09 us
  transfers between devices with their start and end apart: 17, of which 12 were waited for; matrix products, arithmetic and copies ran while one was open for 8% of the time, Pallas kernels for 11%

profile of v4, /device:TPU:1, one launch (start us, length us, event | category | flops | bytes accessed | tf_op | source)
XLA Modules:
  0.0 216.3 jit_solution(884592454117088569)
XLA Ops:
  8.1 4.5 %shard_map.122 = (bf16[8,144,512]{2,1,0:T(8,128)(2,1)}, bf16[8,144,512]{2,1,0:T(8,128)(2,1)}, s32[8]{0:T(128)}) custom-call(s32[1]{0:T(128)} %bitcast.1.par_ref.refs_2_, s32[8]{0:T(128)} %len_in.1, bf16[64,64,576]{2,1,0:T(8,128)(2,1)} %refs_5_.1), custom_call_target="tpu_custom_call" | custom-call | tf_op jit(solution)/shard_map/pallas_call | solution.py:131
  13.4 1.4 fusion.5
  15.7 1.5 maximum_bitcast_fusion
  18.8 2.2 %collective-permute-start = (bf16[8,144,512]{2,1,0:T(8,128)(2,1)}, bf16[8,144,512]{2,1,0:T(8,128)(2,1)S(1)}, u32[]{:S(2)}, u32[]{:S(2)}) collective-permute-start(bf16[8,144,512]{2,1,0:T(8,128)(2,1)} %get-tuple-element.36.refs_0_), channel_id=1, source_target_pairs={{0,64},{4,68},{8,72},{12,76},{16,80},{20,84},{24,88},{28,92},{32,9... | collective-permute-start | bytes 3538952 | tf_op jit(solution)/shard_map/ppermute | solution.py:33
  21.0 1.5 collective-permute-start.1
  22.6 23.9 %collective-permute-done.refs_2_ = bf16[8,144,512]{2,1,0:T(8,128)(2,1)S(1)} collective-permute-done((bf16[8,144,512]{2,1,0:T(8,128)(2,1)}, bf16[8,144,512]{2,1,0:T(8,128)(2,1)S(1)}, u32[]{:S(2)}, u32[]{:S(2)}) %collective-permute-start) | collective-permute-done | bytes 1179680 | tf_op jit(solution)/shard_map/ppermute | solution.py:33
  46.4 1.2 collective-permute-done.1.refs_3_
  47.6 1.6 collective-permute-start.2
  49.2 1.5 collective-permute-start.3
  50.6 2.5 %collective-permute-start.4 = (bf16[8,144,512]{2,1,0:T(8,128)(2,1)}, bf16[8,144,512]{2,1,0:T(8,128)(2,1)S(1)}, u32[]{:S(2)}, u32[]{:S(2)}) collective-permute-start(bf16[8,144,512]{2,1,0:T(8,128)(2,1)} %get-tuple-element.40.refs_4_), channel_id=1, source_target_pairs={{0,1},{1,2},{2,3},{3,0},{4,5},{5,6},{6,7},{7,4},{8,9},{9,10},{10,1... | collective-permute-start | bytes 3538952 | tf_op jit(solution)/shard_map/ppermute | solution.py:39
  53.1 1.3 collective-permute-start.5
  55.0 8.1 %all-reduce.5.cloned.1.call-done.refs_6_ = f32[8,4,576]{2,1,0:T(4,128)} async-done(((f32[8,4,576]{2,1,0:T(4,128)}), f32[8,4,576]{2,1,0:T(4,128)}) %all-reduce.5.cloned.1.call-update) | async-done | bytes 73744 | tf_op jit(solution)/shard_map/psum | solution.py:452
  63.1 11.2 %collective-permute-done.2.refs_0_ = bf16[8,144,512]{2,1,0:T(8,128)(2,1)} collective-permute-done((bf16[8,144,512]{2,1,0:T(8,128)(2,1)}, bf16[8,144,512]{2,1,0:T(8,128)(2,1)}, u32[]{:S(2)}, u32[]{:S(2)}) %collective-permute-start.2) | collective-permute-done | bytes 1179680 | tf_op jit(solution)/shard_map/ppermute | solution.py:33
  74.8 4.5 %collective-permute-done.4.refs_2_ = bf16[8,144,512]{2,1,0:T(8,128)(2,1)S(1)} collective-permute-done((bf16[8,144,512]{2,1,0:T(8,128)(2,1)}, bf16[8,144,512]{2,1,0:T(8,128)(2,1)S(1)}, u32[]{:S(2)}, u32[]{:S(2)}) %collective-permute-start.4) | collective-permute-done | bytes 1179680 | tf_op jit(solution)/shard_map/ppermute | solution.py:39
  80.3 2.7 %collective-permute-start.7 = (bf16[8,144,512]{2,1,0:T(8,128)(2,1)}, bf16[8,144,512]{2,1,0:T(8,128)(2,1)}, u32[]{:S(2)}, u32[]{:S(2)}) collective-permute-start(bf16[8,144,512]{2,1,0:T(8,128)(2,1)} %get-tuple-element.43.refs_10_), channel_id=1, source_target_pairs={{0,192},{4,196},{8,200},{12,204},{16,208},{20,212},{24,216},{28,22... | collective-permute-start | bytes 3538952 | tf_op jit(solution)/shard_map/ppermute | solution.py:33
  83.0 1.9 collective-permute-start.8
  87.8 1.4 fusion.60
  95.5 1.3 fusion.38
  96.8 11.3 %shard_map.125 = (f32[128,64,128]{2,1,0:T(8,128)}, f32[128,128]{1,0:T(8,128)}) custom-call(s32[4096]{0:T(1024)} %reshape.206.refs_0_, s32[512]{0:T(512)} %bitcast.119, s32[1]{0:T(128)} %bitcast.1.par_ref.refs_2_, bf16[128,64,640]{2,1,0:T(8,128)(2,1)} %all-gather.2.cloned.1.call-done.refs_3_, bf16[16,512,128]{2,1,0:T(8,128)(2,1)} %refs_4_.5, ...), custom_call_target="tpu_custom_call" | custom-call | flops 2281701376 | bytes 22020096 | tf_op jit(solution)/shard_map/pallas_call | solution.py:364
  108.2 2.3 %collective-permute-done.9.refs_3_ = bf16[8,144,512]{2,1,0:T(8,128)(2,1)} collective-permute-done((bf16[8,144,512]{2,1,0:T(8,128)(2,1)}, bf16[8,144,512]{2,1,0:T(8,128)(2,1)}, u32[]{:S(2)}, u32[]{:S(2)}) %collective-permute-start.9) | collective-permute-done | bytes 1179680 | tf_op jit(solution)/shard_map/ppermute | solution.py:39
  110.4 2.7 %collective-permute-start.11 = (bf16[8,144,512]{2,1,0:T(8,128)(2,1)}, bf16[8,144,512]{2,1,0:T(8,128)(2,1)}, u32[]{:S(2)}, u32[]{:S(2)}) collective-permute-start(bf16[8,144,512]{2,1,0:T(8,128)(2,1)} %get-tuple-element.52.refs_14_.refs_6_), channel_id=1, source_target_pairs={{0,3},{1,0},{2,1},{3,2},{4,7},{5,4},{6,5},{7,6},{8,11},{9,8},{10,9... | collective-permute-start | bytes 3538952 | tf_op jit(solution)/shard_map/ppermute | solution.py:39
  113.1 13.5 %shard_map.127 = (f32[128,64,128]{2,1,0:T(8,128)}, f32[128,128]{1,0:T(8,128)}) custom-call(s32[4096]{0:T(1024)} %reshape.206.refs_0_, s32[512]{0:T(512)} %bitcast.120, s32[1]{0:T(128)} %bitcast.1.par_ref.refs_2_, bf16[128,64,640]{2,1,0:T(8,128)(2,1)} %all-gather.2.cloned.1.call-done.refs_3_, bf16[16,512,128]{2,1,0:T(8,128)(2,1)} %refs_4_.5, ...), custom_call_target="tpu_custom_call" | custom-call | flops 4563402752 | bytes 27262976 | tf_op jit(solution)/shard_map/pallas_call | solution.py:364
  126.6 8.3 %collective-permute-done.10.refs_7_ = bf16[8,144,512]{2,1,0:T(8,128)(2,1)S(1)} collective-permute-done((bf16[8,144,512]{2,1,0:T(8,128)(2,1)}, bf16[8,144,512]{2,1,0:T(8,128)(2,1)S(1)}, u32[]{:S(2)}, u32[]{:S(2)}) %collective-permute-start.10) | collective-permute-done | bytes 1179680 | tf_op jit(solution)/shard_map/ppermute | solution.py:39
  135.9 14.8 %shard_map.128 = (f32[128,64,128]{2,1,0:T(8,128)}, f32[128,128]{1,0:T(8,128)}) custom-call(s32[4096]{0:T(1024)} %reshape.206.refs_0_, s32[512]{0:T(512)} %bitcast.121, s32[1]{0:T(128)} %bitcast.1.par_ref.refs_2_, bf16[128,64,640]{2,1,0:T(8,128)(2,1)} %all-gather.2.cloned.1.call-done.refs_3_, ...), custom_call_target="tpu_custom_call", output_to_operand_aliasing={{0}: (9, {})} | custom-call | flops 2281701376 | bytes 22020096 | tf_op jit(solution)/shard_map/pallas_call | solution.py:364
  150.7 2.8 %fusion.30 = bf16[8,8,64,128]{3,2,1,0:T(8,128)(2,1)} fusion(f32[8,2,8,64,128]{4,3,2,1,0:T(8,128)} %bitcast.108, s32[]{:T(128)S(6)} %select_n.83), kind=kLoop, calls=%fused_computation.22 | loop fusion | bytes 2097156 | tf_op jit(solution)/shard_map/convert_element_type | solution.py:531
  154.1 2.1 collective-permute-done.13
  157.6 2.6 %fusion.4 = bf16[8,8,64,128]{3,2,1,0:T(8,128)(2,1)S(1)} fusion(bf16[8,8,64,128]{3,2,1,0:T(8,128)(2,1)} %get-tuple-element.62, f32[8,2,8,64,128]{4,3,2,1,0:T(8,128)} %get-tuple-element.60, s32[]{:T(128)S(6)} %select_n.84, f32[8,8,64]{2,1,0:T(8,128)S(1)} %get-tuple-element.83, f32[8,8,64]{2,1,0:T(8,128)S(1)} %get-tuple-element.82), kind=kLoop, calls=%fused_computation.7 | loop fusion | flops 2621440 | bytes 4227076 | tf_op jit(solution)/shard_map/convert_element_type | solution.py:547
  160.2 1.1 fusion.29
  161.3 13.2 %all-to-all-start = ((bf16[8,528,128]{2,1,0:T(8,128)(2,1)}), bf16[8,528,128]{2,1,0:T(8,128)(2,1)S(1)}, u32[]{:S(2)}, u32[]{:S(2)}) async-start(bf16[8,528,128]{2,1,0:T(8,128)(2,1)} %fusion.29), calls=%async_computation | async-start | bytes 2162688 | tf_op jit(solution)/shard_map/all_to_all | solution.py:549
  175.0 1.1 copy.107
  176.1 28.4 %all-to-all-done = bf16[8,528,128]{2,1,0:T(8,128)(2,1)S(1)} async-done(((bf16[8,528,128]{2,1,0:T(8,128)(2,1)}), bf16[8,528,128]{2,1,0:T(8,128)(2,1)S(1)}, u32[]{:S(2)}, u32[]{:S(2)}) %all-to-all-start) | async-done | bytes 1081376 | tf_op jit(solution)/shard_map/all_to_all | solution.py:549
  206.0 2.1 fusion.25
  (130 shorter events, 19.2 us)
Async XLA Ops:
  8.0 5.3 %copy-start = (bf16[1792,576]{0,1:T(8,128)(2,1)S(1)}, bf16[1792,576]{0,1:T(8,128)(2,1)}, u32[]{:S(2)}) copy-start(bf16[1792,576]{0,1:T(8,128)(2,1)} %param.12) | copy-start | bytes 6193156
  8.0 55.1 %all-reduce.5.cloned.1.call-start = ((), (), s32[]{:S(2)}) async-start(), calls=%async_computation.2 | async-start | bytes 163840 | tf_op jit(solution)/shard_map/psum | solution.py:452
  8.1 5.3 %copy-start.10 = (bf16[8,4,1792]{2,1,0:T(4,128)(2,1)S(1)}, bf16[8,4,1792]{2,1,0:T(4,128)(2,1)}, u32[]{:S(2)}) copy-start(bf16[8,4,1792]{2,1,0:T(4,128)(2,1)} %param.11) | copy-start | bytes 344068
  12.6 2.2 %copy-start.25 = (s32[8]{0:T(128)S(1)}, s32[8]{0:T(128)}, u32[]{:S(2)}) copy-start(s32[8]{0:T(128)} %get-tuple-element.33) | copy-start | bytes 100
  12.6 2.5 %copy-start.14 = (bf16[8,4,1024]{2,1,0:T(4,128)(2,1)S(1)}, bf16[8,4,1024]{2,1,0:T(4,128)(2,1)}, u32[]{:S(2)}) copy-start(bf16[8,4,1024]{2,1,0:T(4,128)(2,1)} %param.15) | copy-start | bytes 196612
  14.8 75.1 %all-gather.2.cloned.1.call-start = ((), (), s32[]{:S(2)}) async-start(), calls=%async_computation.1 | async-start | bytes 11141120 | tf_op jit(solution)/shard_map/all_gather | solution.py:442
  15.7 2.1 copy-start.23
  18.8 27.6 %collective-permute-start = (bf16[8,144,512]{2,1,0:T(8,128)(2,1)}, bf16[8,144,512]{2,1,0:T(8,128)(2,1)S(1)}, u32[]{:S(2)}, u32[]{:S(2)}) collective-permute-start(bf16[8,144,512]{2,1,0:T(8,128)(2,1)} %get-tuple-element.36.refs_0_), channel_id=1, source_target_pairs={{0,64},{4,68},{8,72},{12,76},{16,80},{20,84},{24,88},{28,92},{32,9... | collective-permute-start | bytes 3538952 | tf_op jit(solution)/shard_map/ppermute | solution.py:33
  21.0 33.9 %copy-start.26 = (s32[4]{0:T(128)S(1)}, s32[4]{0:T(128)}, u32[]{:S(2)}) copy-start(s32[4]{0:T(128)} %constant.145.clone) | copy-start | bytes 52
  21.0 26.6 %collective-permute-start.1 = (bf16[8,144,512]{2,1,0:T(8,128)(2,1)}, bf16[8,144,512]{2,1,0:T(8,128)(2,1)}, u32[]{:S(2)}, u32[]{:S(2)}) collective-permute-start(bf16[8,144,512]{2,1,0:T(8,128)(2,1)} %get-tuple-element.37.refs_1_), channel_id=1, source_target_pairs={{0,192},{4,196},{8,200},{12,204},{16,208},{20,212},{24,216},{28,22... | collective-permute-start | bytes 3538952 | tf_op jit(solution)/shard_map/ppermute | solution.py:33
  47.6 26.7 %collective-permute-start.2 = (bf16[8,144,512]{2,1,0:T(8,128)(2,1)}, bf16[8,144,512]{2,1,0:T(8,128)(2,1)}, u32[]{:S(2)}, u32[]{:S(2)}) collective-permute-start(bf16[8,144,512]{2,1,0:T(8,128)(2,1)} %get-tuple-element.38), channel_id=1, source_target_pairs={{0,64},{4,68},{8,72},{12,76},{16,80},{20,84},{24,88},{28,92},{32,9... | collective-permute-start | bytes 3538952 | tf_op jit(solution)/shard_map/ppermute | solution.py:33
  49.2 25.6 %collective-permute-start.3 = (bf16[8,144,512]{2,1,0:T(8,128)(2,1)}, bf16[8,144,512]{2,1,0:T(8,128)(2,1)}, u32[]{:S(2)}, u32[]{:S(2)}) collective-permute-start(bf16[8,144,512]{2,1,0:T(8,128)(2,1)} %get-tuple-element.39), channel_id=1, source_target_pairs={{0,192},{4,196},{8,200},{12,204},{16,208},{20,212},{24,216},{28,22... | collective-permute-start | bytes 3538952 | tf_op jit(solution)/shard_map/ppermute | solution.py:33
  50.6 28.7 %collective-permute-start.4 = (bf16[8,144,512]{2,1,0:T(8,128)(2,1)}, bf16[8,144,512]{2,1,0:T(8,128)(2,1)S(1)}, u32[]{:S(2)}, u32[]{:S(2)}) collective-permute-start(bf16[8,144,512]{2,1,0:T(8,128)(2,1)} %get-tuple-element.40.refs_4_), channel_id=1, source_target_pairs={{0,1},{1,2},{2,3},{3,0},{4,5},{5,6},{6,7},{7,4},{8,9},{9,10},{10,1... | collective-permute-start | bytes 3538952 | tf_op jit(solution)/shard_map/ppermute | solution.py:39
  53.1 26.3 %collective-permute-start.5 = (bf16[8,144,512]{2,1,0:T(8,128)(2,1)}, bf16[8,144,512]{2,1,0:T(8,128)(2,1)}, u32[]{:S(2)}, u32[]{:S(2)}) collective-permute-start(bf16[8,144,512]{2,1,0:T(8,128)(2,1)} %get-tuple-element.41.refs_5_), channel_id=1, source_target_pairs={{0,3},{1,0},{2,1},{3,2},{4,7},{5,4},{6,5},{7,6},{8,11},{9,8},{10,9... | collective-permute-start | bytes 3538952 | tf_op jit(solution)/shard_map/ppermute | solution.py:39
  54.9 34.3 %copy-start.20 = (pred[64,4]{0,1:T(4,128)(4,1)}, pred[64,4]{0,1:T(4,128)(4,1)S(1)}, u32[]{:S(2)}) copy-start(pred[64,4]{0,1:T(4,128)(4,1)S(1)} %iota_compare_fusion.3) | copy-start | bytes 772
  55.0 36.2 %copy-start.19 = (s32[4]{0:T(128)}, s32[4]{0:T(128)S(1)}, u32[]{:S(2)}) copy-start(s32[4]{0:T(128)S(1)} %fusion.51) | copy-start | bytes 52
  55.0 31.8 %copy-start.24 = (f32[512]{0:T(512)S(1)}, f32[512]{0:T(512)}, u32[]{:S(2)}) copy-start(f32[512]{0:T(512)} %param.13) | copy-start | bytes 6148
  80.3 27.8 %collective-permute-start.6 = (bf16[8,144,512]{2,1,0:T(8,128)(2,1)}, bf16[8,144,512]{2,1,0:T(8,128)(2,1)S(1)}, u32[]{:S(2)}, u32[]{:S(2)}) collective-permute-start(bf16[8,144,512]{2,1,0:T(8,128)(2,1)} %get-tuple-element.42.refs_5_), channel_id=1, source_target_pairs={{0,64},{4,68},{8,72},{12,76},{16,80},{20,84},{24,88},{28,92},{32,9... | collective-permute-start | bytes 3538952 | tf_op jit(solution)/shard_map/ppermute | solution.py:33
  80.3 27.8 %collective-permute-start.7 = (bf16[8,144,512]{2,1,0:T(8,128)(2,1)}, bf16[8,144,512]{2,1,0:T(8,128)(2,1)}, u32[]{:S(2)}, u32[]{:S(2)}) collective-permute-start(bf16[8,144,512]{2,1,0:T(8,128)(2,1)} %get-tuple-element.43.refs_10_), channel_id=1, source_target_pairs={{0,192},{4,196},{8,200},{12,204},{16,208},{20,212},{24,216},{28,22... | collective-permute-start | bytes 3538952 | tf_op jit(solution)/shard_map/ppermute | solution.py:33
  83.0 25.1 %collective-permute-start.8 = (bf16[8,144,512]{2,1,0:T(8,128)(2,1)}, bf16[8,144,512]{2,1,0:T(8,128)(2,1)}, u32[]{:S(2)}, u32[]{:S(2)}) collective-permute-start(bf16[8,144,512]{2,1,0:T(8,128)(2,1)} %get-tuple-element.44.refs_6_), channel_id=1, source_target_pairs={{0,3},{1,0},{2,1},{3,2},{4,7},{5,4},{6,5},{7,6},{8,11},{9,8},{10,9... | collective-permute-start | bytes 3538952 | tf_op jit(solution)/shard_map/ppermute | solution.py:39
  84.9 25.5 %collective-permute-start.9 = (bf16[8,144,512]{2,1,0:T(8,128)(2,1)}, bf16[8,144,512]{2,1,0:T(8,128)(2,1)}, u32[]{:S(2)}, u32[]{:S(2)}) collective-permute-start(bf16[8,144,512]{2,1,0:T(8,128)(2,1)} %get-tuple-element.45.refs_9_), channel_id=1, source_target_pairs={{0,1},{1,2},{2,3},{3,0},{4,5},{5,6},{6,7},{7,4},{8,9},{9,10},{10,1... | collective-permute-start | bytes 3538952 | tf_op jit(solution)/shard_map/ppermute | solution.py:39
  108.1 2.3 %copy-start.1 = (bf16[8,144,512]{2,1,0:T(8,128)(2,1)}, bf16[8,144,512]{2,1,0:T(8,128)(2,1)S(1)}, u32[]{:S(2)}) copy-start(bf16[8,144,512]{2,1,0:T(8,128)(2,1)S(1)} %collective-permute-done.6.refs_0_) | copy-start | bytes 3538948
  110.4 24.5 %collective-permute-start.10 = (bf16[8,144,512]{2,1,0:T(8,128)(2,1)}, bf16[8,144,512]{2,1,0:T(8,128)(2,1)S(1)}, u32[]{:S(2)}, u32[]{:S(2)}) collective-permute-start(bf16[8,144,512]{2,1,0:T(8,128)(2,1)} %get-tuple-element.51.refs_13_.refs_5_), channel_id=1, source_target_pairs={{0,1},{1,2},{2,3},{3,0},{4,5},{5,6},{6,7},{7,4},{8,9},{9,10},{10,1... | collective-permute-start | bytes 3538952 | tf_op jit(solution)/shard_map/ppermute | solution.py:39
  110.4 24.5 %collective-permute-start.11 = (bf16[8,144,512]{2,1,0:T(8,128)(2,1)}, bf16[8,144,512]{2,1,0:T(8,128)(2,1)}, u32[]{:S(2)}, u32[]{:S(2)}) collective-permute-start(bf16[8,144,512]{2,1,0:T(8,128)(2,1)} %get-tuple-element.52.refs_14_.refs_6_), channel_id=1, source_target_pairs={{0,3},{1,0},{2,1},{3,2},{4,7},{5,4},{6,5},{7,6},{8,11},{9,8},{10,9... | collective-permute-start | bytes 3538952 | tf_op jit(solution)/shard_map/ppermute | solution.py:39
  150.7 3.3 %copy-start.15 = (f32[128,128]{1,0:T(8,128)S(1)}, f32[128,128]{1,0:T(8,128)}, u32[]{:S(2)}) copy-start(f32[128,128]{1,0:T(8,128)} %get-tuple-element.61) | copy-start | bytes 196612
  153.5 3.0 %collective-permute-start.12 = (bf16[8,8,64,128]{3,2,1,0:T(8,128)(2,1)}, bf16[8,8,64,128]{3,2,1,0:T(8,128)(2,1)S(1)}, u32[]{:S(2)}, u32[]{:S(2)}) collective-permute-start(bf16[8,8,64,128]{3,2,1,0:T(8,128)(2,1)} %fusion.30), channel_id=1, source_target_pairs={{0,4},{4,0},{8,12},{12,8},{16,20},{20,16},{24,28},{28,24},{32,36},... | collective-permute-start | bytes 3145736 | tf_op jit(solution)/shard_map/ppermute | solution.py:43
  154.0 2.2 %collective-permute-start.13 = (f32[8,8,64]{2,1,0:T(8,128)S(1)}, f32[8,8,64]{2,1,0:T(8,128)S(1)}, u32[]{:S(2)}, u32[]{:S(2)}) collective-permute-start(f32[8,8,64]{2,1,0:T(8,128)S(1)} %dynamic-slice_bitcast_fusion), channel_id=1, source_target_pairs={{0,4},{4,0},{8,12},{12,8},{16,20},{20,16},{24,28},{28,24},{32,36},... | collective-permute-start | bytes 49160 | tf_op jit(solution)/shard_map/ppermute | solution.py:43
  161.3 13.2 %copy-start.17 = (f32[8,64]{1,0:T(8,128)S(1)}, f32[8,64]{1,0:T(8,128)}, u32[]{:S(2)}) copy-start(f32[8,64]{1,0:T(8,128)} %copy-done.16) | copy-start | bytes 6148
  161.3 13.3 %copy-start.12 = (f32[8,64]{1,0:T(8,128)S(1)}, f32[8,64]{1,0:T(8,128)}, u32[]{:S(2)}) copy-start(f32[8,64]{1,0:T(8,128)} %copy-done.11) | copy-start | bytes 6148
  161.3 13.3 %copy-start.21 = (pred[64,4]{0,1:T(4,128)(4,1)S(1)}, pred[64,4]{0,1:T(4,128)(4,1)}, u32[]{:S(2)}) copy-start(pred[64,4]{0,1:T(4,128)(4,1)} %copy-done.20) | copy-start | bytes 772
  161.3 43.2 %all-to-all-start = ((bf16[8,528,128]{2,1,0:T(8,128)(2,1)}), bf16[8,528,128]{2,1,0:T(8,128)(2,1)S(1)}, u32[]{:S(2)}, u32[]{:S(2)}) async-start(bf16[8,528,128]{2,1,0:T(8,128)(2,1)} %fusion.29), calls=%async_computation | async-start | bytes 2162688 | tf_op jit(solution)/shard_map/all_to_all | solution.py:549
  174.5 30.0 %copy-start.13 = (f32[8,64]{1,0:T(8,128)S(1)}, f32[8,64]{1,0:T(8,128)}, u32[]{:S(2)}) copy-start(f32[8,64]{1,0:T(8,128)} %get-tuple-element.63) | copy-start | bytes 6148
  (12 other events, 13.3 us)
Sparse Core Ops, SparseCore 0:
  14.9 48.1 all-reduce.4
Sparse Core Ops, SparseCore 1:
  18.9 69.9 all-gather.1

commit v5 on v4

--- a/solution.py
+++ b/solution.py
@@ -493,9 +493,12 @@
                 pieces.append((owner, "all", 0))
                 arrays.append(latent_cache)
             else:
-                pieces += [(owner, "mine", 0), (owner, "mine", PAIRS)]
-                pieces += [(owner, "other", 0), (owner, "other", PAIRS)]
-                arrays += quarters
+                for which, quarter in enumerate(quarters):
+                    offset = which % 2 * PAIRS
+                    for array in quarter if isinstance(quarter, tuple) else (quarter,):
+                        pieces.append((owner, "mine" if which < 2 else "other", offset))
+                        arrays.append(array)
+                        offset += array.shape[0]
         return attend(
             all_queries,
             w_uv,
@@ -512,9 +515,12 @@
         )
 
     state = stage_of("first", 0, [None], (m_l, p_r))
-    t_a, t_b, m_r, p_l, own_lse, *state = gate(t_a, t_b, m_r, p_l, own_lse, *state)
-    t_l = along_x(t_a, 1)
-    t_r = along_x(t_b, -1)
+    part_l, part_r = m_l[PAIRS // 2 :], p_r[PAIRS // 2 :]
+    t_a, t_b, m_r, p_l, part_l, part_r, own_lse, *state = gate(
+        t_a, t_b, m_r, p_l, part_l, part_r, own_lse, *state
+    )
+    t_l = (along_x(t_a[: PAIRS // 2], 1), along_y(part_l, 1))
+    t_r = (along_x(t_b[: PAIRS // 2], -1), along_y(part_r, -1))
     state = stage_of(
         "middle",
         1,

time: 216 us -> 216 us (level)
  waiting for transfers between devices: 90.8 us -> 81.9 us
  local copies, waits for them, and re-layouts: 12.4 us -> 19.4 us
  starting transfers between devices: 31.7 us -> 37.4 us
  other arithmetic: 15.2 us -> 12.7 us
    ppermute x6, waiting for transfers between devices: 15.2 us -> 6.53 us  [along_x(): lax.ppermute(array, 'tensor', [(i, (i + by) % NX) for i in range(NX)])]
    slice x0 -> x4, local copies, waits for them, and re-layouts: none -> 7.89 us  [the longest x2 3.92 us: body(): part_l, part_r = (m_l[PAIRS // 2:], p_r[PAIRS // 2:])]
    ppermute x6 -> x8, starting transfers between devices: 9.45 us -> 12.2 us  [along_y(): lax.ppermute(array, 'cache', [(place(y, z, c), place(y + by, z, c)) for y...]
    ppermute x2, starting transfers between devices: 0.58 us -> 2.84 us  [other_core(): lax.ppermute(array, 'cache', [(place(y, z, c), place(y, z, 1 - c)) for y,...]
    unnamed x57 -> x63, local copies, waits for them, and re-layouts: 4.76 us -> 3.76 us
    ppermute x6 -> x8, waiting for transfers between devices: 36.7 us -> 36.7 us  [along_y(): lax.ppermute(array, 'cache', [(place(y, z, c), place(y + by, z, c)) for y...]
  transfers between devices with their start and end apart: 17 -> 19, of which waited for: 12 -> 11; matrix products, arithmetic and copies ran while one was open for 8% -> 9% of each run, Pallas kernels for 11% -> 12%
where the time goes in v5:
time: 216 us; the launch traced here: 215 us
  waiting for transfers between devices  81.9 us (38%)
  Pallas kernels  42.4 us (20%)
  starting transfers between devices  37.4 us (17%)
  local copies, waits for them, and re-layouts  19.4 us (9%)
  between operations  16.8 us (8%)
  other arithmetic  12.7 us (6%)
  matrix products  4.14 us (2%)
    pallas_call x3, Pallas kernels, attend(): pl.pallas_call(functools.partial(attend_kernel, base, owners, pieces, len...  37.9 us
    ppermute x8, waiting for transfers between devices, along_y(): lax.ppermute(array, 'cache', [(place(y, z, c), place(y + by, z, c)) for y...  36.7 us
    all_to_all x1, waiting for transfers between devices, body(): lax.all_to_all(jnp.concatenate([chip_part, stats], 1), 'cache', split_axi...  28.4 us
    all_to_all x1, starting transfers between devices, body(): lax.all_to_all(jnp.concatenate([chip_part, stats], 1), 'cache', split_axi...  13.9 us
    ppermute x8, starting transfers between devices, along_y(): lax.ppermute(array, 'cache', [(place(y, z, c), place(y + by, z, c)) for y...  12.2 us
    ppermute x6, starting transfers between devices, along_x(): lax.ppermute(array, 'tensor', [(i, (i + by) % NX) for i in range(NX)])  8.35 us
    psum x1, waiting for transfers between devices, body(): summed = lax.psum(partial_sum, 'tensor')  8.07 us
    ppermute x6, waiting for transfers between devices, along_x(): lax.ppermute(array, 'tensor', [(i, (i + by) % NX) for i in range(NX)])  6.53 us
  transfers between devices with their start and end apart: 19, of which 11 were waited for; matrix products, arithmetic and copies ran while one was open for 9% of the time, Pallas kernels for 12%

profile of v5, /device:TPU:1, one launch (start us, length us, event | category | flops | bytes accessed | tf_op | source)
XLA Modules:
  0.0 214.6 jit_solution(15431052260256221412)
XLA Ops:
  8.1 4.5 %shard_map.122 = (bf16[8,144,512]{2,1,0:T(8,128)(2,1)}, bf16[8,144,512]{2,1,0:T(8,128)(2,1)}, s32[8]{0:T(128)}) custom-call(s32[1]{0:T(128)} %bitcast.1.par_ref.refs_2_, s32[8]{0:T(128)} %len_in.1, bf16[64,64,576]{2,1,0:T(8,128)(2,1)} %refs_5_.1), custom_call_target="tpu_custom_call" | custom-call | tf_op jit(solution)/shard_map/pallas_call | solution.py:131
  13.4 1.4 fusion.5
  15.7 1.5 maximum_bitcast_fusion
  18.8 2.2 %collective-permute-start = (bf16[8,144,512]{2,1,0:T(8,128)(2,1)}, bf16[8,144,512]{2,1,0:T(8,128)(2,1)S(1)}, u32[]{:S(2)}, u32[]{:S(2)}) collective-permute-start(bf16[8,144,512]{2,1,0:T(8,128)(2,1)} %get-tuple-element.38.refs_0_), channel_id=1, source_target_pairs={{0,64},{4,68},{8,72},{12,76},{16,80},{20,84},{24,88},{28,92},{32,9... | collective-permute-start | bytes 3538952 | tf_op jit(solution)/shard_map/ppermute | solution.py:33
  21.0 1.5 collective-permute-start.1
  22.5 23.9 %collective-permute-done.refs_2_ = bf16[8,144,512]{2,1,0:T(8,128)(2,1)S(1)} collective-permute-done((bf16[8,144,512]{2,1,0:T(8,128)(2,1)}, bf16[8,144,512]{2,1,0:T(8,128)(2,1)S(1)}, u32[]{:S(2)}, u32[]{:S(2)}) %collective-permute-start) | collective-permute-done | bytes 1179680 | tf_op jit(solution)/shard_map/ppermute | solution.py:33
  47.6 1.6 collective-permute-start.2
  49.1 1.5 collective-permute-start.3
  50.7 2.5 %collective-permute-start.4 = (bf16[8,144,512]{2,1,0:T(8,128)(2,1)}, bf16[8,144,512]{2,1,0:T(8,128)(2,1)S(1)}, u32[]{:S(2)}, u32[]{:S(2)}) collective-permute-start(bf16[8,144,512]{2,1,0:T(8,128)(2,1)} %get-tuple-element.42.refs_4_), channel_id=1, source_target_pairs={{0,1},{1,2},{2,3},{3,0},{4,5},{5,6},{6,7},{7,4},{8,9},{9,10},{10,1... | collective-permute-start | bytes 3538952 | tf_op jit(solution)/shard_map/ppermute | solution.py:39
  55.0 8.1 %all-reduce.5.cloned.1.call-done.refs_6_ = f32[8,4,576]{2,1,0:T(4,128)} async-done(((f32[8,4,576]{2,1,0:T(4,128)}), f32[8,4,576]{2,1,0:T(4,128)}) %all-reduce.5.cloned.1.call-update) | async-done | bytes 73744 | tf_op jit(solution)/shard_map/psum | solution.py:452
  63.1 11.2 %collective-permute-done.2.refs_0_ = bf16[8,144,512]{2,1,0:T(8,128)(2,1)} collective-permute-done((bf16[8,144,512]{2,1,0:T(8,128)(2,1)}, bf16[8,144,512]{2,1,0:T(8,128)(2,1)}, u32[]{:S(2)}, u32[]{:S(2)}) %collective-permute-start.2) | collective-permute-done | bytes 1179680 | tf_op jit(solution)/shard_map/ppermute | solution.py:33
  74.8 4.6 %collective-permute-done.4.refs_2_ = bf16[8,144,512]{2,1,0:T(8,128)(2,1)S(1)} collective-permute-done((bf16[8,144,512]{2,1,0:T(8,128)(2,1)}, bf16[8,144,512]{2,1,0:T(8,128)(2,1)S(1)}, u32[]{:S(2)}, u32[]{:S(2)}) %collective-permute-start.4) | collective-permute-done | bytes 1179680 | tf_op jit(solution)/shard_map/ppermute | solution.py:39
  80.4 2.7 %collective-permute-start.7 = (bf16[8,144,512]{2,1,0:T(8,128)(2,1)}, bf16[8,144,512]{2,1,0:T(8,128)(2,1)}, u32[]{:S(2)}, u32[]{:S(2)}) collective-permute-start(bf16[8,144,512]{2,1,0:T(8,128)(2,1)} %get-tuple-element.45.refs_10_), channel_id=1, source_target_pairs={{0,192},{4,196},{8,200},{12,204},{16,208},{20,212},{24,216},{28,22... | collective-permute-start | bytes 3538952 | tf_op jit(solution)/shard_map/ppermute | solution.py:33
  83.1 1.9 collective-permute-start.8
  85.0 2.0 slice.77.refs_4_
  86.9 2.0 slice.78.refs_5_
  95.9 1.3 fusion.38
  97.2 11.3 %shard_map.125 = (f32[128,64,128]{2,1,0:T(8,128)}, f32[128,128]{1,0:T(8,128)}) custom-call(s32[4096]{0:T(1024)} %reshape.206.refs_0_, s32[512]{0:T(512)} %bitcast.119, s32[1]{0:T(128)} %bitcast.1.par_ref.refs_2_, bf16[128,64,640]{2,1,0:T(8,128)(2,1)} %all-gather.2.cloned.1.call-done.refs_3_, bf16[16,512,128]{2,1,0:T(8,128)(2,1)} %refs_4_.5, ...), custom_call_target="tpu_custom_call" | custom-call | flops 2281701376 | bytes 22020096 | tf_op jit(solution)/shard_map/pallas_call | solution.py:364
  108.6 1.8 collective-permute-done.9.refs_3_
  110.4 2.0 slice.83
  112.4 1.9 slice.84
  114.4 2.7 %collective-permute-start.12 = (bf16[4,144,512]{2,1,0:T(8,128)(2,1)}, bf16[4,144,512]{2,1,0:T(8,128)(2,1)}, u32[]{:S(2)}, u32[]{:S(2)}) collective-permute-start(bf16[4,144,512]{2,1,0:T(8,128)(2,1)} %slice.84), channel_id=1, source_target_pairs={{0,3},{1,0},{2,1},{3,2},{4,7},{5,4},{6,5},{7,6},{8,11},{9,8},{10,9... | collective-permute-start | bytes 1769480 | tf_op jit(solution)/shard_map/ppermute | solution.py:39
  117.0 2.7 %collective-permute-start.13 = (bf16[4,144,512]{2,1,0:T(8,128)(2,1)S(1)}, bf16[4,144,512]{2,1,0:T(8,128)(2,1)}, u32[]{:S(2)}, u32[]{:S(2)}) collective-permute-start(bf16[4,144,512]{2,1,0:T(8,128)(2,1)S(1)} %copy-done.8), channel_id=1, source_target_pairs={{0,192},{4,196},{8,200},{12,204},{16,208},{20,212},{24,216},{28,22... | collective-permute-start | bytes 1769480 | tf_op jit(solution)/shard_map/ppermute | solution.py:33
  119.7 15.0 %shard_map.127 = (f32[128,64,128]{2,1,0:T(8,128)}, f32[128,128]{1,0:T(8,128)}) custom-call(s32[4096]{0:T(1024)} %reshape.206.refs_0_, s32[512]{0:T(512)} %bitcast.120, s32[1]{0:T(128)} %bitcast.1.par_ref.refs_2_, bf16[128,64,640]{2,1,0:T(8,128)(2,1)} %all-gather.2.cloned.1.call-done.refs_3_, bf16[16,512,128]{2,1,0:T(8,128)(2,1)} %refs_4_.5, ...), custom_call_target="tpu_custom_call" | custom-call | flops 4563402752 | bytes 27262976 | tf_op jit(solution)/shard_map/pallas_call | solution.py:364
  134.8 11.6 %shard_map.128 = (f32[128,64,128]{2,1,0:T(8,128)}, f32[128,128]{1,0:T(8,128)}) custom-call(s32[4096]{0:T(1024)} %reshape.206.refs_0_, s32[512]{0:T(512)} %bitcast.121, s32[1]{0:T(128)} %bitcast.1.par_ref.refs_2_, bf16[128,64,640]{2,1,0:T(8,128)(2,1)} %all-gather.2.cloned.1.call-done.refs_3_, ...), custom_call_target="tpu_custom_call", output_to_operand_aliasing={{0}: (11, {})} | custom-call | flops 2281701376 | bytes 22020096 | tf_op jit(solution)/shard_map/pallas_call | solution.py:364
  146.3 2.8 %fusion.30 = bf16[8,8,64,128]{3,2,1,0:T(8,128)(2,1)} fusion(f32[8,2,8,64,128]{4,3,2,1,0:T(8,128)} %bitcast.108, s32[]{:T(128)S(6)} %select_n.83), kind=kLoop, calls=%fused_computation.22 | loop fusion | bytes 2097156 | tf_op jit(solution)/shard_map/convert_element_type | solution.py:537
  149.2 2.5 %collective-permute-start.14 = (bf16[8,8,64,128]{3,2,1,0:T(8,128)(2,1)}, bf16[8,8,64,128]{3,2,1,0:T(8,128)(2,1)S(1)}, u32[]{:S(2)}, u32[]{:S(2)}) collective-permute-start(bf16[8,8,64,128]{3,2,1,0:T(8,128)(2,1)} %fusion.30), channel_id=1, source_target_pairs={{0,4},{4,0},{8,12},{12,8},{16,20},{20,16},{24,28},{28,24},{32,36},... | collective-permute-start | bytes 3145736 | tf_op jit(solution)/shard_map/ppermute | solution.py:43
  152.0 2.0 collective-permute-done.15
  155.2 2.6 %fusion.4 = bf16[8,8,64,128]{3,2,1,0:T(8,128)(2,1)S(1)} fusion(bf16[8,8,64,128]{3,2,1,0:T(8,128)(2,1)} %get-tuple-element.66, f32[8,2,8,64,128]{4,3,2,1,0:T(8,128)} %get-tuple-element.64, s32[]{:T(128)S(6)} %select_n.84, f32[8,8,64]{2,1,0:T(8,128)S(1)} %get-tuple-element.87, f32[8,8,64]{2,1,0:T(8,128)S(1)} %get-tuple-element.86), kind=kLoop, calls=%fused_computation.7 | loop fusion | flops 2621440 | bytes 4227076 | tf_op jit(solution)/shard_map/convert_element_type | solution.py:553
  158.9 13.9 %all-to-all-start = ((bf16[8,528,128]{2,1,0:T(8,128)(2,1)}), bf16[8,528,128]{2,1,0:T(8,128)(2,1)S(1)}, u32[]{:S(2)}, u32[]{:S(2)}) async-start(bf16[8,528,128]{2,1,0:T(8,128)(2,1)} %fusion.29), calls=%async_computation | async-start | bytes 2162688 | tf_op jit(solution)/shard_map/all_to_all | solution.py:555
  174.4 28.4 %all-to-all-done = bf16[8,528,128]{2,1,0:T(8,128)(2,1)S(1)} async-done(((bf16[8,528,128]{2,1,0:T(8,128)(2,1)}), bf16[8,528,128]{2,1,0:T(8,128)(2,1)S(1)}, u32[]{:S(2)}, u32[]{:S(2)}) %all-to-all-start) | async-done | bytes 1081376 | tf_op jit(solution)/shard_map/all_to_all | solution.py:555
  204.3 2.1 fusion.25
  (144 shorter events, 20.2 us)
Async XLA Ops:
  8.0 5.3 %copy-start = (bf16[1792,576]{0,1:T(8,128)(2,1)S(1)}, bf16[1792,576]{0,1:T(8,128)(2,1)}, u32[]{:S(2)}) copy-start(bf16[1792,576]{0,1:T(8,128)(2,1)} %param.12) | copy-start | bytes 6193156
  8.0 55.1 %all-reduce.5.cloned.1.call-start = ((), (), s32[]{:S(2)}) async-start(), calls=%async_computation.2 | async-start | bytes 163840 | tf_op jit(solution)/shard_map/psum | solution.py:452
  14.8 75.5 %all-gather.2.cloned.1.call-start = ((), (), s32[]{:S(2)}) async-start(), calls=%async_computation.1 | async-start | bytes 11141120 | tf_op jit(solution)/shard_map/all_gather | solution.py:442
  18.8 27.6 %collective-permute-start = (bf16[8,144,512]{2,1,0:T(8,128)(2,1)}, bf16[8,144,512]{2,1,0:T(8,128)(2,1)S(1)}, u32[]{:S(2)}, u32[]{:S(2)}) collective-permute-start(bf16[8,144,512]{2,1,0:T(8,128)(2,1)} %get-tuple-element.38.refs_0_), channel_id=1, source_target_pairs={{0,64},{4,68},{8,72},{12,76},{16,80},{20,84},{24,88},{28,92},{32,9... | collective-permute-start | bytes 3538952 | tf_op jit(solution)/shard_map/ppermute | solution.py:33
  21.0 34.0 %copy-start.29 = (s32[4]{0:T(128)S(1)}, s32[4]{0:T(128)}, u32[]{:S(2)}) copy-start(s32[4]{0:T(128)} %constant.145.clone) | copy-start | bytes 52
  21.0 26.6 %collective-permute-start.1 = (bf16[8,144,512]{2,1,0:T(8,128)(2,1)}, bf16[8,144,512]{2,1,0:T(8,128)(2,1)}, u32[]{:S(2)}, u32[]{:S(2)}) collective-permute-start(bf16[8,144,512]{2,1,0:T(8,128)(2,1)} %get-tuple-element.39.refs_1_), channel_id=1, source_target_pairs={{0,192},{4,196},{8,200},{12,204},{16,208},{20,212},{24,216},{28,22... | collective-permute-start | bytes 3538952 | tf_op jit(solution)/shard_map/ppermute | solution.py:33
  47.6 26.8 %collective-permute-start.2 = (bf16[8,144,512]{2,1,0:T(8,128)(2,1)}, bf16[8,144,512]{2,1,0:T(8,128)(2,1)}, u32[]{:S(2)}, u32[]{:S(2)}) collective-permute-start(bf16[8,144,512]{2,1,0:T(8,128)(2,1)} %get-tuple-element.40), channel_id=1, source_target_pairs={{0,64},{4,68},{8,72},{12,76},{16,80},{20,84},{24,88},{28,92},{32,9... | collective-permute-start | bytes 3538952 | tf_op jit(solution)/shard_map/ppermute | solution.py:33
  49.1 25.6 %collective-permute-start.3 = (bf16[8,144,512]{2,1,0:T(8,128)(2,1)}, bf16[8,144,512]{2,1,0:T(8,128)(2,1)}, u32[]{:S(2)}, u32[]{:S(2)}) collective-permute-start(bf16[8,144,512]{2,1,0:T(8,128)(2,1)} %get-tuple-element.41), channel_id=1, source_target_pairs={{0,192},{4,196},{8,200},{12,204},{16,208},{20,212},{24,216},{28,22... | collective-permute-start | bytes 3538952 | tf_op jit(solution)/shard_map/ppermute | solution.py:33
  50.7 28.7 %collective-permute-start.4 = (bf16[8,144,512]{2,1,0:T(8,128)(2,1)}, bf16[8,144,512]{2,1,0:T(8,128)(2,1)S(1)}, u32[]{:S(2)}, u32[]{:S(2)}) collective-permute-start(bf16[8,144,512]{2,1,0:T(8,128)(2,1)} %get-tuple-element.42.refs_4_), channel_id=1, source_target_pairs={{0,1},{1,2},{2,3},{3,0},{4,5},{5,6},{6,7},{7,4},{8,9},{9,10},{10,1... | collective-permute-start | bytes 3538952 | tf_op jit(solution)/shard_map/ppermute | solution.py:39
  53.2 26.3 %collective-permute-start.5 = (bf16[8,144,512]{2,1,0:T(8,128)(2,1)}, bf16[8,144,512]{2,1,0:T(8,128)(2,1)}, u32[]{:S(2)}, u32[]{:S(2)}) collective-permute-start(bf16[8,144,512]{2,1,0:T(8,128)(2,1)} %get-tuple-element.43.refs_5_), channel_id=1, source_target_pairs={{0,3},{1,0},{2,1},{3,2},{4,7},{5,4},{6,5},{7,6},{8,11},{9,8},{10,9... | collective-permute-start | bytes 3538952 | tf_op jit(solution)/shard_map/ppermute | solution.py:39
  55.0 34.6 %copy-start.23 = (pred[64,4]{0,1:T(4,128)(4,1)}, pred[64,4]{0,1:T(4,128)(4,1)S(1)}, u32[]{:S(2)}) copy-start(pred[64,4]{0,1:T(4,128)(4,1)S(1)} %iota_compare_fusion.3) | copy-start | bytes 772
  55.0 36.5 %copy-start.22 = (s32[4]{0:T(128)}, s32[4]{0:T(128)S(1)}, u32[]{:S(2)}) copy-start(s32[4]{0:T(128)S(1)} %fusion.51) | copy-start | bytes 52
  80.4 8.5 %copy-start.9 = (f32[8,4,576]{2,1,0:T(4,128)S(1)}, f32[8,4,576]{2,1,0:T(4,128)}, u32[]{:S(2)}) copy-start(f32[8,4,576]{2,1,0:T(4,128)} %get-tuple-element.50) | copy-start | bytes 221188
  80.4 8.7 %copy-start.27 = (f32[512]{0:T(512)S(1)}, f32[512]{0:T(512)}, u32[]{:S(2)}) copy-start(f32[512]{0:T(512)} %param.13) | copy-start | bytes 6148
  80.4 28.1 %collective-permute-start.6 = (bf16[8,144,512]{2,1,0:T(8,128)(2,1)}, bf16[8,144,512]{2,1,0:T(8,128)(2,1)S(1)}, u32[]{:S(2)}, u32[]{:S(2)}) collective-permute-start(bf16[8,144,512]{2,1,0:T(8,128)(2,1)} %get-tuple-element.44.refs_5_), channel_id=1, source_target_pairs={{0,64},{4,68},{8,72},{12,76},{16,80},{20,84},{24,88},{28,92},{32,9... | collective-permute-start | bytes 3538952 | tf_op jit(solution)/shard_map/ppermute | solution.py:33
  80.4 28.2 %collective-permute-start.7 = (bf16[8,144,512]{2,1,0:T(8,128)(2,1)}, bf16[8,144,512]{2,1,0:T(8,128)(2,1)}, u32[]{:S(2)}, u32[]{:S(2)}) collective-permute-start(bf16[8,144,512]{2,1,0:T(8,128)(2,1)} %get-tuple-element.45.refs_10_), channel_id=1, source_target_pairs={{0,192},{4,196},{8,200},{12,204},{16,208},{20,212},{24,216},{28,22... | collective-permute-start | bytes 3538952 | tf_op jit(solution)/shard_map/ppermute | solution.py:33
  83.1 25.5 %collective-permute-start.8 = (bf16[8,144,512]{2,1,0:T(8,128)(2,1)}, bf16[8,144,512]{2,1,0:T(8,128)(2,1)}, u32[]{:S(2)}, u32[]{:S(2)}) collective-permute-start(bf16[8,144,512]{2,1,0:T(8,128)(2,1)} %get-tuple-element.46.refs_6_), channel_id=1, source_target_pairs={{0,3},{1,0},{2,1},{3,2},{4,7},{5,4},{6,5},{7,6},{8,11},{9,8},{10,9... | collective-permute-start | bytes 3538952 | tf_op jit(solution)/shard_map/ppermute | solution.py:39
  85.0 25.4 %collective-permute-start.9 = (bf16[8,144,512]{2,1,0:T(8,128)(2,1)}, bf16[8,144,512]{2,1,0:T(8,128)(2,1)}, u32[]{:S(2)}, u32[]{:S(2)}) collective-permute-start(bf16[8,144,512]{2,1,0:T(8,128)(2,1)} %get-tuple-element.47.refs_9_), channel_id=1, source_target_pairs={{0,1},{1,2},{2,3},{3,0},{4,5},{5,6},{6,7},{7,4},{8,9},{9,10},{10,1... | collective-permute-start | bytes 3538952 | tf_op jit(solution)/shard_map/ppermute | solution.py:39
  110.4 6.7 %copy-start.7 = (bf16[4,144,512]{2,1,0:T(8,128)(2,1)S(1)}, bf16[4,144,512]{2,1,0:T(8,128)(2,1)}, u32[]{:S(2)}) copy-start(bf16[4,144,512]{2,1,0:T(8,128)(2,1)} %get-tuple-element.55) | copy-start | bytes 1769476
  110.4 6.7 %copy-start.8 = (bf16[4,144,512]{2,1,0:T(8,128)(2,1)S(1)}, bf16[4,144,512]{2,1,0:T(8,128)(2,1)}, u32[]{:S(2)}) copy-start(bf16[4,144,512]{2,1,0:T(8,128)(2,1)} %get-tuple-element.56) | copy-start | bytes 1769476
  112.4 22.3 %collective-permute-start.10 = (bf16[4,144,512]{2,1,0:T(8,128)(2,1)}, bf16[4,144,512]{2,1,0:T(8,128)(2,1)}, u32[]{:S(2)}, u32[]{:S(2)}) collective-permute-start(bf16[4,144,512]{2,1,0:T(8,128)(2,1)} %slice.83), channel_id=1, source_target_pairs={{0,1},{1,2},{2,3},{3,0},{4,5},{5,6},{6,7},{7,4},{8,9},{9,10},{10,1... | collective-permute-start | bytes 1769480 | tf_op jit(solution)/shard_map/ppermute | solution.py:39
  114.4 20.4 %collective-permute-start.12 = (bf16[4,144,512]{2,1,0:T(8,128)(2,1)}, bf16[4,144,512]{2,1,0:T(8,128)(2,1)}, u32[]{:S(2)}, u32[]{:S(2)}) collective-permute-start(bf16[4,144,512]{2,1,0:T(8,128)(2,1)} %slice.84), channel_id=1, source_target_pairs={{0,3},{1,0},{2,1},{3,2},{4,7},{5,4},{6,5},{7,6},{8,11},{9,8},{10,9... | collective-permute-start | bytes 1769480 | tf_op jit(solution)/shard_map/ppermute | solution.py:39
  117.0 17.7 %collective-permute-start.11 = (bf16[4,144,512]{2,1,0:T(8,128)(2,1)S(1)}, bf16[4,144,512]{2,1,0:T(8,128)(2,1)}, u32[]{:S(2)}, u32[]{:S(2)}) collective-permute-start(bf16[4,144,512]{2,1,0:T(8,128)(2,1)S(1)} %copy-done.7), channel_id=1, source_target_pairs={{0,64},{4,68},{8,72},{12,76},{16,80},{20,84},{24,88},{28,92},{32,9... | collective-permute-start | bytes 1769480 | tf_op jit(solution)/shard_map/ppermute | solution.py:33
  117.0 17.7 %collective-permute-start.13 = (bf16[4,144,512]{2,1,0:T(8,128)(2,1)S(1)}, bf16[4,144,512]{2,1,0:T(8,128)(2,1)}, u32[]{:S(2)}, u32[]{:S(2)}) collective-permute-start(bf16[4,144,512]{2,1,0:T(8,128)(2,1)S(1)} %copy-done.8), channel_id=1, source_target_pairs={{0,192},{4,196},{8,200},{12,204},{16,208},{20,212},{24,216},{28,22... | collective-permute-start | bytes 1769480 | tf_op jit(solution)/shard_map/ppermute | solution.py:33
  146.3 5.4 %copy-start.18 = (f32[128,128]{1,0:T(8,128)S(1)}, f32[128,128]{1,0:T(8,128)}, u32[]{:S(2)}) copy-start(f32[128,128]{1,0:T(8,128)} %get-tuple-element.65) | copy-start | bytes 196612
  149.2 5.0 %collective-permute-start.14 = (bf16[8,8,64,128]{3,2,1,0:T(8,128)(2,1)}, bf16[8,8,64,128]{3,2,1,0:T(8,128)(2,1)S(1)}, u32[]{:S(2)}, u32[]{:S(2)}) collective-permute-start(bf16[8,8,64,128]{3,2,1,0:T(8,128)(2,1)} %fusion.30), channel_id=1, source_target_pairs={{0,4},{4,0},{8,12},{12,8},{16,20},{20,16},{24,28},{28,24},{32,36},... | collective-permute-start | bytes 3145736 | tf_op jit(solution)/shard_map/ppermute | solution.py:43
  151.7 2.3 %collective-permute-start.15 = (f32[8,8,64]{2,1,0:T(8,128)S(1)}, f32[8,8,64]{2,1,0:T(8,128)S(1)}, u32[]{:S(2)}, u32[]{:S(2)}) collective-permute-start(f32[8,8,64]{2,1,0:T(8,128)S(1)} %dynamic-slice_bitcast_fusion), channel_id=1, source_target_pairs={{0,4},{4,0},{8,12},{12,8},{16,20},{20,16},{24,28},{28,24},{32,36},... | collective-permute-start | bytes 49160 | tf_op jit(solution)/shard_map/ppermute | solution.py:43
  158.9 13.9 %copy-start.20 = (f32[8,64]{1,0:T(8,128)S(1)}, f32[8,64]{1,0:T(8,128)}, u32[]{:S(2)}) copy-start(f32[8,64]{1,0:T(8,128)} %copy-done.19) | copy-start | bytes 6148
  158.9 14.0 %copy-start.15 = (f32[8,64]{1,0:T(8,128)S(1)}, f32[8,64]{1,0:T(8,128)}, u32[]{:S(2)}) copy-start(f32[8,64]{1,0:T(8,128)} %copy-done.14) | copy-start | bytes 6148
  158.9 14.0 %copy-start.24 = (pred[64,4]{0,1:T(4,128)(4,1)S(1)}, pred[64,4]{0,1:T(4,128)(4,1)}, u32[]{:S(2)}) copy-start(pred[64,4]{0,1:T(4,128)(4,1)} %copy-done.23) | copy-start | bytes 772
  158.9 43.9 %all-to-all-start = ((bf16[8,528,128]{2,1,0:T(8,128)(2,1)}), bf16[8,528,128]{2,1,0:T(8,128)(2,1)S(1)}, u32[]{:S(2)}, u32[]{:S(2)}) async-start(bf16[8,528,128]{2,1,0:T(8,128)(2,1)} %fusion.29), calls=%async_computation | async-start | bytes 2162688 | tf_op jit(solution)/shard_map/all_to_all | solution.py:555
  172.9 30.0 %copy-start.16 = (f32[8,64]{1,0:T(8,128)S(1)}, f32[8,64]{1,0:T(8,128)}, u32[]{:S(2)}) copy-start(f32[8,64]{1,0:T(8,128)} %get-tuple-element.67) | copy-start | bytes 6148
  (17 other events, 29.4 us)
Sparse Core Ops, SparseCore 0:
  14.9 48.1 all-reduce.4
Sparse Core Ops, SparseCore 1:
  18.9 69.9 all-gather.1
